TPU v7x, 128 devices: a whole 4x4x4 slice. The times are simulated.
128 devices in a mesh: gx: 8 (over z, core), gy: 16 (over x, y).
Axes of the slice: x: 4, y: 4, z: 4, core: 2. Of those that a mesh axis runs over, the one named last changes fastest.
Arguments:
- features: bfloat16 [131072, 512], P(('gx', 'gy')), may hold values from -6 to 6
- weight: bfloat16 [512, 512], replicated, may hold values from -0.25 to 0.25
- attn_src: float32 [512], replicated, may hold values from -0.6 to 0.6
- attn_dst: float32 [512], replicated, may hold values from -0.6 to 0.6
- upstream: bfloat16 [131072, 512], P(('gx', 'gy')), may hold values from -6 to 6
- scores: float32 [131072, 80], P(('gx', 'gy')), may hold values from -8 to 300
- neighbour_lists: int32 [1024, 16], P(('gx', 'gy')), may hold values from 0 to 1023, as said below
- edge_index: int32 [131072, 80], P(('gx', 'gy')), may hold values from 0 to 2047, as said below
Outputs:
- grad_features: bfloat16 [131072, 512], P(('gx', 'gy'))
- grad_weight: float32 [512, 512], replicated
- grad_src: float32 [512], replicated
- grad_dst: float32 [512], replicated
Inputs may be any that keep to these rules, and one draw needn't show every extreme that they name: `neighbour_lists`: blocks are numbered device by device in mesh order, 8 to a device. The list of block b names 16 different blocks, all held by devices whose gx and gy indices are within one of b's device's (wrapping around both axes); the first entry is b itself. `edge_index`: the 80 entries of one node are different.
All inputs are finite; a program needn't handle non-finite values.
Results may differ from a plain program's by a relative error of at most 0.0057.
Values may be sent and summed in bfloat16 or wider, within the bound.
No kernel may reach another device: no remote copies, remote signals or barrier semaphores. Data moves between devices by JAX's collectives and lax.ppermute only.
A program may use at most 128 MiB of HBM per device.

v0:
```python
import jax
import jax.numpy as jnp
from jax import lax
from jax.sharding import PartitionSpec as P

exact = lax.Precision.HIGHEST


def shifted(array, axis, by):
    count = lax.axis_size(axis)
    return lax.ppermute(array, axis, [(i, (i + by) % count) for i in range(count)])


def padded(block, sides, width):
    for axis, dim in sides:
        count = lax.axis_size(axis)
        forward = [(i, i + 1) for i in range(count - 1)]
        forward.append((count - 1, 0))
        backward = [(target, source) for source, target in forward]
        low = lax.ppermute(
            lax.slice_in_dim(block, block.shape[dim] - width, None, axis=dim), axis, forward
        )
        high = lax.ppermute(lax.slice_in_dim(block, 0, width, axis=dim), axis, backward)
        block = jnp.concatenate([low, block, high], axis=dim)
    return block


def back_along_x(stack, dim):
    total = lax.index_in_dim(stack, 1, dim, False)
    for offset in (1, -1):
        total = total + shifted(lax.index_in_dim(stack, 1 + offset, dim, False), "gx", offset)
    return total


def back_along_y(stack, dim):
    total = lax.index_in_dim(stack, 1, dim, False)
    for offset in (1, -1):
        total = total + shifted(lax.index_in_dim(stack, 1 + offset, dim, False), "gy", offset)
    return total


def one_hots(index_blk, nlist, node_block):
    slot_hot = (index_blk // node_block)[:, :, None] == jnp.arange(nlist, dtype=jnp.int32)[
        None, None, :
    ]
    row_hot = (index_blk % node_block)[:, :, None] == jnp.arange(node_block, dtype=jnp.int32)[
        None, None, :
    ]
    return (slot_hot.astype(jnp.float32), row_hot.astype(jnp.float32))


def on_device(features, weight, attn_src, attn_dst, upstream, scores, neighbour_lists, edge_index):
    rows = features.shape[0]
    block_width = weight.shape[1]
    node_block = 128
    nlist = neighbour_lists.shape[1]
    block_count = rows // node_block
    edges = scores.shape[1]
    slot_count = 9 * block_count
    projected = jnp.dot(features, weight, preferred_element_type=jnp.float32).astype(jnp.bfloat16)
    neighbour_table = padded(projected[None, None], (("gx", 0), ("gy", 1)), 1)
    neighbour_table_flat = neighbour_table.reshape(slot_count, node_block * block_width)
    size_x = lax.axis_size("gx")
    size_y = lax.axis_size("gy")
    here_x = lax.axis_index("gx")
    here_y = lax.axis_index("gy")
    owner = neighbour_lists // block_count
    off_x = (owner // size_y - here_x + 1) % size_x
    off_y = (owner % size_y - here_y + 1) % size_y
    slots = (off_x * 3 + off_y) * block_count + neighbour_lists % block_count
    slot_range = jnp.arange(slot_count, dtype=jnp.int32)
    logit_all = jnp.where(scores > 0, scores, 0.2 * scores)
    alpha_all = jax.nn.softmax(logit_all, axis=1)

    def step(carry, item):
        accum, src_acc, dst_acc = carry
        slot_ids, grad_blk, score_blk, index_blk, own_blk, alpha = item
        select = slot_ids[:, None] == slot_range[None, :]
        select_low = select.astype(jnp.bfloat16)
        select_high = select.astype(jnp.float32)
        cand = jnp.dot(select_low, neighbour_table_flat, preferred_element_type=jnp.float32).astype(
            jnp.bfloat16
        )
        cand = cand.reshape(nlist * node_block, block_width)
        slot_hot, row_hot = one_hots(index_blk, nlist, node_block)
        dense = lax.dot_general(
            grad_blk, cand, (((1,), (1,)), ((), ())), preferred_element_type=jnp.float32
        )
        picked_rows = jnp.einsum(
            "isr,ikr->iks", dense.reshape(node_block, nlist, node_block), row_hot, precision=exact
        )
        dalpha = jnp.sum(picked_rows * slot_hot, axis=2)
        inner = jnp.sum(alpha * dalpha, axis=1, keepdims=True)
        dz = alpha * (dalpha - inner) * jnp.where(score_blk > 0, 1.0, 0.2)
        du = jnp.sum(dz, axis=1)
        dz_dense = jnp.einsum("iks,ikr->isr", slot_hot * dz[:, :, None], row_hot, precision=exact)
        column_sums = jnp.sum(dz_dense, axis=0).reshape(nlist * node_block)
        alpha_low = alpha.astype(jnp.bfloat16)
        weights_dense = jnp.einsum(
            "iks,ikr->isr",
            slot_hot.astype(jnp.bfloat16) * alpha_low[:, :, None],
            row_hot.astype(jnp.bfloat16),
            preferred_element_type=jnp.float32,
        ).astype(jnp.bfloat16)
        contrib = lax.dot_general(
            weights_dense.reshape(node_block, nlist * node_block),
            grad_blk,
            (((0,), (0,)), ((), ())),
            preferred_element_type=jnp.float32,
        )
        contrib = contrib + column_sums[:, None] * attn_dst[None, :]
        accum = accum + lax.dot_general(
            select_high,
            contrib.reshape(nlist, node_block * block_width),
            (((0,), (0,)), ((), ())),
            precision=exact,
        )
        dst_acc = dst_acc + jnp.dot(column_sums, cand.astype(jnp.float32), precision=exact)
        src_acc = src_acc + jnp.dot(du, own_blk.astype(jnp.float32), precision=exact)
        return ((accum, src_acc, dst_acc), du)

    first_node = jnp.zeros((slot_count, node_block * block_width), jnp.float32)
    start = (
        first_node,
        jnp.zeros((block_width,), jnp.float32),
        jnp.zeros((block_width,), jnp.float32),
    )
    items = (
        slots,
        upstream.reshape(block_count, node_block, block_width),
        scores.reshape(block_count, node_block, edges),
        edge_index.reshape(block_count, node_block, edges),
        projected.reshape(block_count, node_block, block_width),
        alpha_all.reshape(block_count, node_block, edges),
    )
    (accum, src_acc, dst_acc), du_all = lax.scan(step, start, items)
    accum = accum.reshape(3, 3, rows, block_width)
    returned = back_along_y(back_along_x(accum, 0), 0)
    grad_proj = returned + du_all.reshape(rows)[:, None] * attn_src[None, :]
    grad_low = grad_proj.astype(jnp.bfloat16)
    grad_features = lax.dot_general(
        grad_low, weight, (((1,), (1,)), ((), ())), preferred_element_type=jnp.float32
    ).astype(jnp.bfloat16)
    weight_term = lax.dot_general(
        features, grad_low, (((0,), (0,)), ((), ())), preferred_element_type=jnp.float32
    )
    weight_total, src_total, dst_total = lax.psum((weight_term, src_acc, dst_acc), ("gx", "gy"))
    scale = 1.0 / jnp.sqrt(jnp.float32(rows * size_x * size_y))
    return (grad_features, weight_total * scale, src_total * scale, dst_total * scale)


def solution(mesh):
    return jax.shard_map(
        on_device,
        mesh=mesh,
        in_specs=(
            P(("gx", "gy"), None),
            P(),
            P(),
            P(),
            P(("gx", "gy"), None),
            P(("gx", "gy"), None),
            P(("gx", "gy"), None),
            P(("gx", "gy"), None),
        ),
        out_specs=(P(("gx", "gy"), None), P(), P(), P()),
        check_vma=False,
    )
```

profile of v0, /device:TPU:1, one launch (start us, length us, event | category | flops | bytes accessed | tf_op | source)
XLA Modules:
  0.0 910.1 jit_solution(1687363352871852656)
XLA Ops:
  13.2 12.8 %collective-permute-done.1 = bf16[1,1,1024,512]{3,2,1,0:T(8,128)(2,1)S(1)} collective-permute-done((bf16[1,1,1024,512]{3,2,1,0:T(8,128)(2,1)S(1)}, bf16[1,1,1024,512]{3,2,1,0:T(8,128)(2,1)S(1)}, u32[]{:S(2)}, u32[]{:S(2)}) %collective-permute-start.1) | collective-permute-done | bytes 1048608 | tf_op jit(solution)/shard_map/ppermute | solution.py:23
  29.0 4.9 collective-permute-start.3
  39.9 57.1 %collective-permute-done.3 = bf16[3,1,1024,512]{3,2,1,0:T(8,128)(2,1)} collective-permute-done((bf16[3,1,1024,512]{3,2,1,0:T(8,128)(2,1)}, bf16[3,1,1024,512]{3,2,1,0:T(8,128)(2,1)}, u32[]{:S(2)}, u32[]{:S(2)}) %collective-permute-start.3) | collective-permute-done | bytes 3145760 | tf_op jit(solution)/shard_map/ppermute | solution.py:23
  97.0 5.2 collective-permute-done.2
  102.3 8.2 pad_maximum_fusion
  110.5 12.5 %reshape.172 = bf16[72,65536]{1,0:T(8,128)(2,1)} reshape(bf16[3,3,1024,512]{3,2,1,0:T(8,128)(2,1)} %pad_maximum_fusion) | data formatting | bytes 18874368 | tf_op jit(solution)/shard_map/reshape | solution.py:62
  123.0 454.8 %while.19 = (s32[]{:T(128)}, f32[72,65536]{1,0:T(8,128)}, f32[512]{0:T(512)S(1)}, f32[512]{0:T(512)S(1)}, f32[8,128]{1,0:T(8,128)S(1)}, /*index=5*/s32[8,16]{1,0...) while((s32[]{:T(128)}, f32[72,65536]{1,0:T(8,128)}, ...), condition=%wide.region_6.7_spmd.clone, body=%wide.region_2.6_spmd.clone.sunk | while | flops 2171539456 | bytes 109000216 | solution.py:136
  125.8 5.3 convolution_convert_fusion.4
  138.6 6.6 fusion.124
  149.4 4.6 fusion.127
  156.1 3.6 multiply_add_fusion.2
  159.7 4.0 reshape.186
  163.7 13.8 %convolution_add_fusion.2 = f32[72,65536]{1,0:T(8,128)} fusion(f32[16,65536]{1,0:T(8,128)} %reshape.186, f32[72,65536]{1,0:T(8,128)} %get-tuple-element.389, pred[]{:T(512)S(6)} %compare.23, s32[16]{0:T(128)S(1)} %fusion.122), kind=kOutput, calls=%fused_computation.1.clone.1 | convolution fusion | flops 915408000 | bytes 41943104 | tf_op jit(solution)/shard_map/while/body/eval_jaxpr/dot_general | solution.py:112
  180.3 5.3 convolution_convert_fusion.4
  193.1 6.6 fusion.124
  203.8 4.6 fusion.127
  210.6 3.6 multiply_add_fusion.2
  214.2 4.0 reshape.186
  218.2 16.5 %convolution_add_fusion.2 = f32[72,65536]{1,0:T(8,128)} fusion(f32[16,65536]{1,0:T(8,128)} %reshape.186, f32[72,65536]{1,0:T(8,128)} %get-tuple-element.389, pred[]{:T(512)S(6)} %compare.23, s32[16]{0:T(128)S(1)} %fusion.122), kind=kOutput, calls=%fused_computation.1.clone.1 | convolution fusion | flops 915408000 | bytes 41943104 | tf_op jit(solution)/shard_map/while/body/eval_jaxpr/dot_general | solution.py:112
  237.5 5.3 convolution_convert_fusion.4
  250.3 6.6 fusion.124
  261.0 4.6 fusion.127
  267.7 3.6 multiply_add_fusion.2
  271.4 4.0 reshape.186
  275.4 16.5 %convolution_add_fusion.2 = f32[72,65536]{1,0:T(8,128)} fusion(f32[16,65536]{1,0:T(8,128)} %reshape.186, f32[72,65536]{1,0:T(8,128)} %get-tuple-element.389, pred[]{:T(512)S(6)} %compare.23, s32[16]{0:T(128)S(1)} %fusion.122), kind=kOutput, calls=%fused_computation.1.clone.1 | convolution fusion | flops 915408000 | bytes 41943104 | tf_op jit(solution)/shard_map/while/body/eval_jaxpr/dot_general | solution.py:112
  294.7 5.3 convolution_convert_fusion.4
  307.5 6.6 fusion.124
  318.2 4.6 fusion.127
  324.9 3.6 multiply_add_fusion.2
  328.6 4.0 reshape.186
  332.6 16.5 %convolution_add_fusion.2 = f32[72,65536]{1,0:T(8,128)} fusion(f32[16,65536]{1,0:T(8,128)} %reshape.186, f32[72,65536]{1,0:T(8,128)} %get-tuple-element.389, pred[]{:T(512)S(6)} %compare.23, s32[16]{0:T(128)S(1)} %fusion.122), kind=kOutput, calls=%fused_computation.1.clone.1 | convolution fusion | flops 915408000 | bytes 41943104 | tf_op jit(solution)/shard_map/while/body/eval_jaxpr/dot_general | solution.py:112
  351.9 5.3 convolution_convert_fusion.4
  364.7 6.6 fusion.124
  375.4 4.6 fusion.127
  382.1 3.6 multiply_add_fusion.2
  385.8 4.0 reshape.186
  389.8 16.5 %convolution_add_fusion.2 = f32[72,65536]{1,0:T(8,128)} fusion(f32[16,65536]{1,0:T(8,128)} %reshape.186, f32[72,65536]{1,0:T(8,128)} %get-tuple-element.389, pred[]{:T(512)S(6)} %compare.23, s32[16]{0:T(128)S(1)} %fusion.122), kind=kOutput, calls=%fused_computation.1.clone.1 | convolution fusion | flops 915408000 | bytes 41943104 | tf_op jit(solution)/shard_map/while/body/eval_jaxpr/dot_general | solution.py:112
  409.0 5.3 convolution_convert_fusion.4
  421.8 6.6 fusion.124
  432.6 4.6 fusion.127
  439.3 3.6 multiply_add_fusion.2
  442.9 4.0 reshape.186
  446.9 16.5 %convolution_add_fusion.2 = f32[72,65536]{1,0:T(8,128)} fusion(f32[16,65536]{1,0:T(8,128)} %reshape.186, f32[72,65536]{1,0:T(8,128)} %get-tuple-element.389, pred[]{:T(512)S(6)} %compare.23, s32[16]{0:T(128)S(1)} %fusion.122), kind=kOutput, calls=%fused_computation.1.clone.1 | convolution fusion | flops 915408000 | bytes 41943104 | tf_op jit(solution)/shard_map/while/body/eval_jaxpr/dot_general | solution.py:112
  466.2 5.3 convolution_convert_fusion.4
  479.0 6.6 fusion.124
  489.8 4.6 fusion.127
  500.1 4.0 reshape.186
  504.1 16.5 %convolution_add_fusion.2 = f32[72,65536]{1,0:T(8,128)} fusion(f32[16,65536]{1,0:T(8,128)} %reshape.186, f32[72,65536]{1,0:T(8,128)} %get-tuple-element.389, pred[]{:T(512)S(6)} %compare.23, s32[16]{0:T(128)S(1)} %fusion.122), kind=kOutput, calls=%fused_computation.1.clone.1 | convolution fusion | flops 915408000 | bytes 41943104 | tf_op jit(solution)/shard_map/while/body/eval_jaxpr/dot_general | solution.py:112
  523.4 5.3 convolution_convert_fusion.4
  536.2 6.6 fusion.124
  547.0 4.6 fusion.127
  557.3 4.0 reshape.186
  561.3 16.5 %convolution_add_fusion.2 = f32[72,65536]{1,0:T(8,128)} fusion(f32[16,65536]{1,0:T(8,128)} %reshape.186, f32[72,65536]{1,0:T(8,128)} %get-tuple-element.389, pred[]{:T(512)S(6)} %compare.23, s32[16]{0:T(128)S(1)} %fusion.122), kind=kOutput, calls=%fused_computation.1.clone.1 | convolution fusion | flops 915408000 | bytes 41943104 | tf_op jit(solution)/shard_map/while/body/eval_jaxpr/dot_general | solution.py:112
  577.8 13.5 %fusion.68 = (f32[24,65536]{1,0:T(8,128)}, f32[24,65536]{1,0:T(8,128)}, f32[24,65536]{1,0:T(8,128)}) fusion(f32[72,65536]{1,0:T(8,128)} %get-tuple-element.183), kind=kLoop, calls=%fused_computation.115 | loop fusion | bytes 37748736 | tf_op jit(solution)/shard_map/slice | solution.py:31
  591.4 6.8 squeeze.49
  598.2 6.9 squeeze.50
  605.1 5.8 collective-permute-start.5
  612.1 6.8 squeeze.48
  619.0 62.4 %collective-permute-done.5 = f32[3,1024,512]{2,1,0:T(8,128)} collective-permute-done((f32[3,1024,512]{2,1,0:T(8,128)}, f32[3,1024,512]{2,1,0:T(8,128)}, u32[]{:S(2)}, u32[]{:S(2)}) %collective-permute-start.5) | collective-permute-done | bytes 6291488 | tf_op jit(solution)/shard_map/ppermute | solution.py:11
  681.4 11.5 %add_add_fusion = f32[3,1024,512]{2,1,0:T(8,128)} fusion(f32[3,1024,512]{2,1,0:T(8,128)} %collective-permute-done.5, f32[3,1024,512]{2,1,0:T(8,128)} %squeeze.48, f32[3,1024,512]{2,1,0:T(8,128)} %collective-permute-done.4), kind=kLoop, calls=%fused_computation.64 | loop fusion | flops 3145728 | bytes 25165824 | tf_op jit(solution)/shard_map/add | solution.py:31
  695.6 4.8 collective-permute-start.7
  700.4 40.2 %collective-permute-done.6 = f32[1024,512]{1,0:T(8,128)S(1)} collective-permute-done((f32[1024,512]{1,0:T(8,128)S(1)}, f32[1024,512]{1,0:T(8,128)S(1)}, u32[]{:S(2)}, u32[]{:S(2)}) %collective-permute-start.6) | collective-permute-done | bytes 2097184 | tf_op jit(solution)/shard_map/ppermute | solution.py:11
  744.4 75.0 %all-reduce = (f32[512]{0:T(512)S(1)}, f32[512]{0:T(512)S(1)}) all-reduce(f32[512]{0:T(512)S(1)} %get-tuple-element.185, f32[512]{0:T(512)S(1)} %get-tuple-element.186), channel_id=1, replica_groups=mesh['gx'=8,'gy'=16] {'gx','gy'}, use_global_device_ids=true, to_apply=%region_8.9 | all-reduce | flops 1024 | bytes 8192 | tf_op jit(solution)/shard_map/psum | solution.py:147
  821.6 79.0 %all-reduce.3.cloned.1.call-done = f32[512,512]{0,1:T(8,128)} async-done(((f32[512,512]{0,1:T(8,128)}), f32[512,512]{0,1:T(8,128)}) %all-reduce.3.cloned.1.call-update) | async-done | bytes 1048592 | tf_op jit(solution)/shard_map/psum | solution.py:147
  (222 shorter events, 166.0 us)
Async XLA Ops:
  7.2 1.2 copy-start
  7.2 26.8 %copy-start.4 = (f32[1024,80]{0,1:T(8,128)S(1)}, f32[1024,80]{0,1:T(8,128)}, u32[]{:S(2)}) copy-start(f32[1024,80]{0,1:T(8,128)} %param.15) | copy-start | bytes 983044
  7.2 893.4 %all-reduce.3.cloned.1.call-start = ((), (), s32[]{:S(2)}) async-start(), calls=%async_computation | async-start | bytes 2097152 | tf_op jit(solution)/shard_map/psum | solution.py:147
  10.1 29.8 %copy-start.7 = (s32[8,16]{1,0:T(8,128)S(1)}, s32[8,16]{1,0:T(8,128)}, u32[]{:S(2)}) copy-start(s32[8,16]{1,0:T(8,128)} %param.16) | copy-start | bytes 1540
  10.2 15.8 %collective-permute-start.1 = (bf16[1,1,1024,512]{3,2,1,0:T(8,128)(2,1)S(1)}, bf16[1,1,1024,512]{3,2,1,0:T(8,128)(2,1)S(1)}, u32[]{:S(2)}, u32[]{:S(2)}) collective-permute-start(bf16[1,1,1024,512]{3,2,1,0:T(8,128)(2,1)S(1)} %bitcast.148), channel_id=1, source_target_pairs={{16,0},{32,16},{48,32},{64,48},{80,64},{96,80},{112,96},{0,112},{1... | collective-permute-start | bytes 3145736 | tf_op jit(solution)/shard_map/ppermute | solution.py:23
  11.6 14.4 %collective-permute-start = (bf16[1,1,1024,512]{3,2,1,0:T(8,128)(2,1)S(1)}, bf16[1,1,1024,512]{3,2,1,0:T(8,128)(2,1)S(1)}, u32[]{:S(2)}, u32[]{:S(2)}) collective-permute-start(bf16[1,1,1024,512]{3,2,1,0:T(8,128)(2,1)S(1)} %bitcast.149), channel_id=1, source_target_pairs={{0,16},{16,32},{32,48},{48,64},{64,80},{80,96},{96,112},{112,0},{1... | collective-permute-start | bytes 3145736 | tf_op jit(solution)/shard_map/ppermute | solution.py:20
  26.0 1.0 copy-start.5
  29.0 68.0 %collective-permute-start.3 = (bf16[3,1,1024,512]{3,2,1,0:T(8,128)(2,1)}, bf16[3,1,1024,512]{3,2,1,0:T(8,128)(2,1)}, u32[]{:S(2)}, u32[]{:S(2)}) collective-permute-start(bf16[3,1,1024,512]{3,2,1,0:T(8,128)(2,1)} %pad_maximum_fusion.1), channel_id=1, source_target_pairs={{1,0},{2,1},{3,2},{4,3},{5,4},{6,5},{7,6},{8,7},{9,8},{10,9},{11,1... | collective-permute-start | bytes 9437192 | tf_op jit(solution)/shard_map/ppermute | solution.py:23
  33.9 68.3 %collective-permute-start.2 = (bf16[3,1,1024,512]{3,2,1,0:T(8,128)(2,1)}, bf16[3,1,1024,512]{3,2,1,0:T(8,128)(2,1)}, u32[]{:S(2)}, u32[]{:S(2)}) collective-permute-start(bf16[3,1,1024,512]{3,2,1,0:T(8,128)(2,1)} %pad_maximum_fusion.1), channel_id=1, source_target_pairs={{0,1},{1,2},{2,3},{3,4},{4,5},{5,6},{6,7},{7,8},{8,9},{9,10},{10,1... | collective-permute-start | bytes 9437192 | tf_op jit(solution)/shard_map/ppermute | solution.py:20
  110.5 12.5 %copy-start.6 = (f32[512]{0:T(512)S(1)}, f32[512]{0:T(512)}, u32[]{:S(2)}) copy-start(f32[512]{0:T(512)} %param.13) | copy-start | bytes 6148
  123.0 2.7 copy-start.2
  145.2 8.8 copy-start.1
  163.7 13.8 %copy-start.3 = (bf16[8,128,512]{2,1,0:T(8,128)(2,1)S(1)}, bf16[8,128,512]{2,1,0:T(8,128)(2,1)}, u32[]{:S(2)}) copy-start(bf16[8,128,512]{2,1,0:T(8,128)(2,1)} %copy-done.2) | copy-start | bytes 3145732 | tf_op jit(solution)/shard_map/while
  177.5 2.7 copy-start.2
  199.7 8.8 copy-start.1
  218.2 16.5 %copy-start.3 = (bf16[8,128,512]{2,1,0:T(8,128)(2,1)S(1)}, bf16[8,128,512]{2,1,0:T(8,128)(2,1)}, u32[]{:S(2)}) copy-start(bf16[8,128,512]{2,1,0:T(8,128)(2,1)} %copy-done.2) | copy-start | bytes 3145732 | tf_op jit(solution)/shard_map/while
  234.7 2.7 copy-start.2
  256.9 8.8 copy-start.1
  275.4 16.5 %copy-start.3 = (bf16[8,128,512]{2,1,0:T(8,128)(2,1)S(1)}, bf16[8,128,512]{2,1,0:T(8,128)(2,1)}, u32[]{:S(2)}) copy-start(bf16[8,128,512]{2,1,0:T(8,128)(2,1)} %copy-done.2) | copy-start | bytes 3145732 | tf_op jit(solution)/shard_map/while
  291.9 2.7 copy-start.2
  314.1 8.8 copy-start.1
  332.6 16.5 %copy-start.3 = (bf16[8,128,512]{2,1,0:T(8,128)(2,1)S(1)}, bf16[8,128,512]{2,1,0:T(8,128)(2,1)}, u32[]{:S(2)}) copy-start(bf16[8,128,512]{2,1,0:T(8,128)(2,1)} %copy-done.2) | copy-start | bytes 3145732 | tf_op jit(solution)/shard_map/while
  349.1 2.7 copy-start.2
  371.2 8.8 copy-start.1
  389.8 16.5 %copy-start.3 = (bf16[8,128,512]{2,1,0:T(8,128)(2,1)S(1)}, bf16[8,128,512]{2,1,0:T(8,128)(2,1)}, u32[]{:S(2)}) copy-start(bf16[8,128,512]{2,1,0:T(8,128)(2,1)} %copy-done.2) | copy-start | bytes 3145732 | tf_op jit(solution)/shard_map/while
  406.2 2.7 copy-start.2
  428.4 8.8 copy-start.1
  446.9 16.5 %copy-start.3 = (bf16[8,128,512]{2,1,0:T(8,128)(2,1)S(1)}, bf16[8,128,512]{2,1,0:T(8,128)(2,1)}, u32[]{:S(2)}) copy-start(bf16[8,128,512]{2,1,0:T(8,128)(2,1)} %copy-done.2) | copy-start | bytes 3145732 | tf_op jit(solution)/shard_map/while
  463.4 2.7 copy-start.2
  485.6 8.8 copy-start.1
  504.1 16.5 %copy-start.3 = (bf16[8,128,512]{2,1,0:T(8,128)(2,1)S(1)}, bf16[8,128,512]{2,1,0:T(8,128)(2,1)}, u32[]{:S(2)}) copy-start(bf16[8,128,512]{2,1,0:T(8,128)(2,1)} %copy-done.2) | copy-start | bytes 3145732 | tf_op jit(solution)/shard_map/while
  520.6 2.7 copy-start.2
  542.8 8.8 copy-start.1
  561.3 16.5 %copy-start.3 = (bf16[8,128,512]{2,1,0:T(8,128)(2,1)S(1)}, bf16[8,128,512]{2,1,0:T(8,128)(2,1)}, u32[]{:S(2)}) copy-start(bf16[8,128,512]{2,1,0:T(8,128)(2,1)} %copy-done.2) | copy-start | bytes 3145732 | tf_op jit(solution)/shard_map/while
  605.1 76.3 %collective-permute-start.5 = (f32[3,1024,512]{2,1,0:T(8,128)}, f32[3,1024,512]{2,1,0:T(8,128)}, u32[]{:S(2)}, u32[]{:S(2)}) collective-permute-start(f32[3,1024,512]{2,1,0:T(8,128)} %squeeze.50), channel_id=1, source_target_pairs={{0,112},{16,0},{32,16},{48,32},{64,48},{80,64},{96,80},{112,96},{1... | collective-permute-start | bytes 18874376 | tf_op jit(solution)/shard_map/ppermute | solution.py:11
  610.9 70.5 %collective-permute-start.4 = (f32[3,1024,512]{2,1,0:T(8,128)}, f32[3,1024,512]{2,1,0:T(8,128)}, u32[]{:S(2)}, u32[]{:S(2)}) collective-permute-start(f32[3,1024,512]{2,1,0:T(8,128)} %squeeze.49), channel_id=1, source_target_pairs={{0,16},{16,32},{32,48},{48,64},{64,80},{80,96},{96,112},{112,0},{1... | collective-permute-start | bytes 18874376 | tf_op jit(solution)/shard_map/ppermute | solution.py:11
  692.9 47.8 %copy-start.8 = (f32[512]{0:T(512)S(1)}, f32[512]{0:T(512)}, u32[]{:S(2)}) copy-start(f32[512]{0:T(512)} %param.12) | copy-start | bytes 6148
  695.6 45.1 %collective-permute-start.6 = (f32[1024,512]{1,0:T(8,128)S(1)}, f32[1024,512]{1,0:T(8,128)S(1)}, u32[]{:S(2)}, u32[]{:S(2)}) collective-permute-start(f32[1024,512]{1,0:T(8,128)S(1)} %get-tuple-element.274), channel_id=1, source_target_pairs={{0,1},{1,2},{2,3},{3,4},{4,5},{5,6},{6,7},{7,8},{8,9},{9,10},{10,1... | collective-permute-start | bytes 6291464 | tf_op jit(solution)/shard_map/ppermute | solution.py:11
  695.6 45.0 %collective-permute-start.7 = (f32[1024,512]{1,0:T(8,128)S(1)}, f32[1024,512]{1,0:T(8,128)S(1)}, u32[]{:S(2)}, u32[]{:S(2)}) collective-permute-start(f32[1024,512]{1,0:T(8,128)S(1)} %get-tuple-element.275), channel_id=1, source_target_pairs={{0,15},{1,0},{2,1},{3,2},{4,3},{5,4},{6,5},{7,6},{8,7},{9,8},{10,9... | collective-permute-start | bytes 6291464 | tf_op jit(solution)/shard_map/ppermute | solution.py:11
  742.6 77.3 %copy-start.9 = (bf16[512,512]{1,0:T(8,128)(2,1)S(1)}, bf16[512,512]{1,0:T(8,128)(2,1)}, u32[]{:S(2)}) copy-start(bf16[512,512]{1,0:T(8,128)(2,1)} %param.11) | copy-start | bytes 1572868
Sparse Core Ops, SparseCore 0:
  744.5 156.0 all-reduce.2
where the time goes:
time: 914 us; the launch traced here: 910 us
  matrix products  351 us (38%)
  waiting for transfers between devices  257 us (28%)
  local copies, waits for them, and re-layouts  120 us (13%)
  blocking collectives  75 us (8%)
  other arithmetic  73.2 us (8%)
  starting transfers between devices  19.9 us (2%)
  between operations  14.1 us (2%)
    dot_general x8, matrix products, step(): lax.dot_general(select_high, contrib.reshape(nlist, node_block * block_wi...  129 us
    ppermute x4, waiting for transfers between devices, shifted(): lax.ppermute(array, axis, [(i, (i + by) % count) for i in range(count)])  103 us
    psum x1, waiting for transfers between devices, on_device(): lax.psum((weight_term, src_acc, dst_acc), ('gx', 'gy'))  79 us
    psum x1, blocking collectives, on_device(): lax.psum((weight_term, src_acc, dst_acc), ('gx', 'gy'))  75 us
    ppermute x2, waiting for transfers between devices, padded(): lax.ppermute(lax.slice_in_dim(block, 0, width, axis=dim), axis, backward)  69.8 us
    dot_general x8, matrix products, step(): jnp.einsum('isr,ikr->iks', dense.reshape(node_block, nlist, node_block),...  52.7 us
    dot_general x8, matrix products, step(): jnp.dot(select_low, neighbour_table_flat, preferred_element_type=jnp.floa...  42.8 us
    dot_general x8, matrix products, step(): jnp.einsum('iks,ikr->isr', slot_hot * dz[:, :, None], row_hot, precision=...  37.2 us
  transfers between devices with their start and end apart: 9, of which 6 were waited for; matrix products, arithmetic and copies ran while one was open for 2% of the time, Pallas kernels for 0%

commit v1 on v0

v1 whole, which is shorter than its diff:
```python
import functools
import math

import jax
import jax.numpy as jnp
from jax import lax
from jax.experimental import pallas as pl
from jax.experimental.pallas import tpu as pltpu
from jax.sharding import PartitionSpec as P

BLK = 128
NBL = 16
WIDE = 256
HALVES = NBL * BLK // WIDE
LANES = 128
MIB = 1 << 20

f32 = jnp.float32
bf16 = jnp.bfloat16


def spread_body(blocks, edges, slots, score_ref, index_ref, grad_ref, dense_ref, own_ref, core_ref,
                far_ref, hi_scr, lo_scr, main_scr, rest_scr, grad_t, left_scr, right_scr, acc):
    step = pl.program_id(0)
    per = 3 * blocks

    @pl.when(step == 0)
    def _():
        own_ref[...] = jnp.zeros_like(own_ref)
        acc[...] = jnp.zeros_like(acc)
        hi_scr[...] = jnp.full_like(hi_scr, -1)
        lo_scr[...] = jnp.zeros_like(lo_scr)
        main_scr[...] = jnp.zeros_like(main_scr)
        rest_scr[...] = jnp.zeros_like(rest_scr)

    score = score_ref[...]
    logit = jnp.where(score > 0, score, 0.2 * score)
    expo = jnp.exp(logit - jnp.max(logit, axis=1, keepdims=True))
    alpha = expo / jnp.sum(expo, axis=1, keepdims=True)
    main = alpha.astype(bf16).astype(f32)
    rest = (alpha - main).astype(bf16).astype(f32)
    main_scr[:, 0:edges] = jnp.where(score > 0, main, -main)
    rest_scr[:, 0:edges] = jnp.where(score > 0, rest, -rest)
    index = index_ref[...]
    hi_scr[:, 0:edges] = index // WIDE
    lo_scr[:, 0:edges] = (index % WIDE).astype(f32)
    lo_scr[...] = lo_scr[...].T
    grad_t[...] = grad_ref[...].T

    wide_iota = lax.broadcasted_iota(jnp.int32, (edges, WIDE), 1).astype(f32).astype(bf16)
    half_iota = lax.broadcasted_iota(jnp.int32, (HALVES, LANES), 0)
    one = jnp.ones((edges, WIDE), bf16)
    none = jnp.zeros((edges, WIDE), bf16)
    tail = jnp.zeros((LANES - edges, WIDE), bf16)

    def group(g, carry):
        base = pl.multiple_of(g * 8, 8)
        cols = pltpu.roll(lo_scr[0:edges, :], LANES - base, 1).astype(bf16)
        hi = hi_scr[pl.ds(base, 8), :]
        main_g = main_scr[pl.ds(base, 8), :]
        rest_g = rest_scr[pl.ds(base, 8), :]
        for j in range(8):
            here = jnp.broadcast_to(hi[j:j + 1, :], (HALVES, LANES)) == half_iota
            lhs = jnp.concatenate(
                [
                    jnp.where(here, jnp.broadcast_to(main_g[j:j + 1, :], (HALVES, LANES)), 0.0),
                    jnp.where(here, jnp.broadcast_to(rest_g[j:j + 1, :], (HALVES, LANES)), 0.0),
                ],
                axis=0,
            ).astype(bf16)
            col = jnp.broadcast_to(cols[:, j:j + 1], (edges, WIDE))
            rhs = jnp.concatenate([jnp.where(col == wide_iota, one, none), tail], axis=0)
            out = jnp.dot(lhs, rhs, preferred_element_type=f32)
            where = pl.ds(pl.multiple_of((base + j) * 16, 16), 16)
            left_scr[where, :] = out[:, :LANES]
            right_scr[where, :] = out[:, LANES:]
        return carry

    lax.fori_loop(0, BLK // 8, group, 0)

    for h in range(HALVES):
        main_h = jnp.concatenate([r[pl.ds(h, BLK, stride=16), :] for r in (left_scr, right_scr)], axis=1)
        rest_h = jnp.concatenate([r[pl.ds(HALVES + h, BLK, stride=16), :] for r in (left_scr, right_scr)], axis=1)
        dense_ref[0, :, h * WIDE:(h + 1) * WIDE] = main_h + rest_h
        contrib = jnp.dot(grad_t[...], jnp.abs(main_h).astype(bf16), preferred_element_type=f32)
        for part in range(2):
            slot = slots[step, 2 * h + part]
            piece = contrib[:, part * BLK:(part + 1) * BLK]

            @pl.when(slot < per)
            def _():
                own_ref[pl.ds(slot, 1)] += piece[None]

            @pl.when(slot >= per)
            def _():
                acc[pl.ds(slot - per, 1)] += piece[None]

    @pl.when(step == pl.num_programs(0) - 1)
    def _():
        def cast(k, carry):
            core_ref[pl.ds(k, 1)] = acc[pl.ds(k, 1)].astype(bf16)
            far_ref[pl.ds(k, 1)] = acc[pl.ds(per + k, 1)].astype(bf16)
            return carry

        lax.fori_loop(0, per, cast, 0)


def spread(slots, scores, index, grad):
    rows, edges = scores.shape
    width = grad.shape[1]
    blocks = rows // BLK
    per = 3 * blocks
    whole = lambda: pl.BlockSpec((per, width, BLK), lambda b, s: (0, 0, 0), pipeline_mode=pl.Buffered(1))
    return pl.pallas_call(
        functools.partial(spread_body, blocks, edges),
        grid_spec=pltpu.PrefetchScalarGridSpec(
            num_scalar_prefetch=1,
            grid=(blocks,),
            in_specs=[
                pl.BlockSpec((BLK, edges), lambda b, s: (b, 0)),
                pl.BlockSpec((BLK, edges), lambda b, s: (b, 0)),
                pl.BlockSpec((BLK, width), lambda b, s: (b, 0)),
            ],
            out_specs=[
                pl.BlockSpec((1, BLK, NBL * BLK), lambda b, s: (b, 0, 0)),
                whole(), whole(), whole(),
            ],
            scratch_shapes=[
                pltpu.VMEM((BLK, LANES), jnp.int32),
                pltpu.VMEM((BLK, LANES), f32),
                pltpu.VMEM((BLK, LANES), f32),
                pltpu.VMEM((BLK, LANES), f32),
                pltpu.VMEM((width, BLK), bf16),
                pltpu.VMEM((BLK * 16, LANES), f32),
                pltpu.VMEM((BLK * 16, LANES), f32),
                pltpu.VMEM((2 * per, width, BLK), f32),
            ],
        ),
        out_shape=[
            jax.ShapeDtypeStruct((blocks, BLK, NBL * BLK), f32),
            jax.ShapeDtypeStruct((per, width, BLK), f32),
            jax.ShapeDtypeStruct((per, width, BLK), bf16),
            jax.ShapeDtypeStruct((per, width, BLK), bf16),
        ],
        compiler_params=pltpu.CompilerParams(
            dimension_semantics=("arbitrary",), vmem_limit_bytes=56 * MIB
        ),
        cost_estimate=pl.CostEstimate(
            flops=20 * 10**9, bytes_accessed=24 * MIB, transcendentals=rows * LANES
        ),
        name="spread",
    )(slots, scores, index, grad)


def softmax_grad_body(blocks, slots, dense_ref, probe_ref, *rest):
    tables = rest[:9]
    sums_ref, du_ref, vec_ref, table, prod, sem = rest[9:]
    step = pl.program_id(0)
    width = vec_ref.shape[1]

    @pl.when(step == 0)
    def _():
        copies = [
            pltpu.make_async_copy(t, table.at[pl.ds(k * blocks, blocks)], sem.at[k])
            for k, t in enumerate(tables)
        ]
        for copy in copies:
            copy.start()
        sums_ref[...] = jnp.zeros_like(sums_ref)
        for copy in copies:
            copy.wait()

    inner = jnp.zeros((BLK, BLK), f32)
    total = jnp.zeros((BLK, BLK), f32)
    for s in range(NBL):
        cols = slice(s * BLK, (s + 1) * BLK)
        cand = table[slots[step, s]]
        d = lax.dot_general(
            probe_ref[...], cand, (((1,), (1,)), ((), ())), preferred_element_type=f32
        )
        prod[:, cols] = d
        a = jnp.abs(dense_ref[0, :, cols])
        inner = inner + a * d
        total = total + a
    mean = jnp.sum(inner, axis=1, keepdims=True) / jnp.sum(total, axis=1, keepdims=True)
    du = jnp.zeros((BLK, BLK), f32)
    for s in range(NBL):
        cols = slice(s * BLK, (s + 1) * BLK)
        a = dense_ref[0, :, cols]
        dz = jnp.where(a > 0, a, -0.2 * a) * (prod[:, cols] - mean)
        du = du + dz
        slot = slots[step, s]
        sums_ref[pl.ds(slot, 1)] += jnp.sum(dz, axis=0, keepdims=True)[None]
    row = jnp.broadcast_to(jnp.sum(du, axis=1, keepdims=True), (BLK, BLK)).T
    du_ref[pl.ds(step, 1)] = row[0:1, :][None]

    @pl.when(step == pl.num_programs(0) - 1)
    def _():
        sub = lax.broadcasted_iota(jnp.int32, (16, BLK), 0)

        def two_rows(row):
            row = jnp.broadcast_to(row, (16, BLK))
            main = row.astype(bf16).astype(f32)
            both = jnp.where(sub == 0, main, jnp.where(sub == 1, row - main, 0.0))
            return both.astype(bf16)

        def product(ref, first):
            lhs = jnp.concatenate([two_rows(ref[first + k]) for k in range(blocks)], axis=1)
            rhs = table[pl.ds(first, blocks)].reshape(blocks * BLK, width)
            out = jnp.dot(lhs, rhs, preferred_element_type=f32)
            return out[0:1, :] + out[1:2, :]

        vec_ref[0:1, :] = product(du_ref, 0)
        vec_ref[1:2, :] = lax.fori_loop(
            0, 9, lambda k, v: v + product(sums_ref, pl.multiple_of(k * blocks, blocks)),
            jnp.zeros((1, width), f32),
        )


def softmax_grad(slots, dense, probe, tables):
    blocks = dense.shape[0]
    width = probe.shape[1]
    count = 9 * blocks
    return pl.pallas_call(
        functools.partial(softmax_grad_body, blocks),
        grid_spec=pltpu.PrefetchScalarGridSpec(
            num_scalar_prefetch=1,
            grid=(blocks,),
            in_specs=[
                pl.BlockSpec((1, BLK, NBL * BLK), lambda b, s: (b, 0, 0)),
                pl.BlockSpec((BLK, width), lambda b, s: (b, 0)),
            ] + [pl.BlockSpec(memory_space=pl.ANY)] * 9,
            out_specs=[
                pl.BlockSpec((count, 1, BLK), lambda b, s: (0, 0, 0)),
                pl.BlockSpec((blocks, 1, BLK), lambda b, s: (0, 0, 0)),
                pl.BlockSpec((2, width), lambda b, s: (0, 0)),
            ],
            scratch_shapes=[
                pltpu.VMEM((count, BLK, width), bf16),
                pltpu.VMEM((BLK, NBL * BLK), f32),
                pltpu.SemaphoreType.DMA((9,)),
            ],
        ),
        out_shape=[
            jax.ShapeDtypeStruct((count, 1, BLK), f32),
            jax.ShapeDtypeStruct((blocks, 1, BLK), f32),
            jax.ShapeDtypeStruct((2, width), f32),
        ],
        compiler_params=pltpu.CompilerParams(
            dimension_semantics=("arbitrary",), vmem_limit_bytes=40 * MIB
        ),
        cost_estimate=pl.CostEstimate(
            flops=8 * 10**9, bytes_accessed=20 * MIB, transcendentals=0
        ),
        name="softmax_grad",
    )(slots, dense, probe, *tables)


def weight_body(blocks, place, own_ref, twin_ref, far_ref, *rest):
    tables = rest[:9]
    out_ref, own, twin, far, table, total, sem = rest[9:]
    per = 3 * blocks
    copies = []
    for k in range(9):
        src, dst = ((own_ref, own), (twin_ref, twin), (far_ref, far))[k // 3]
        piece = pl.ds(k % 3 * blocks, blocks)
        copies.append((
            pltpu.make_async_copy(src.at[piece], dst.at[piece], sem.at[k]),
            pltpu.make_async_copy(tables[k], table.at[pl.ds(k * blocks, blocks)], sem.at[9 + k]),
        ))
    for pair in copies:
        for copy in pair:
            copy.start()
    for k in range(9):
        for copy in copies[k]:
            copy.wait()
        part = (own, twin, far)[k // 3]
        lhs = jnp.concatenate(
            [part[k % 3 * blocks + b].astype(bf16) for b in range(blocks)], axis=1
        )
        rhs = table[k * blocks:(k + 1) * blocks].reshape(blocks * BLK, table.shape[2])
        term = jnp.dot(lhs, rhs, preferred_element_type=f32)
        if k == 0:
            total[...] = term
        else:
            total[...] += term
    across = total.shape[1] // LANES
    for q in range(out_ref.shape[0]):
        r, c = q // across * 16, q % across * LANES
        out_ref[pl.ds(place[q], 1)] = total[r:r + 16, c:c + LANES][None]


def weight_terms(place, own, twin, far, tables):
    per, width, _ = own.shape
    depth = tables[0].shape[2]
    chunks = width * depth // (16 * LANES)
    return pl.pallas_call(
        functools.partial(weight_body, per // 3),
        grid_spec=pltpu.PrefetchScalarGridSpec(
            num_scalar_prefetch=1,
            grid=(1,),
            in_specs=[pl.BlockSpec(memory_space=pl.ANY)] * 12,
            out_specs=pl.BlockSpec((chunks, 16, LANES), lambda i, p: (0, 0, 0)),
            scratch_shapes=[
                pltpu.VMEM((per, width, BLK), f32),
                pltpu.VMEM((per, width, BLK), bf16),
                pltpu.VMEM((per, width, BLK), bf16),
                pltpu.VMEM((3 * per, BLK, depth), bf16),
                pltpu.VMEM((width, depth), f32),
                pltpu.SemaphoreType.DMA((18,)),
            ],
        ),
        out_shape=jax.ShapeDtypeStruct((chunks, 16, LANES), f32),
        compiler_params=pltpu.CompilerParams(
            dimension_semantics=("arbitrary",), vmem_limit_bytes=48 * MIB
        ),
        cost_estimate=pl.CostEstimate(
            flops=6 * 10**9, bytes_accessed=22 * MIB, transcendentals=0
        ),
        name="weight_terms",
    )(place, own, twin, far, *tables)


def finish_weight_body(scale, place, parts_ref, vec_ref, src_ref, dst_ref, out_ref, total):
    across = total.shape[1] // LANES
    for q in range(parts_ref.shape[0]):
        r, c = q // across * 16, q % across * LANES
        total[r:r + 16, c:c + LANES] = parts_ref[place[q]].astype(f32)
    full = total[...] + src_ref[...] * vec_ref[0:1, :] + dst_ref[...] * vec_ref[1:2, :]
    out_ref[...] = full.T * scale


def finish_weight(place, parts, vec, src, dst, scale):
    width, depth = src.shape[0], vec.shape[1]
    whole = lambda shape: pl.BlockSpec(shape, lambda i, p: (0,) * len(shape))
    return pl.pallas_call(
        functools.partial(finish_weight_body, scale),
        grid_spec=pltpu.PrefetchScalarGridSpec(
            num_scalar_prefetch=1,
            grid=(1,),
            in_specs=[whole(parts.shape), whole(vec.shape), whole(src.shape), whole(dst.shape)],
            out_specs=whole((depth, width)),
            scratch_shapes=[pltpu.VMEM((width, depth), f32)],
        ),
        out_shape=jax.ShapeDtypeStruct((depth, width), f32),
        compiler_params=pltpu.CompilerParams(
            dimension_semantics=("arbitrary",), vmem_limit_bytes=16 * MIB
        ),
        name="finish_weight",
    )(place, parts, vec, src, dst)


def finish_features_body(own_ref, twin_ref, far_ref, above_ref, below_ref, du_ref, sums_ref,
                         src_ref, dst_ref, weight_ref, out_ref):
    total = own_ref[0] + twin_ref[0].astype(f32) + far_ref[0].astype(f32)
    total = total + above_ref[0].astype(f32) + below_ref[0].astype(f32)
    total = total + src_ref[...] * du_ref[0] + dst_ref[...] * sums_ref[0]
    out_ref[...] = lax.dot_general(
        total.T.astype(bf16), weight_ref[...], (((1,), (1,)), ((), ())),
        preferred_element_type=f32,
    ).astype(bf16)


def finish_features(own, twin, far, above, below, du, sums, src, dst, weight):
    blocks, width, _ = above.shape
    depth = weight.shape[0]
    tile = pl.BlockSpec((1, width, BLK), lambda b: (b, 0, 0))
    line = pl.BlockSpec((1, 1, BLK), lambda b: (b, 0, 0))
    column = pl.BlockSpec((width, 1), lambda b: (0, 0))
    return pl.pallas_call(
        finish_features_body,
        grid=(blocks,),
        in_specs=[tile] * 5 + [line] * 2 + [column] * 2
        + [pl.BlockSpec(weight.shape, lambda b: (0, 0))],
        out_specs=pl.BlockSpec((BLK, depth), lambda b: (b, 0)),
        out_shape=jax.ShapeDtypeStruct((blocks * BLK, depth), bf16),
        compiler_params=pltpu.CompilerParams(
            dimension_semantics=("arbitrary",), vmem_limit_bytes=16 * MIB
        ),
        cost_estimate=pl.CostEstimate(
            flops=10**9, bytes_accessed=8 * MIB, transcendentals=0
        ),
        name="finish_features",
    )(own, twin, far, above, below, du, sums, src, dst, weight)


def ring(axis, low, count, offset):
    size = lax.axis_size(axis)
    turned = lambda i: ((i >> low) + offset) % count - (i >> low) % count
    return [(i, i + (turned(i) << low)) for i in range(size)]


def summed(parts, stages):
    tail = parts.shape[1:]
    parts = parts.reshape(tuple(n for _, _, n in stages) + tail)
    for axis, low, count in stages:
        total = parts[0]
        for k in range(1, count):
            total = total + lax.ppermute(parts[k], axis, ring(axis, low, count, k))
        parts = total
    for axis, low, count in stages[::-1]:
        parts = jnp.stack(
            [parts]
            + [lax.ppermute(parts, axis, ring(axis, low, count, k)) for k in range(1, count)]
        )
    return parts.reshape((-1,) + tail)


def summed_whole(array, stages):
    for axis, low, count in stages:
        others = [lax.ppermute(array, axis, ring(axis, low, count, k)) for k in range(1, count)]
        array = sum(others, array)
    return array


def places(stages, sign):
    chunk = jnp.arange(math.prod(n for _, _, n in stages), dtype=jnp.int32)
    place, stride = jnp.zeros_like(chunk), 1
    for axis, low, count in stages[::-1]:
        here = (lax.axis_index(axis) >> low) % count
        place = place + (sign * (chunk // stride % count - here)) % count * stride
        stride = stride * count
    return place


def on_device(features, weight, attn_src, attn_dst, upstream, scores, neighbour_lists, edge_index):
    rows, depth = features.shape
    width = weight.shape[1]
    blocks = rows // BLK
    size_x = lax.axis_size("gx")
    size_y = lax.axis_size("gy")
    here_x = lax.axis_index("gx")
    here_y = lax.axis_index("gy")
    twin = [(i, i ^ 1) for i in range(size_x)]
    far = [(i, (((i + 1) ^ 1) - 1) % size_x) for i in range(size_x)]
    up = [(i, (i + 1) % size_y) for i in range(size_y)]
    down = [(i, (i - 1) % size_y) for i in range(size_y)]

    owner = neighbour_lists // blocks
    owner_x, owner_y = owner // size_y, owner % size_y
    part_x = jnp.where(owner_x == here_x, 0, jnp.where(owner_x // 2 == here_x // 2, 1, 2))
    part_y = jnp.where(owner_y == here_y, 0, jnp.where(owner_y == (here_y + 1) % size_y, 1, 2))
    slots = (part_x * 3 + part_y) * blocks + neighbour_lists % blocks

    own = features.reshape(blocks, BLK, depth)
    above = lax.ppermute(own, "gy", down)
    below = lax.ppermute(own, "gy", up)
    tables = [own, above, below]
    tables = tables + [lax.ppermute(t, "gx", twin) for t in tables] + [
        lax.ppermute(t, "gx", far) for t in tables
    ]

    dense, acc_own, acc_twin, acc_far = spread(slots, scores, edge_index, upstream)
    probe = lax.dot_general(
        upstream, weight, (((1,), (1,)), ((), ())), preferred_element_type=f32
    ).astype(bf16)

    stages = (("gx", 0, 2), ("gx", 1, size_x // 2), ("gy", 0, 4), ("gy", 2, size_y // 4))
    terms = weight_terms(places(stages, 1), acc_own, acc_twin, acc_far, tables)
    weight_total = summed(terms, stages)

    split = (3, blocks, width, BLK)
    acc_own = acc_own.reshape(split)
    from_twin = lax.ppermute(acc_twin, "gx", twin).reshape(split)
    from_far = lax.ppermute(acc_far, "gx", far).reshape(split)
    column = [
        (acc_own[k] + from_twin[k].astype(f32) + from_far[k].astype(f32)).astype(bf16)
        for k in (1, 2)
    ]
    from_below = lax.ppermute(column[0], "gy", up)
    from_above = lax.ppermute(column[1], "gy", down)

    sums, du, vec = softmax_grad(slots, dense, probe, tables)
    sums = sums.reshape(3, 3, blocks, 1, BLK)
    sums = sums[0] + lax.ppermute(sums[1], "gx", twin) + lax.ppermute(sums[2], "gx", far)
    sums = sums[0] + lax.ppermute(sums[1], "gy", up) + lax.ppermute(sums[2], "gy", down)

    src = attn_src[:, None]
    dst = attn_dst[:, None]
    grad_features = finish_features(
        acc_own[0], from_twin[0], from_far[0], from_above, from_below, du, sums, src, dst, weight
    )

    scale = 1.0 / math.sqrt(rows * size_x * size_y)
    vec = summed_whole(vec, stages)
    vectors = jnp.dot(vec, weight.astype(f32), precision=lax.Precision.HIGHEST) * scale
    grad_weight = finish_weight(places(stages, -1), weight_total, vec, src, dst, scale)
    return (grad_features, grad_weight, vectors[0], vectors[1])


def solution(mesh):
    rows = P(("gx", "gy"), None)
    return jax.shard_map(
        on_device,
        mesh=mesh,
        in_specs=(rows, P(), P(), P(), rows, rows, rows, rows),
        out_specs=(rows, P(), P(), P()),
        check_vma=False,
    )
```

time: 914 us -> 244 us (0.27)
  matrix products: 351 us -> 2.34 us
  waiting for transfers between devices: 257 us -> 51 us
  local copies, waits for them, and re-layouts: 120 us -> 8.56 us
  Pallas kernels: 0 us -> 109 us
  blocking collectives: 75 us -> 0 us
  other arithmetic: 73.2 us -> 4.85 us
  starting transfers between devices: 19.9 us -> 63.5 us
  between operations: 14.1 us -> 1.04 us
    dot_general x75 -> x2, matrix products: 351 us -> 2.34 us  [the longest x1 2.04 us: on_device(): lax.dot_general(upstream, weight, (((1,), (1,)), ((), ())), preferred_ele...]
    ppermute x8 -> x46, waiting for transfers between devices: 178 us -> 51 us  [the longest x10 15 us: summed(): total = total + lax.ppermute(parts[k], axis, ring(axis, low, count, k))]
    pallas_call x0 -> x5, Pallas kernels: none -> 109 us  [the longest x1 77 us: spread(): pl.pallas_call(functools.partial(spread_body, blocks, edges), grid_spec=p...]
    psum x1 -> x0, waiting for transfers between devices: 79 us -> none  [on_device(): lax.psum((weight_term, src_acc, dst_acc), ('gx', 'gy'))]
    psum x1 -> x0, blocking collectives: 75 us -> none  [on_device(): lax.psum((weight_term, src_acc, dst_acc), ('gx', 'gy'))]
    reshape x17 -> x0, local copies, waits for them, and re-layouts: 60.6 us -> none  [the longest x8 32 us: step(): contrib.reshape(nlist, node_block * block_width)]
    ppermute x8 -> x46, starting transfers between devices: 19.9 us -> 63.5 us  [the longest x10 13.1 us: summed(): lax.ppermute(parts, axis, ring(axis, low, count, k))]
    squeeze x4 -> x3, local copies, waits for them, and re-layouts: 23.3 us -> 0.04 us  [summed(): total = total + lax.ppermute(parts[k], axis, ring(axis, low, count, k))]
  transfers between devices with their start and end apart: 9 -> 46, of which waited for: 6 -> 17; matrix products, arithmetic and copies ran while one was open for 2% -> 6% of each run, Pallas kernels for 0% -> 43%
where the time goes in v1:
time: 244 us; the launch traced here: 241 us
  Pallas kernels  109 us (45%)
  starting transfers between devices  63.5 us (26%)
  waiting for transfers between devices  51 us (21%)
  local copies, waits for them, and re-layouts  8.56 us (4%)
  other arithmetic  4.85 us (2%)
    pallas_call x1, Pallas kernels, spread(): pl.pallas_call(functools.partial(spread_body, blocks, edges), grid_spec=p...  77 us
    pallas_call x1, Pallas kernels, softmax_grad(): pl.pallas_call(functools.partial(softmax_grad_body, blocks), grid_spec=pl...  17 us
    ppermute x10, waiting for transfers between devices, summed(): total = total + lax.ppermute(parts[k], axis, ring(axis, low, count, k))  15 us
    ppermute x1, waiting for transfers between devices, on_device(): lax.ppermute(sums[1], 'gy', up)  14.5 us
    ppermute x1, waiting for transfers between devices, on_device(): above = lax.ppermute(own, 'gy', down)  14.4 us
    ppermute x10, starting transfers between devices, summed(): lax.ppermute(parts, axis, ring(axis, low, count, k))  13.1 us
    ppermute x10, starting transfers between devices, summed_whole(): lax.ppermute(array, axis, ring(axis, low, count, k))  10.8 us
    ppermute x10, starting transfers between devices, summed(): total = total + lax.ppermute(parts[k], axis, ring(axis, low, count, k))  8.71 us
  transfers between devices with their start and end apart: 46, of which 17 were waited for; matrix products, arithmetic and copies ran while one was open for 6% of the time, Pallas kernels for 43%

profile of v1, /device:TPU:1, one launch (start us, length us, event | category | flops | bytes accessed | tf_op | source)
XLA Modules:
  0.0 240.5 jit_solution(11739819960993266386)
XLA Ops:
  0.6 5.8 %collective-permute-start.4 = (bf16[8,128,512]{2,1,0:T(8,128)(2,1)}, bf16[8,128,512]{2,1,0:T(8,128)(2,1)S(1)}, u32[]{:S(2)}, u32[]{:S(2)}) collective-permute-start(bf16[8,128,512]{2,1,0:T(8,128)(2,1)} %bitcast.83), channel_id=1, source_target_pairs={{0,15},{1,0},{2,1},{3,2},{4,3},{5,4},{6,5},{7,6},{8,7},{9,8},{10,9... | collective-permute-start | bytes 3145736 | tf_op jit(solution)/shard_map/ppermute | solution.py:446
  6.5 1.0 collective-permute-start.6
  7.4 1.5 collective-permute-start.9
  8.9 2.0 copy.15.score_ref
  10.9 2.0 copy.16.index_ref
  12.9 1.3 fusion.11.slots
  14.2 14.4 %collective-permute-done.4.rest_1_ = bf16[8,128,512]{2,1,0:T(8,128)(2,1)S(1)} collective-permute-done((bf16[8,128,512]{2,1,0:T(8,128)(2,1)}, bf16[8,128,512]{2,1,0:T(8,128)(2,1)S(1)}, u32[]{:S(2)}, u32[]{:S(2)}) %collective-permute-start.4) | collective-permute-done | bytes 1048608 | tf_op jit(solution)/shard_map/ppermute | solution.py:446
  28.6 3.1 %collective-permute-start.10 = (bf16[8,128,512]{2,1,0:T(8,128)(2,1)S(1)}, bf16[8,128,512]{2,1,0:T(8,128)(2,1)}, u32[]{:S(2)}, u32[]{:S(2)}) collective-permute-start(bf16[8,128,512]{2,1,0:T(8,128)(2,1)S(1)} %collective-permute-done.4.rest_1_), channel_id=1, source_target_pairs={{0,112},{16,32},{32,16},{48,64},{64,48},{80,96},{96,80},{112,0},{1... | collective-permute-start | bytes 3145736 | tf_op jit(solution)/shard_map/ppermute | solution.py:450
  31.7 1.1 collective-permute-start.7
  32.8 1.0 collective-permute-done.5.rest_2_
  33.8 3.4 %collective-permute-start.11 = (bf16[8,128,512]{2,1,0:T(8,128)(2,1)}, bf16[8,128,512]{2,1,0:T(8,128)(2,1)}, u32[]{:S(2)}, u32[]{:S(2)}) collective-permute-start(bf16[8,128,512]{2,1,0:T(8,128)(2,1)} %collective-permute-done.5.rest_2_), channel_id=1, source_target_pairs={{0,112},{16,32},{32,16},{48,64},{64,48},{80,96},{96,80},{112,0},{1... | collective-permute-start | bytes 3145736 | tf_op jit(solution)/shard_map/ppermute | solution.py:450
  37.2 1.0 copy-done.2
  38.2 0.8 collective-permute-start.8
  38.9 77.0 %spread.1 = (f32[8,128,2048]{2,1,0:T(8,128)}, f32[24,512,128]{2,1,0:T(8,128)}, bf16[24,512,128]{2,1,0:T(8,128)(2,1)}, bf16[24,512,128]{2,1,0:T(8,128)(2,1)}) custom-call(s32[8,16]{1,0:T(8,128)} %fusion.11.slots, f32[1024,80]{1,0:T(8,128)} %copy.15.score_ref, s32[1024,80]{1,0:T(8,128)} %copy.16.index_ref, bf16[1024,512]{1,0:T(8,128)(2,1)} %grad_ref.1), custom_call_target="tpu_custom_call" | custom-call | flops 20000000000 | bytes 25165824 | tf_op jit(solution)/shard_map/spread/pallas_call | solution.py:114
  116.4 2.0 convolution_convert_fusion.probe_ref
  118.6 1.4 collective-permute-start.1
  120.0 8.1 %weight_terms.1 = f32[128,16,128]{2,1,0:T(8,128)S(1)} custom-call(s32[128]{0:T(128)S(1)} %fusion.32.place, f32[24,512,128]{2,1,0:T(8,128)} %get-tuple-element.11.own_ref, bf16[24,512,128]{2,1,0:T(8,128)(2,1)} %get-tuple-element.12.twin_ref, bf16[24,512,128]{2,1,0:T(8,128)(2,1)} %get-tuple-element.13.far_ref, bf16[8,128,512]{2,1,0:T(8,128)(2,1)S(1)} %bitcast.87, ...), custom_call_target="tpu_custom_call" | custom-call | flops 6000000000 | bytes 23068672 | tf_op jit(solution)/shard_map/weight_terms/pallas_call | solution.py:297
  128.1 0.8 collective-permute-start.16
  129.0 17.0 %softmax_grad.1 = (f32[72,1,128]{2,1,0:T(1,128)S(1)}, f32[8,1,128]{2,1,0:T(1,128)S(1)}, f32[2,512]{1,0:T(2,128)S(1)}) custom-call(s32[8,16]{1,0:T(8,128)S(1)} %copy-done.4, f32[8,128,2048]{2,1,0:T(8,128)} %get-tuple-element.14.dense_ref, bf16[1024,512]{1,0:T(8,128)(2,1)S(1)} %convolution_convert_fusion.probe_ref, bf16[8,128,512]{2,1,0:T(8,128)(2,1)S(1)} %bitcast.88, ...), custom_call_target="tpu_custom_call" | custom-call | flops 8000000000 | bytes 20971520 | tf_op jit(solution)/shard_map/softmax_grad/pallas_call | solution.py:224
  146.0 0.3 collective-permute-start.36
  146.5 1.1 collective-permute-start.17
  147.5 1.9 collective-permute-start.18
  149.5 0.8 collective-permute-start.19
  150.3 10.5 %collective-permute-done.17 = f32[4,4,16,128]{3,2,1,0:T(8,128)S(1)} collective-permute-done((f32[4,4,16,128]{3,2,1,0:T(8,128)S(1)}, f32[4,4,16,128]{3,2,1,0:T(8,128)S(1)}, u32[]{:S(2)}, u32[]{:S(2)}) %collective-permute-start.17) | collective-permute-done | bytes 131104 | tf_op jit(solution)/shard_map/ppermute | solution.py:399
  160.8 1.5 collective-permute-done.18
  162.3 1.6 collective-permute-start.38
  163.9 2.1 collective-permute-start.39
  166.1 0.2 collective-permute-done.38
  166.3 0.4 collective-permute-done.39
  166.7 2.1 collective-permute-start.22
  168.9 1.5 collective-permute-done.20
  170.4 0.6 collective-permute-done.21
  171.0 0.7 collective-permute-start.41
  171.7 1.8 collective-permute-start.42
  173.5 0.5 collective-permute-done.40
  174.1 0.9 collective-permute-done.41
  174.9 1.9 collective-permute-start.25
  176.8 0.9 collective-permute-done.23
  177.8 3.7 %collective-permute-start.12 = (f32[3,8,1,128]{3,1,2,0:T(8,128)S(1)}, f32[3,8,1,128]{3,1,2,0:T(8,128)S(1)}, u32[]{:S(2)}, u32[]{:S(2)}) collective-permute-start(f32[3,8,1,128]{3,1,2,0:T(8,128)S(1)} %bitcast.104), channel_id=1, source_target_pairs={{0,16},{16,0},{32,48},{48,32},{64,80},{80,64},{96,112},{112,96},{1... | collective-permute-start | bytes 36872 | tf_op jit(solution)/shard_map/ppermute | solution.py:475
  181.5 2.1 collective-permute-start.13
  183.7 0.5 collective-permute-start.27
  184.2 0.8 collective-permute-done.13
  184.9 1.5 collective-permute-start.28
  186.4 0.9 collective-permute-done.26
  187.3 0.4 collective-permute-done.27
  187.7 0.6 collective-permute-done.28
  188.3 2.3 collective-permute-start.30
  190.6 0.4 collective-permute-start.31
  191.0 1.3 collective-permute-done.29
  192.3 1.4 collective-permute-start.43
  193.7 1.8 collective-permute-start.44
  195.6 0.9 collective-permute-start.45
  196.6 4.1 %collective-permute-start.33 = (f32[4,4,16,128]{3,2,1,0:T(8,128)S(1)}, f32[4,4,16,128]{3,2,1,0:T(8,128)S(1)}, u32[]{:S(2)}, u32[]{:S(2)}) collective-permute-start(f32[4,4,16,128]{3,2,1,0:T(8,128)S(1)} %get-tuple-element.29), channel_id=1, source_target_pairs={{0,64},{16,80},{32,96},{48,112},{64,0},{80,16},{96,32},{112,48},{1... | collective-permute-start | bytes 393224 | tf_op jit(solution)/shard_map/ppermute | solution.py:404
  200.7 3.1 %add_convert_fusion = (bf16[8,512,128]{2,1,0:T(8,128)(2,1)S(1)}, bf16[8,512,128]{2,1,0:T(8,128)(2,1)S(1)}, f32[8,512,128]{2,1,0:T(8,128)S(1)}) fusion(f32[24,512,128]{2,1,0:T(8,128)S(1)} %bitcast.90, bf16[24,512,128]{2,1,0:T(8,128)(2,1)} %collective-permute-done.1, bf16[24,512,128]{2,1,0:T(8,128)(2,1)} %collective-permute-done), kind=kLoop, calls=%fused_computation | loop fusion | flops 5242880 | bytes 14680064 | tf_op jit(solution)/shard_map/convert_element_type | solution.py:467
  204.0 2.1 collective-permute-start.2
  206.2 4.8 %collective-permute-start.15 = (f32[8,1,128]{2,1,0:T(1,128)S(1)}, f32[8,1,128]{2,1,0:T(1,128)S(1)}, u32[]{:S(2)}, u32[]{:S(2)}) collective-permute-start(f32[8,1,128]{2,1,0:T(1,128)S(1)} %bitcast.108), channel_id=1, source_target_pairs={{0,15},{1,0},{2,1},{3,2},{4,3},{5,4},{6,5},{7,6},{8,7},{9,8},{10,9... | collective-permute-start | bytes 12296 | tf_op jit(solution)/shard_map/ppermute | solution.py:476
  211.2 4.1 %collective-permute-start.35 = (f32[4,4,4,16,128]{4,3,2,1,0:T(8,128)S(1)}, f32[4,4,4,16,128]{4,3,2,1,0:T(8,128)S(1)}, u32[]{:S(2)}, u32[]{:S(2)}) collective-permute-start(f32[4,4,4,16,128]{4,3,2,1,0:T(8,128)S(1)} %get-tuple-element.24), channel_id=1, source_target_pairs={{0,16},{16,0},{32,48},{48,32},{64,80},{80,64},{96,112},{112,96},{1... | collective-permute-start | bytes 1572872 | tf_op jit(solution)/shard_map/ppermute | solution.py:404
  215.3 0.3 convolution_multiply_fusion
  215.6 0.6 fusion.50
  216.2 14.5 %collective-permute-done.14 = f32[8,1,128]{2,0,1:T(8,128)S(1)} collective-permute-done((f32[8,1,128]{2,0,1:T(8,128)S(1)}, f32[8,1,128]{2,0,1:T(8,128)S(1)}, u32[]{:S(2)}, u32[]{:S(2)}) %collective-permute-start.14) | collective-permute-done | bytes 4128 | tf_op jit(solution)/shard_map/ppermute | solution.py:476
  230.7 1.3 slice.138.twin_ref
  232.0 1.3 slice.139.far_ref
  233.4 2.0 finish_weight.1
  235.4 5.1 %finish_features.1 = bf16[1024,512]{1,0:T(8,128)(2,1)} custom-call(f32[8,512,128]{2,1,0:T(8,128)S(1)} %get-tuple-element.20.own_ref, bf16[8,512,128]{2,1,0:T(8,128)(2,1)S(1)} %slice.138.twin_ref, bf16[8,512,128]{2,1,0:T(8,128)(2,1)S(1)} %slice.139.far_ref, bf16[8,512,128]{2,1,0:T(8,128)(2,1)S(1)} %collective-permute-done.2.above_ref, ...), custom_call_target="tpu_custom_call" | custom-call | flops 1000000000 | bytes 8388608 | tf_op jit(solution)/shard_map/finish_features/pallas_call | solution.py:370
  (86 shorter events, 1.5 us)
Async XLA Ops:
  0.6 28.0 %collective-permute-start.4 = (bf16[8,128,512]{2,1,0:T(8,128)(2,1)}, bf16[8,128,512]{2,1,0:T(8,128)(2,1)S(1)}, u32[]{:S(2)}, u32[]{:S(2)}) collective-permute-start(bf16[8,128,512]{2,1,0:T(8,128)(2,1)} %bitcast.83), channel_id=1, source_target_pairs={{0,15},{1,0},{2,1},{3,2},{4,3},{5,4},{6,5},{7,6},{8,7},{9,8},{10,9... | collective-permute-start | bytes 3145736 | tf_op jit(solution)/shard_map/ppermute | solution.py:446
  6.5 27.3 %collective-permute-start.5 = (bf16[8,128,512]{2,1,0:T(8,128)(2,1)}, bf16[8,128,512]{2,1,0:T(8,128)(2,1)}, u32[]{:S(2)}, u32[]{:S(2)}) collective-permute-start(bf16[8,128,512]{2,1,0:T(8,128)(2,1)} %bitcast.84), channel_id=1, source_target_pairs={{0,1},{1,2},{2,3},{3,4},{4,5},{5,6},{6,7},{7,8},{8,9},{9,10},{10,1... | collective-permute-start | bytes 3145736 | tf_op jit(solution)/shard_map/ppermute | solution.py:447
  6.5 30.7 %collective-permute-start.6 = (bf16[8,128,512]{2,1,0:T(8,128)(2,1)}, bf16[8,128,512]{2,1,0:T(8,128)(2,1)S(1)}, u32[]{:S(2)}, u32[]{:S(2)}) collective-permute-start(bf16[8,128,512]{2,1,0:T(8,128)(2,1)} %bitcast.85), channel_id=1, source_target_pairs={{0,16},{16,0},{32,48},{48,32},{64,80},{80,64},{96,112},{112,96},{1... | collective-permute-start | bytes 3145736 | tf_op jit(solution)/shard_map/ppermute | solution.py:449
  7.4 111.0 %collective-permute-start.9 = (bf16[8,128,512]{2,1,0:T(8,128)(2,1)}, bf16[8,128,512]{2,1,0:T(8,128)(2,1)}, u32[]{:S(2)}, u32[]{:S(2)}) collective-permute-start(bf16[8,128,512]{2,1,0:T(8,128)(2,1)} %bitcast.86), channel_id=1, source_target_pairs={{0,112},{16,32},{32,16},{48,64},{64,48},{80,96},{96,80},{112,0},{1... | collective-permute-start | bytes 3145736 | tf_op jit(solution)/shard_map/ppermute | solution.py:450
  14.2 101.8 %copy-start.5 = (f32[512]{0:T(512)S(1)}, f32[512]{0:T(512)}, u32[]{:S(2)}) copy-start(f32[512]{0:T(512)} %param.10) | copy-start | bytes 6148
  14.2 101.9 %copy-start.6 = (f32[512]{0:T(512)S(1)}, f32[512]{0:T(512)}, u32[]{:S(2)}) copy-start(f32[512]{0:T(512)} %param.11) | copy-start | bytes 6148
  14.2 102.2 %copy-start = (bf16[512,512]{1,0:T(8,128)(2,1)S(1)}, bf16[512,512]{1,0:T(8,128)(2,1)}, u32[]{:S(2)}) copy-start(bf16[512,512]{1,0:T(8,128)(2,1)} %weight_ref.1) | copy-start | bytes 1572868
  28.6 90.0 %collective-permute-start.10 = (bf16[8,128,512]{2,1,0:T(8,128)(2,1)S(1)}, bf16[8,128,512]{2,1,0:T(8,128)(2,1)}, u32[]{:S(2)}, u32[]{:S(2)}) collective-permute-start(bf16[8,128,512]{2,1,0:T(8,128)(2,1)S(1)} %collective-permute-done.4.rest_1_), channel_id=1, source_target_pairs={{0,112},{16,32},{32,16},{48,64},{64,48},{80,96},{96,80},{112,0},{1... | collective-permute-start | bytes 3145736 | tf_op jit(solution)/shard_map/ppermute | solution.py:450
  31.7 88.3 %collective-permute-start.7 = (bf16[8,128,512]{2,1,0:T(8,128)(2,1)S(1)}, bf16[8,128,512]{2,1,0:T(8,128)(2,1)}, u32[]{:S(2)}, u32[]{:S(2)}) collective-permute-start(bf16[8,128,512]{2,1,0:T(8,128)(2,1)S(1)} %collective-permute-done.4.rest_1_), channel_id=1, source_target_pairs={{0,16},{16,0},{32,48},{48,32},{64,80},{80,64},{96,112},{112,96},{1... | collective-permute-start | bytes 3145736 | tf_op jit(solution)/shard_map/ppermute | solution.py:449
  33.8 86.1 %collective-permute-start.11 = (bf16[8,128,512]{2,1,0:T(8,128)(2,1)}, bf16[8,128,512]{2,1,0:T(8,128)(2,1)}, u32[]{:S(2)}, u32[]{:S(2)}) collective-permute-start(bf16[8,128,512]{2,1,0:T(8,128)(2,1)} %collective-permute-done.5.rest_2_), channel_id=1, source_target_pairs={{0,112},{16,32},{32,16},{48,64},{64,48},{80,96},{96,80},{112,0},{1... | collective-permute-start | bytes 3145736 | tf_op jit(solution)/shard_map/ppermute | solution.py:450
  37.2 1.0 copy-start.2
  38.2 81.8 %collective-permute-start.8 = (bf16[8,128,512]{2,1,0:T(8,128)(2,1)}, bf16[8,128,512]{2,1,0:T(8,128)(2,1)}, u32[]{:S(2)}, u32[]{:S(2)}) collective-permute-start(bf16[8,128,512]{2,1,0:T(8,128)(2,1)} %collective-permute-done.5.rest_2_), channel_id=1, source_target_pairs={{0,16},{16,0},{32,48},{48,32},{64,80},{80,64},{96,112},{112,96},{1... | collective-permute-start | bytes 3145736 | tf_op jit(solution)/shard_map/ppermute | solution.py:449
  116.0 4.0 %copy-start.1 = (bf16[1024,512]{1,0:T(8,128)(2,1)S(1)}, bf16[1024,512]{1,0:T(8,128)(2,1)}, u32[]{:S(2)}) copy-start(bf16[1024,512]{1,0:T(8,128)(2,1)} %param.8) | copy-start | bytes 3145732
  116.3 3.6 %copy-start.3 = (bf16[8,128,512]{2,1,0:T(8,128)(2,1)S(1)}, bf16[8,128,512]{2,1,0:T(8,128)(2,1)}, u32[]{:S(2)}) copy-start(bf16[8,128,512]{2,1,0:T(8,128)(2,1)} %copy-done.2) | copy-start | bytes 3145732
  118.4 78.1 %collective-permute-start = (bf16[24,512,128]{2,1,0:T(8,128)(2,1)}, bf16[24,512,128]{2,1,0:T(8,128)(2,1)}, u32[]{:S(2)}, u32[]{:S(2)}) collective-permute-start(bf16[24,512,128]{2,1,0:T(8,128)(2,1)} %get-tuple-element.12.twin_ref), channel_id=1, source_target_pairs={{0,16},{16,0},{32,48},{48,32},{64,80},{80,64},{96,112},{112,96},{1... | collective-permute-start | bytes 9437192 | tf_op jit(solution)/shard_map/ppermute | solution.py:464
  118.6 78.1 %collective-permute-start.1 = (bf16[24,512,128]{2,1,0:T(8,128)(2,1)}, bf16[24,512,128]{2,1,0:T(8,128)(2,1)}, u32[]{:S(2)}, u32[]{:S(2)}) collective-permute-start(bf16[24,512,128]{2,1,0:T(8,128)(2,1)} %get-tuple-element.13.far_ref), channel_id=1, source_target_pairs={{0,112},{16,32},{32,16},{48,64},{64,48},{80,96},{96,80},{112,0},{1... | collective-permute-start | bytes 9437192 | tf_op jit(solution)/shard_map/ppermute | solution.py:465
  128.1 0.9 copy-start.4
  128.1 18.2 %collective-permute-start.16 = (f32[4,4,4,16,128]{4,3,2,1,0:T(8,128)S(1)}, f32[4,4,4,16,128]{4,3,2,1,0:T(8,128)S(1)}, u32[]{:S(2)}, u32[]{:S(2)}) collective-permute-start(f32[4,4,4,16,128]{4,3,2,1,0:T(8,128)S(1)} %bitcast.93), channel_id=1, source_target_pairs={{0,16},{16,0},{32,48},{48,32},{64,80},{80,64},{96,112},{112,96},{1... | collective-permute-start | bytes 1572872 | tf_op jit(solution)/shard_map/ppermute | solution.py:399
  129.0 71.8 %slice-start = ((s8[6291456]{0:T(1024)(128)(4,1)}), s8[4194304]{0:T(1024)(128)(4,1)S(1)}, s32[]{:S(2)}) async-start(s8[6291456]{0:T(1024)(128)(4,1)} %bitcast.89), calls=%async_computation | async-start | bytes 8388608
  129.0 71.8 %slice-start.1 = ((s8[6291456]{0:T(1024)(128)(4,1)}), s8[2097152]{0:T(1024)(128)(4,1)S(1)}, s32[]{:S(2)}) async-start(s8[6291456]{0:T(1024)(128)(4,1)} %bitcast.89), calls=%async_computation.1 | async-start | bytes 4194304
  146.0 3.5 %collective-permute-start.36 = (f32[2,512]{1,0:T(2,128)S(1)}, f32[2,512]{1,0:T(2,128)S(1)}, u32[]{:S(2)}, u32[]{:S(2)}) collective-permute-start(f32[2,512]{1,0:T(2,128)S(1)} %get-tuple-element.17), channel_id=1, source_target_pairs={{0,16},{16,0},{32,48},{48,32},{64,80},{80,64},{96,112},{112,96},{1... | collective-permute-start | bytes 12296 | tf_op jit(solution)/shard_map/ppermute | solution.py:411
  146.5 14.3 %collective-permute-start.17 = (f32[4,4,16,128]{3,2,1,0:T(8,128)S(1)}, f32[4,4,16,128]{3,2,1,0:T(8,128)S(1)}, u32[]{:S(2)}, u32[]{:S(2)}) collective-permute-start(f32[4,4,16,128]{3,2,1,0:T(8,128)S(1)} %get-tuple-element.25), channel_id=1, source_target_pairs={{0,32},{16,48},{32,64},{48,80},{64,96},{80,112},{96,0},{112,16},{1... | collective-permute-start | bytes 393224 | tf_op jit(solution)/shard_map/ppermute | solution.py:399
  147.5 14.8 %collective-permute-start.18 = (f32[4,4,16,128]{3,2,1,0:T(8,128)S(1)}, f32[4,4,16,128]{3,2,1,0:T(8,128)S(1)}, u32[]{:S(2)}, u32[]{:S(2)}) collective-permute-start(f32[4,4,16,128]{3,2,1,0:T(8,128)S(1)} %get-tuple-element.27), channel_id=1, source_target_pairs={{0,64},{16,80},{32,96},{48,112},{64,0},{80,16},{96,32},{112,48},{1... | collective-permute-start | bytes 393224 | tf_op jit(solution)/shard_map/ppermute | solution.py:399
  149.5 14.4 %collective-permute-start.19 = (f32[4,4,16,128]{3,2,1,0:T(8,128)S(1)}, f32[4,4,16,128]{3,2,1,0:T(8,128)S(1)}, u32[]{:S(2)}, u32[]{:S(2)}) collective-permute-start(f32[4,4,16,128]{3,2,1,0:T(8,128)S(1)} %get-tuple-element.26), channel_id=1, source_target_pairs={{0,96},{16,112},{32,0},{48,16},{64,32},{80,48},{96,64},{112,80},{1... | collective-permute-start | bytes 393224 | tf_op jit(solution)/shard_map/ppermute | solution.py:399
  160.7 5.3 %collective-permute-start.37 = (f32[2,512]{1,0:T(2,128)S(1)}, f32[2,512]{1,0:T(2,128)S(1)}, u32[]{:S(2)}, u32[]{:S(2)}) collective-permute-start(f32[2,512]{1,0:T(2,128)S(1)} %add.253), channel_id=1, source_target_pairs={{0,32},{16,48},{32,64},{48,80},{64,96},{80,112},{96,0},{112,16},{1... | collective-permute-start | bytes 12296 | tf_op jit(solution)/shard_map/ppermute | solution.py:411
  162.3 4.0 %collective-permute-start.38 = (f32[2,512]{1,0:T(2,128)S(1)}, f32[2,512]{1,0:T(2,128)S(1)}, u32[]{:S(2)}, u32[]{:S(2)}) collective-permute-start(f32[2,512]{1,0:T(2,128)S(1)} %add.253), channel_id=1, source_target_pairs={{0,64},{16,80},{32,96},{48,112},{64,0},{80,16},{96,32},{112,48},{1... | collective-permute-start | bytes 12296 | tf_op jit(solution)/shard_map/ppermute | solution.py:411
  163.9 2.8 %collective-permute-start.39 = (f32[2,512]{1,0:T(2,128)S(1)}, f32[2,512]{1,0:T(2,128)S(1)}, u32[]{:S(2)}, u32[]{:S(2)}) collective-permute-start(f32[2,512]{1,0:T(2,128)S(1)} %add.253), channel_id=1, source_target_pairs={{0,96},{16,112},{32,0},{48,16},{64,32},{80,48},{96,64},{112,80},{1... | collective-permute-start | bytes 12296 | tf_op jit(solution)/shard_map/ppermute | solution.py:411
  166.0 4.4 %collective-permute-start.20 = (f32[4,16,128]{2,1,0:T(8,128)S(1)}, f32[4,16,128]{2,1,0:T(8,128)S(1)}, u32[]{:S(2)}, u32[]{:S(2)}) collective-permute-start(f32[4,16,128]{2,1,0:T(8,128)S(1)} %get-tuple-element.30), channel_id=1, source_target_pairs={{0,1},{1,2},{2,3},{3,0},{4,5},{5,6},{6,7},{7,4},{8,9},{9,10},{10,1... | collective-permute-start | bytes 98312 | tf_op jit(solution)/shard_map/ppermute | solution.py:399
  166.3 4.7 %collective-permute-start.21 = (f32[4,16,128]{2,1,0:T(8,128)S(1)}, f32[4,16,128]{2,1,0:T(8,128)S(1)}, u32[]{:S(2)}, u32[]{:S(2)}) collective-permute-start(f32[4,16,128]{2,1,0:T(8,128)S(1)} %get-tuple-element.32), channel_id=1, source_target_pairs={{0,2},{1,3},{2,0},{3,1},{4,6},{5,7},{6,4},{7,5},{8,10},{9,11},{10,... | collective-permute-start | bytes 98312 | tf_op jit(solution)/shard_map/ppermute | solution.py:399
  166.7 5.0 %collective-permute-start.22 = (f32[4,16,128]{2,1,0:T(8,128)S(1)}, f32[4,16,128]{2,1,0:T(8,128)S(1)}, u32[]{:S(2)}, u32[]{:S(2)}) collective-permute-start(f32[4,16,128]{2,1,0:T(8,128)S(1)} %get-tuple-element.31), channel_id=1, source_target_pairs={{0,3},{1,0},{2,1},{3,2},{4,7},{5,4},{6,5},{7,6},{8,11},{9,8},{10,9... | collective-permute-start | bytes 98312 | tf_op jit(solution)/shard_map/ppermute | solution.py:399
  170.4 3.7 %collective-permute-start.40 = (f32[2,512]{1,0:T(2,128)S(1)}, f32[2,512]{1,0:T(2,128)S(1)}, u32[]{:S(2)}, u32[]{:S(2)}) collective-permute-start(f32[2,512]{1,0:T(2,128)S(1)} %add_add_fusion.3), channel_id=1, source_target_pairs={{0,1},{1,2},{2,3},{3,0},{4,5},{5,6},{6,7},{7,4},{8,9},{9,10},{10,1... | collective-permute-start | bytes 12296 | tf_op jit(solution)/shard_map/ppermute | solution.py:411
  171.0 4.0 %collective-permute-start.41 = (f32[2,512]{1,0:T(2,128)S(1)}, f32[2,512]{1,0:T(2,128)S(1)}, u32[]{:S(2)}, u32[]{:S(2)}) collective-permute-start(f32[2,512]{1,0:T(2,128)S(1)} %add_add_fusion.3), channel_id=1, source_target_pairs={{0,2},{1,3},{2,0},{3,1},{4,6},{5,7},{6,4},{7,5},{8,10},{9,11},{10,... | collective-permute-start | bytes 12296 | tf_op jit(solution)/shard_map/ppermute | solution.py:411
  171.7 3.3 %collective-permute-start.42 = (f32[2,512]{1,0:T(2,128)S(1)}, f32[2,512]{1,0:T(2,128)S(1)}, u32[]{:S(2)}, u32[]{:S(2)}) collective-permute-start(f32[2,512]{1,0:T(2,128)S(1)} %add_add_fusion.3), channel_id=1, source_target_pairs={{0,3},{1,0},{2,1},{3,2},{4,7},{5,4},{6,5},{7,6},{8,11},{9,8},{10,9... | collective-permute-start | bytes 12296 | tf_op jit(solution)/shard_map/ppermute | solution.py:411
  174.1 3.7 %collective-permute-start.23 = (f32[16,128]{1,0:T(8,128)S(1)}, f32[16,128]{1,0:T(8,128)S(1)}, u32[]{:S(2)}, u32[]{:S(2)}) collective-permute-start(f32[16,128]{1,0:T(8,128)S(1)} %get-tuple-element.38), channel_id=1, source_target_pairs={{0,4},{1,5},{2,6},{3,7},{4,8},{5,9},{6,10},{7,11},{8,12},{9,13},{1... | collective-permute-start | bytes 24584 | tf_op jit(solution)/shard_map/ppermute | solution.py:399
  174.9 6.6 %collective-permute-start.24 = (f32[16,128]{1,0:T(8,128)S(1)}, f32[16,128]{1,0:T(8,128)S(1)}, u32[]{:S(2)}, u32[]{:S(2)}) collective-permute-start(f32[16,128]{1,0:T(8,128)S(1)} %get-tuple-element.40), channel_id=1, source_target_pairs={{0,8},{1,9},{2,10},{3,11},{4,12},{5,13},{6,14},{7,15},{8,0},{9,1},... | collective-permute-start | bytes 24584 | tf_op jit(solution)/shard_map/ppermute | solution.py:399
  174.9 8.6 %collective-permute-start.25 = (f32[16,128]{1,0:T(8,128)S(1)}, f32[16,128]{1,0:T(8,128)S(1)}, u32[]{:S(2)}, u32[]{:S(2)}) collective-permute-start(f32[16,128]{1,0:T(8,128)S(1)} %get-tuple-element.39), channel_id=1, source_target_pairs={{0,12},{1,13},{2,14},{3,15},{4,0},{5,1},{6,2},{7,3},{8,4},{9,5},{1... | collective-permute-start | bytes 24584 | tf_op jit(solution)/shard_map/ppermute | solution.py:399
  177.8 5.9 %collective-permute-start.12 = (f32[3,8,1,128]{3,1,2,0:T(8,128)S(1)}, f32[3,8,1,128]{3,1,2,0:T(8,128)S(1)}, u32[]{:S(2)}, u32[]{:S(2)}) collective-permute-start(f32[3,8,1,128]{3,1,2,0:T(8,128)S(1)} %bitcast.104), channel_id=1, source_target_pairs={{0,16},{16,0},{32,48},{48,32},{64,80},{80,64},{96,112},{112,96},{1... | collective-permute-start | bytes 36872 | tf_op jit(solution)/shard_map/ppermute | solution.py:475
  181.5 3.4 %collective-permute-start.13 = (f32[3,8,1,128]{3,1,2,0:T(8,128)S(1)}, f32[3,8,1,128]{3,1,2,0:T(8,128)S(1)}, u32[]{:S(2)}, u32[]{:S(2)}) collective-permute-start(f32[3,8,1,128]{3,1,2,0:T(8,128)S(1)} %bitcast.103), channel_id=1, source_target_pairs={{0,112},{16,32},{32,16},{48,64},{64,48},{80,96},{96,80},{112,0},{1... | collective-permute-start | bytes 36872 | tf_op jit(solution)/shard_map/ppermute | solution.py:475
  183.6 3.8 %collective-permute-start.26 = (f32[16,128]{1,0:T(8,128)S(1)}, f32[16,128]{1,0:T(8,128)S(1)}, u32[]{:S(2)}, u32[]{:S(2)}) collective-permute-start(f32[16,128]{1,0:T(8,128)S(1)} %fusion.8), channel_id=1, source_target_pairs={{0,4},{1,5},{2,6},{3,7},{4,8},{5,9},{6,10},{7,11},{8,12},{9,13},{1... | collective-permute-start | bytes 24584 | tf_op jit(solution)/shard_map/ppermute | solution.py:404
  183.7 4.1 %collective-permute-start.27 = (f32[16,128]{1,0:T(8,128)S(1)}, f32[16,128]{1,0:T(8,128)S(1)}, u32[]{:S(2)}, u32[]{:S(2)}) collective-permute-start(f32[16,128]{1,0:T(8,128)S(1)} %fusion.8), channel_id=1, source_target_pairs={{0,8},{1,9},{2,10},{3,11},{4,12},{5,13},{6,14},{7,15},{8,0},{9,1},... | collective-permute-start | bytes 24584 | tf_op jit(solution)/shard_map/ppermute | solution.py:404
  184.9 3.4 %collective-permute-start.28 = (f32[16,128]{1,0:T(8,128)S(1)}, f32[16,128]{1,0:T(8,128)S(1)}, u32[]{:S(2)}, u32[]{:S(2)}) collective-permute-start(f32[16,128]{1,0:T(8,128)S(1)} %fusion.8), channel_id=1, source_target_pairs={{0,12},{1,13},{2,14},{3,15},{4,0},{5,1},{6,2},{7,3},{8,4},{9,5},{1... | collective-permute-start | bytes 24584 | tf_op jit(solution)/shard_map/ppermute | solution.py:404
  188.3 4.0 %collective-permute-start.29 = (f32[4,16,128]{2,1,0:T(8,128)S(1)}, f32[4,16,128]{2,1,0:T(8,128)S(1)}, u32[]{:S(2)}, u32[]{:S(2)}) collective-permute-start(f32[4,16,128]{2,1,0:T(8,128)S(1)} %get-tuple-element.37), channel_id=1, source_target_pairs={{0,1},{1,2},{2,3},{3,0},{4,5},{5,6},{6,7},{7,4},{8,9},{9,10},{10,1... | collective-permute-start | bytes 98312 | tf_op jit(solution)/shard_map/ppermute | solution.py:404
  188.3 5.4 %collective-permute-start.30 = (f32[4,16,128]{2,1,0:T(8,128)S(1)}, f32[4,16,128]{2,1,0:T(8,128)S(1)}, u32[]{:S(2)}, u32[]{:S(2)}) collective-permute-start(f32[4,16,128]{2,1,0:T(8,128)S(1)} %get-tuple-element.37), channel_id=1, source_target_pairs={{0,2},{1,3},{2,0},{3,1},{4,6},{5,7},{6,4},{7,5},{8,10},{9,11},{10,... | collective-permute-start | bytes 98312 | tf_op jit(solution)/shard_map/ppermute | solution.py:404
  190.6 5.0 %collective-permute-start.31 = (f32[4,16,128]{2,1,0:T(8,128)S(1)}, f32[4,16,128]{2,1,0:T(8,128)S(1)}, u32[]{:S(2)}, u32[]{:S(2)}) collective-permute-start(f32[4,16,128]{2,1,0:T(8,128)S(1)} %get-tuple-element.37), channel_id=1, source_target_pairs={{0,3},{1,0},{2,1},{3,2},{4,7},{5,4},{6,5},{7,6},{8,11},{9,8},{10,9... | collective-permute-start | bytes 98312 | tf_op jit(solution)/shard_map/ppermute | solution.py:404
  192.3 11.6 %collective-permute-start.43 = (f32[2,512]{1,0:T(2,128)S(1)}, f32[2,512]{1,0:T(2,128)S(1)}, u32[]{:S(2)}, u32[]{:S(2)}) collective-permute-start(f32[2,512]{1,0:T(2,128)S(1)} %add_add_fusion.2), channel_id=1, source_target_pairs={{0,4},{1,5},{2,6},{3,7},{4,8},{5,9},{6,10},{7,11},{8,12},{9,13},{1... | collective-permute-start | bytes 12296 | tf_op jit(solution)/shard_map/ppermute | solution.py:411
  193.7 10.2 %collective-permute-start.44 = (f32[2,512]{1,0:T(2,128)S(1)}, f32[2,512]{1,0:T(2,128)S(1)}, u32[]{:S(2)}, u32[]{:S(2)}) collective-permute-start(f32[2,512]{1,0:T(2,128)S(1)} %add_add_fusion.2), channel_id=1, source_target_pairs={{0,8},{1,9},{2,10},{3,11},{4,12},{5,13},{6,14},{7,15},{8,0},{9,1},... | collective-permute-start | bytes 12296 | tf_op jit(solution)/shard_map/ppermute | solution.py:411
  195.6 10.5 %collective-permute-start.45 = (f32[2,512]{1,0:T(2,128)S(1)}, f32[2,512]{1,0:T(2,128)S(1)}, u32[]{:S(2)}, u32[]{:S(2)}) collective-permute-start(f32[2,512]{1,0:T(2,128)S(1)} %add_add_fusion.2), channel_id=1, source_target_pairs={{0,12},{1,13},{2,14},{3,15},{4,0},{5,1},{6,2},{7,3},{8,4},{9,5},{1... | collective-permute-start | bytes 12296 | tf_op jit(solution)/shard_map/ppermute | solution.py:411
  196.5 9.6 %collective-permute-start.32 = (f32[4,4,16,128]{3,2,1,0:T(8,128)S(1)}, f32[4,4,16,128]{3,2,1,0:T(8,128)S(1)}, u32[]{:S(2)}, u32[]{:S(2)}) collective-permute-start(f32[4,4,16,128]{3,2,1,0:T(8,128)S(1)} %get-tuple-element.29), channel_id=1, source_target_pairs={{0,32},{16,48},{32,64},{48,80},{64,96},{80,112},{96,0},{112,16},{1... | collective-permute-start | bytes 393224 | tf_op jit(solution)/shard_map/ppermute | solution.py:404
  196.6 9.6 %collective-permute-start.33 = (f32[4,4,16,128]{3,2,1,0:T(8,128)S(1)}, f32[4,4,16,128]{3,2,1,0:T(8,128)S(1)}, u32[]{:S(2)}, u32[]{:S(2)}) collective-permute-start(f32[4,4,16,128]{3,2,1,0:T(8,128)S(1)} %get-tuple-element.29), channel_id=1, source_target_pairs={{0,64},{16,80},{32,96},{48,112},{64,0},{80,16},{96,32},{112,48},{1... | collective-permute-start | bytes 393224 | tf_op jit(solution)/shard_map/ppermute | solution.py:404
  203.9 7.2 %collective-permute-start.34 = (f32[4,4,16,128]{3,2,1,0:T(8,128)S(1)}, f32[4,4,16,128]{3,2,1,0:T(8,128)S(1)}, u32[]{:S(2)}, u32[]{:S(2)}) collective-permute-start(f32[4,4,16,128]{3,2,1,0:T(8,128)S(1)} %get-tuple-element.29), channel_id=1, source_target_pairs={{0,96},{16,112},{32,0},{48,16},{64,32},{80,48},{96,64},{112,80},{1... | collective-permute-start | bytes 393224 | tf_op jit(solution)/shard_map/ppermute | solution.py:404
  204.0 31.4 %collective-permute-start.2 = (bf16[8,512,128]{2,1,0:T(8,128)(2,1)S(1)}, bf16[8,512,128]{2,1,0:T(8,128)(2,1)S(1)}, u32[]{:S(2)}, u32[]{:S(2)}) collective-permute-start(bf16[8,512,128]{2,1,0:T(8,128)(2,1)S(1)} %get-tuple-element.19), channel_id=1, source_target_pairs={{0,15},{1,0},{2,1},{3,2},{4,3},{5,4},{6,5},{7,6},{8,7},{9,8},{10,9... | collective-permute-start | bytes 3145736 | tf_op jit(solution)/shard_map/ppermute | solution.py:471
  206.1 29.3 %collective-permute-start.3 = (bf16[8,512,128]{2,1,0:T(8,128)(2,1)S(1)}, bf16[8,512,128]{2,1,0:T(8,128)(2,1)S(1)}, u32[]{:S(2)}, u32[]{:S(2)}) collective-permute-start(bf16[8,512,128]{2,1,0:T(8,128)(2,1)S(1)} %get-tuple-element.18), channel_id=1, source_target_pairs={{0,1},{1,2},{2,3},{3,4},{4,5},{5,6},{6,7},{7,8},{8,9},{9,10},{10,1... | collective-permute-start | bytes 3145736 | tf_op jit(solution)/shard_map/ppermute | solution.py:470
  206.1 24.6 %collective-permute-start.14 = (f32[8,1,128]{2,0,1:T(8,128)S(1)}, f32[8,1,128]{2,0,1:T(8,128)S(1)}, u32[]{:S(2)}, u32[]{:S(2)}) collective-permute-start(f32[8,1,128]{2,0,1:T(8,128)S(1)} %get-tuple-element.42), channel_id=1, source_target_pairs={{0,1},{1,2},{2,3},{3,4},{4,5},{5,6},{6,7},{7,8},{8,9},{9,10},{10,1... | collective-permute-start | bytes 12296 | tf_op jit(solution)/shard_map/ppermute | solution.py:476
  206.2 24.5 %collective-permute-start.15 = (f32[8,1,128]{2,1,0:T(1,128)S(1)}, f32[8,1,128]{2,1,0:T(1,128)S(1)}, u32[]{:S(2)}, u32[]{:S(2)}) collective-permute-start(f32[8,1,128]{2,1,0:T(1,128)S(1)} %bitcast.108), channel_id=1, source_target_pairs={{0,15},{1,0},{2,1},{3,2},{4,3},{5,4},{6,5},{7,6},{8,7},{9,8},{10,9... | collective-permute-start | bytes 12296 | tf_op jit(solution)/shard_map/ppermute | solution.py:476
  211.2 22.1 %collective-permute-start.35 = (f32[4,4,4,16,128]{4,3,2,1,0:T(8,128)S(1)}, f32[4,4,4,16,128]{4,3,2,1,0:T(8,128)S(1)}, u32[]{:S(2)}, u32[]{:S(2)}) collective-permute-start(f32[4,4,4,16,128]{4,3,2,1,0:T(8,128)S(1)} %get-tuple-element.24), channel_id=1, source_target_pairs={{0,16},{16,0},{32,48},{48,32},{64,80},{80,64},{96,112},{112,96},{1... | collective-permute-start | bytes 1572872 | tf_op jit(solution)/shard_map/ppermute | solution.py:404

commit v2 on v1

v2 whole, which is shorter than its diff:
```python
import functools
import math

import jax
import jax.numpy as jnp
from jax import lax
from jax.experimental import pallas as pl
from jax.experimental.pallas import tpu as pltpu
from jax.sharding import PartitionSpec as P

BLK = 128
NBL = 16
WIDE = 256
HALVES = NBL * BLK // WIDE
LANES = 128
CHUNK = 64
MIB = 1 << 20

f32 = jnp.float32
bf16 = jnp.bfloat16


def spread_body(edges, slots, score_ref, index_ref, grad_ref, dense_ref, twin_ref, far_a_ref,
                far_b_ref, left_scr, right_scr, grad_t, acc):
    step = pl.program_id(0)

    @pl.when(step == 0)
    def _():
        acc[...] = jnp.zeros_like(acc)

    grad_t[...] = grad_ref[...].T
    pad = ((0, LANES - edges), (0, 0))
    score = score_ref[...]
    logit = jnp.where(score > 0, score, 0.2 * score)
    expo = jnp.exp(logit - jnp.max(logit, axis=0, keepdims=True))
    alpha = expo / jnp.sum(expo, axis=0, keepdims=True)
    main = alpha.astype(bf16).astype(f32)
    rest = (alpha - main).astype(bf16).astype(f32)
    index = index_ref[...]
    low = (index % WIDE).astype(f32)
    high = jnp.pad((index // WIDE).astype(f32), pad, constant_values=-1.0).T
    main = jnp.pad(jnp.where(score > 0, main, -main), pad).T
    rest = jnp.pad(jnp.where(score > 0, rest, -rest), pad).T

    lanes = lax.broadcasted_iota(jnp.int32, (edges, LANES), 1).astype(f32).astype(bf16)
    halves = lax.broadcasted_iota(jnp.int32, (HALVES, LANES), 0).astype(f32)
    one = jnp.ones((edges, LANES), bf16)
    none = jnp.zeros((edges, LANES), bf16)
    tail = jnp.zeros((LANES - edges, WIDE), bf16)
    for i in range(BLK):
        here = jnp.broadcast_to(high[i:i + 1, :], (HALVES, LANES)) == halves
        lhs = jnp.concatenate(
            [
                jnp.where(here, jnp.broadcast_to(term[i:i + 1, :], (HALVES, LANES)), 0.0)
                for term in (main, rest)
            ],
            axis=0,
        ).astype(bf16)
        column = jnp.broadcast_to(low[:, i:i + 1], (edges, LANES)).astype(bf16)
        rhs = jnp.concatenate(
            [jnp.where(column == lanes + LANES * c, one, none) for c in range(WIDE // LANES)],
            axis=1,
        )
        rhs = jnp.concatenate([rhs, tail], axis=0)
        out = jnp.dot(lhs, rhs, preferred_element_type=f32)
        left_scr[2 * HALVES * i:2 * HALVES * (i + 1), :] = out[:, :LANES]
        right_scr[2 * HALVES * i:2 * HALVES * (i + 1), :] = out[:, LANES:]
    for s in range(NBL):
        scr = (left_scr, right_scr)[s % 2]
        main = scr[pl.ds(s // 2, BLK, stride=2 * HALVES), :]
        rest = scr[pl.ds(HALVES + s // 2, BLK, stride=2 * HALVES), :]
        dense_ref[0, :, s * BLK:(s + 1) * BLK] = main + rest
        low = jnp.abs(main).astype(bf16)
        acc[pl.ds(slots[step, s], 1)] += jnp.dot(grad_t[...], low, preferred_element_type=f32)[None]

    @pl.when(step == pl.num_programs(0) - 1)
    def _():
        per, width, _ = twin_ref.shape
        half = width // 2

        def cast(k, carry):
            twin_ref[pl.ds(k, 1)] = acc[pl.ds(k, 1)].astype(bf16)
            far_a_ref[pl.ds(k, 1)] = acc[pl.ds(per + k, 1), :half].astype(bf16)
            far_b_ref[pl.ds(k, 1)] = acc[pl.ds(per + k, 1), half:].astype(bf16)
            return carry

        lax.fori_loop(0, per, cast, 0)


def spread(slots, scores, index, grad):
    edges, rows = scores.shape
    blocks = rows // BLK
    width = grad.shape[1]
    per = 3 * blocks
    sent = [(per, width, BLK), (per, width // 2, BLK), (per, width // 2, BLK)]
    return pl.pallas_call(
        functools.partial(spread_body, edges),
        grid_spec=pltpu.PrefetchScalarGridSpec(
            num_scalar_prefetch=1,
            grid=(blocks,),
            in_specs=[pl.BlockSpec((edges, BLK), lambda b, s: (0, b))] * 2
            + [pl.BlockSpec((BLK, width), lambda b, s: (b, 0))],
            out_specs=[pl.BlockSpec((1, BLK, NBL * BLK), lambda b, s: (b, 0, 0))] + [
                pl.BlockSpec(shape, lambda b, s: (0, 0, 0), pipeline_mode=pl.Buffered(1))
                for shape in sent
            ],
            scratch_shapes=[
                pltpu.VMEM((2 * HALVES * BLK, LANES), f32),
                pltpu.VMEM((2 * HALVES * BLK, LANES), f32),
                pltpu.VMEM((width, BLK), bf16),
                pltpu.VMEM((2 * per + 1, width, BLK), f32),
            ],
        ),
        out_shape=[jax.ShapeDtypeStruct((blocks, BLK, NBL * BLK), f32)]
        + [jax.ShapeDtypeStruct(shape, bf16) for shape in sent],
        compiler_params=pltpu.CompilerParams(
            dimension_semantics=("arbitrary",), vmem_limit_bytes=60 * MIB
        ),
        cost_estimate=pl.CostEstimate(
            flops=24 * 10**9, bytes_accessed=MIB, transcendentals=0
        ),
        name="spread",
    )(jnp.where(slots >= per, slots - per, 2 * per), scores, index, grad)


def collect_body(slots, dense_ref, grad_ref, own_ref, grad_t, acc):
    step = pl.program_id(0)

    @pl.when(step == 0)
    def _():
        acc[...] = jnp.zeros_like(acc)

    grad_t[...] = grad_ref[...].T
    for s in range(NBL):
        low = jnp.abs(dense_ref[0, :, s * BLK:(s + 1) * BLK]).astype(bf16)
        acc[pl.ds(slots[step, s], 1)] += jnp.dot(grad_t[...], low, preferred_element_type=f32)[None]

    @pl.when(step == pl.num_programs(0) - 1)
    def _():
        own_ref[...] = acc[:own_ref.shape[0]]


def collect(slots, dense, grad):
    blocks = dense.shape[0]
    width = grad.shape[1]
    per = 3 * blocks
    return pl.pallas_call(
        collect_body,
        grid_spec=pltpu.PrefetchScalarGridSpec(
            num_scalar_prefetch=1,
            grid=(blocks,),
            in_specs=[
                pl.BlockSpec((1, BLK, NBL * BLK), lambda b, s: (b, 0, 0)),
                pl.BlockSpec((BLK, width), lambda b, s: (b, 0)),
            ],
            out_specs=pl.BlockSpec(
                (per, width, BLK), lambda b, s: (0, 0, 0), pipeline_mode=pl.Buffered(1)
            ),
            scratch_shapes=[
                pltpu.VMEM((width, BLK), bf16),
                pltpu.VMEM((per + 1, width, BLK), f32),
            ],
        ),
        out_shape=jax.ShapeDtypeStruct((per, width, BLK), f32),
        compiler_params=pltpu.CompilerParams(
            dimension_semantics=("arbitrary",), vmem_limit_bytes=48 * MIB
        ),
        cost_estimate=pl.CostEstimate(
            flops=11 * 10**9, bytes_accessed=MIB, transcendentals=0
        ),
        name="collect",
    )(jnp.minimum(slots, per), dense, grad)


def two_terms(row, first, rows):
    at = lax.broadcasted_iota(jnp.int32, (rows, row.shape[1]), 0)
    row = jnp.broadcast_to(row, at.shape)
    main = row.astype(bf16).astype(f32)
    return jnp.where(at == first, main, jnp.where(at == first + 1, row - main, 0.0))


def gradients_body(blocks, pieces, place, slots, dense_ref, probe_ref, grad_ref, *rest):
    count = len(pieces)
    tables = rest[:count]
    sums_ref, du_ref, keep_ref, send_ref = rest[count:count + 4]
    table, prod, mixed, grad_t, vec, total, sem = rest[count + 4:]
    step = pl.program_id(0)
    depth = table.shape[2]

    @pl.when(step == 0)
    def _():
        copies = [
            pltpu.make_async_copy(t, table.at[pl.ds(first, size)], sem.at[k])
            for k, (t, (first, size)) in enumerate(zip(tables, pieces))
        ]
        for copy in copies:
            copy.start()
        sums_ref[...] = jnp.zeros_like(sums_ref)
        vec[...] = jnp.zeros_like(vec)
        for copy in copies:
            copy.wait()

    inner = jnp.zeros((BLK, BLK), f32)
    sized = jnp.zeros((BLK, BLK), f32)
    for s in range(NBL):
        cols = slice(s * BLK, (s + 1) * BLK)
        cand = table[slots[step, s]]
        d = lax.dot_general(
            probe_ref[...], cand, (((1,), (1,)), ((), ())), preferred_element_type=f32
        )
        prod[:, cols] = d
        a = jnp.abs(dense_ref[0, :, cols])
        inner = inner + a * d
        sized = sized + a
    mean = jnp.sum(inner, axis=1, keepdims=True) / jnp.sum(sized, axis=1, keepdims=True)
    du = jnp.zeros((BLK, BLK), f32)
    mix = jnp.zeros((BLK + 16, depth), f32)
    for s in range(NBL):
        cols = slice(s * BLK, (s + 1) * BLK)
        a = dense_ref[0, :, cols]
        dz = jnp.where(a > 0, a, -0.2 * a) * (prod[:, cols] - mean)
        du = du + dz
        slot = slots[step, s]
        sums = jnp.sum(dz, axis=0, keepdims=True)
        sums_ref[pl.ds(slot, 1)] += sums[None]
        lhs = jnp.concatenate(
            [jnp.abs(a).astype(bf16), two_terms(sums, 0, 16).astype(bf16)], axis=0
        )
        mix = mix + jnp.dot(lhs, table[slot], preferred_element_type=f32)
    row = jnp.broadcast_to(jnp.sum(du, axis=1, keepdims=True), (BLK, BLK)).T[0:1, :]
    du_ref[pl.ds(step, 1)] = row[None]
    mixed[step] = mix[:BLK].astype(bf16)
    vec[...] += mix[BLK:] + jnp.dot(
        two_terms(row, 2, 16).astype(bf16), table[step], preferred_element_type=f32
    )
    grad_t[step] = grad_ref[...].T

    @pl.when(step == pl.num_programs(0) - 1)
    def _():
        lhs = jnp.concatenate([grad_t[b] for b in range(blocks)], axis=1)
        rhs = mixed[...].reshape(blocks * BLK, depth)
        total[...] = jnp.dot(lhs, rhs, preferred_element_type=f32)
        across = depth // LANES
        chunks = keep_ref.shape[0] // CHUNK
        for q in range(2 * chunks):
            r, c = q // across * CHUNK, q % across * LANES
            p = place[q]
            tile = total[r:r + CHUNK, c:c + LANES]

            @pl.when(p < chunks)
            def _():
                keep_ref[pl.ds(pl.multiple_of(p * CHUNK, CHUNK), CHUNK), :] = tile

            @pl.when(p >= chunks)
            def _():
                send_ref[pl.ds(pl.multiple_of((p - chunks) * CHUNK, CHUNK), CHUNK), :] = tile

        ends = jnp.concatenate(
            [
                (vec[r:r + 1, :] + vec[r + 1:r + 2, :])[:, c * LANES:(c + 1) * LANES]
                for r in (2, 0)
                for c in range(across)
            ],
            axis=0,
        )
        keep_ref[chunks * CHUNK:, :] = ends
        send_ref[chunks * CHUNK:, :] = ends


def gradients(place, slots, dense, probe, grad, pieces, tables):
    blocks = dense.shape[0]
    width = grad.shape[1]
    depth = probe.shape[1]
    count = 9 * blocks
    message = (width * depth // (2 * LANES) + 8, LANES)
    fixed = lambda shape: pl.BlockSpec(shape, lambda b, p, s: (0,) * len(shape))
    return pl.pallas_call(
        functools.partial(gradients_body, blocks, pieces),
        grid_spec=pltpu.PrefetchScalarGridSpec(
            num_scalar_prefetch=2,
            grid=(blocks,),
            in_specs=[
                pl.BlockSpec((1, BLK, NBL * BLK), lambda b, p, s: (b, 0, 0)),
                pl.BlockSpec((BLK, depth), lambda b, p, s: (b, 0)),
                pl.BlockSpec((BLK, width), lambda b, p, s: (b, 0)),
            ] + [pl.BlockSpec(memory_space=pl.ANY)] * len(tables),
            out_specs=[
                fixed((count, 1, BLK)), fixed((blocks, 1, BLK)), fixed(message), fixed(message)
            ],
            scratch_shapes=[
                pltpu.VMEM((count, BLK, depth), bf16),
                pltpu.VMEM((BLK, NBL * BLK), f32),
                pltpu.VMEM((blocks, BLK, depth), bf16),
                pltpu.VMEM((blocks, width, BLK), bf16),
                pltpu.VMEM((16, depth), f32),
                pltpu.VMEM((width, depth), f32),
                pltpu.SemaphoreType.DMA((len(tables),)),
            ],
        ),
        out_shape=[
            jax.ShapeDtypeStruct((count, 1, BLK), f32),
            jax.ShapeDtypeStruct((blocks, 1, BLK), f32),
            jax.ShapeDtypeStruct(message, f32),
            jax.ShapeDtypeStruct(message, f32),
        ],
        compiler_params=pltpu.CompilerParams(
            dimension_semantics=("arbitrary",), vmem_limit_bytes=60 * MIB
        ),
        cost_estimate=pl.CostEstimate(flops=22 * 10**9, bytes_accessed=MIB, transcendentals=0),
        name="gradients",
    )(place, slots, dense, probe, grad, *tables)


def columns_of(row):
    return jnp.broadcast_to(row, (LANES, row.shape[1])).T


def finish_weight_body(scale, place, near_ref, away_ref, vec_ref, src_ref, dst_ref, weight_ref,
                       out_ref, grad_src_ref, grad_dst_ref, total):
    across = total.shape[1] // LANES
    chunks = near_ref.shape[0]
    for q in range(2 * chunks):
        r, c = q // across * CHUNK, q % across * LANES
        p = place[q]
        at = lax.rem(p, chunks)
        tile = jnp.where(p < chunks, near_ref[at].astype(f32), away_ref[at].astype(f32))
        total[r:r + CHUNK, c:c + LANES] = tile
    rows = [
        jnp.concatenate([vec_ref[v * across + c][None] for c in range(across)], axis=1)
        for v in range(2)
    ]
    full = total[...]
    for ref, row in zip((src_ref, dst_ref), rows):
        full = full + jnp.concatenate([columns_of(ref[...])] * across, axis=1) * row
    out_ref[...] = full.T * scale
    terms = [two_terms(rows[0], 0, 16), two_terms(rows[1], 2, 16)]
    for v, row in enumerate(rows):
        main = row.astype(bf16).astype(f32)
        last = row - main
        last = last - last.astype(bf16).astype(f32)
        at = lax.broadcasted_iota(jnp.int32, (16, row.shape[1]), 0)
        terms.append(jnp.where(at == 4 + v, last, 0.0))
    lhs = sum(terms[1:], terms[0]).astype(bf16)
    out = jnp.dot(lhs, weight_ref[...], preferred_element_type=f32) * scale
    grad_src_ref[...] = (out[0:1, :] + out[1:2, :] + out[4:5, :]).reshape(out.shape[1])
    grad_dst_ref[...] = (out[2:3, :] + out[3:4, :] + out[5:6, :]).reshape(out.shape[1])


def finish_weight(place, near, away, vec, src, dst, weight, scale):
    depth, width = weight.shape
    whole = lambda shape: pl.BlockSpec(shape, lambda i, p: (0,) * len(shape))
    args = (near, away, vec, src, dst, weight)
    return pl.pallas_call(
        functools.partial(finish_weight_body, scale),
        grid_spec=pltpu.PrefetchScalarGridSpec(
            num_scalar_prefetch=1,
            grid=(1,),
            in_specs=[whole(a.shape) for a in args],
            out_specs=[whole((depth, width)), whole((width,)), whole((width,))],
            scratch_shapes=[pltpu.VMEM((width, depth), f32)],
        ),
        out_shape=[
            jax.ShapeDtypeStruct((depth, width), f32),
            jax.ShapeDtypeStruct((width,), f32),
            jax.ShapeDtypeStruct((width,), f32),
        ],
        compiler_params=pltpu.CompilerParams(
            dimension_semantics=("arbitrary",), vmem_limit_bytes=60 * MIB
        ),
        name="finish_weight",
    )(place, *args)


def finish_features_body(own_ref, twin_ref, far_a_ref, far_b_ref, above_a_ref, above_b_ref,
                         below_a_ref, below_b_ref, du_ref, sums_ref, src_ref, dst_ref, weight_ref,
                         out_ref, src_cols, dst_cols):
    @pl.when(pl.program_id(0) == 0)
    def _():
        src_cols[...] = columns_of(src_ref[...])
        dst_cols[...] = columns_of(dst_ref[...])

    half = far_a_ref.shape[1]
    both = lambda a, b: jnp.concatenate(
        [a[0].astype(f32), b[0, :half].astype(f32)], axis=0
    )
    total = own_ref[0] + twin_ref[0].astype(f32) + both(far_a_ref, far_b_ref)
    total = total + both(above_a_ref, above_b_ref) + both(below_a_ref, below_b_ref)
    sums = sums_ref[0]
    for ref in (above_b_ref, below_b_ref):
        carried = ref[0, half:half + 16].astype(f32)
        sums = sums + carried[0:1] + carried[1:2] + carried[2:3]
    total = total + src_cols[...] * du_ref[0] + dst_cols[...] * sums
    out_ref[...] = lax.dot_general(
        total.T.astype(bf16), weight_ref[...], (((1,), (1,)), ((), ())),
        preferred_element_type=f32,
    ).astype(bf16)


def finish_features(own, twin, halves, du, sums, src, dst, weight):
    blocks = du.shape[0]
    depth, width = weight.shape
    tile = lambda array: pl.BlockSpec((1,) + array.shape[1:], lambda b: (b, 0, 0))
    line = pl.BlockSpec((1, width), lambda b: (0, 0))
    arrays = [own, twin, *halves, du, sums]
    return pl.pallas_call(
        finish_features_body,
        grid=(blocks,),
        in_specs=[tile(array) for array in arrays] + [line] * 2
        + [pl.BlockSpec(weight.shape, lambda b: (0, 0))],
        out_specs=pl.BlockSpec((BLK, depth), lambda b: (b, 0)),
        scratch_shapes=[pltpu.VMEM((width, BLK), f32)] * 2,
        out_shape=jax.ShapeDtypeStruct((blocks * BLK, depth), bf16),
        compiler_params=pltpu.CompilerParams(
            dimension_semantics=("arbitrary",), vmem_limit_bytes=60 * MIB
        ),
        cost_estimate=pl.CostEstimate(
            flops=9 * 10**9, bytes_accessed=MIB, transcendentals=0
        ),
        name="finish_features",
    )(*arrays, src, dst, weight)


def ring(axis, low, count, offset):
    size = lax.axis_size(axis)
    turned = lambda i: ((i >> low) + offset) % count - (i >> low) % count
    return [(i, i + (turned(i) << low)) for i in range(size)]


def turned(array, stage):
    axis, low, count = stage
    return [lax.ppermute(array, axis, ring(axis, low, count, k)) for k in range(1, count)]


def scattered(array, stage, tail):
    axis, low, count = stage
    rows = (array.shape[0] - tail) // count
    chunk = lambda k: jnp.concatenate([array[k * rows:(k + 1) * rows], array[count * rows:]])
    total = chunk(0)
    for k in range(1, count):
        total = total + lax.ppermute(chunk(k), axis, ring(axis, low, count, k))
    return total


def after(array, *others):
    return lax.optimization_barrier((array, *others))[0]


def places(stages, sign):
    chunk = jnp.arange(math.prod(n for _, _, n in stages), dtype=jnp.int32)
    place, stride = jnp.zeros_like(chunk), 1
    for axis, low, count in stages[::-1]:
        here = (lax.axis_index(axis) >> low) % count
        place = place + (sign * (chunk // stride % count - here)) % count * stride
        stride = stride * count
    return place


def on_device(features, weight, attn_src, attn_dst, upstream, scores, neighbour_lists, edge_index):
    rows, depth = features.shape
    width = weight.shape[1]
    blocks = rows // BLK
    size_x = lax.axis_size("gx")
    size_y = lax.axis_size("gy")
    here_x = lax.axis_index("gx")
    here_y = lax.axis_index("gy")
    twin = [(i, i ^ 1) for i in range(size_x)]
    far = [(i, (((i + 1) ^ 1) - 1) % size_x) for i in range(size_x)]
    up = [(i, (i + 1) % size_y) for i in range(size_y)]
    down = [(i, (i - 1) % size_y) for i in range(size_y)]

    owner = neighbour_lists // blocks
    owner_x, owner_y = owner // size_y, owner % size_y
    part_x = jnp.where(owner_x == here_x, 0, jnp.where(owner_x // 2 == here_x // 2, 1, 2))
    part_y = jnp.where(owner_y == here_y, 0, jnp.where(owner_y == (here_y + 1) % size_y, 1, 2))
    slots = (part_x * 3 + part_y) * blocks + neighbour_lists % blocks

    own = features.reshape(blocks, BLK, depth)
    above = lax.ppermute(own, "gy", down)
    below = lax.ppermute(own, "gy", up)
    away = lax.ppermute(own, "gx", far)
    across = lax.ppermute(own, "gx", twin)
    dense, acc_twin, acc_far_a, acc_far_b = spread(slots, scores.T, edge_index.T, upstream)
    (above, below, away, across, dense, acc_twin, acc_far_a, acc_far_b) = (
        lax.optimization_barrier(
            (above, below, away, across, dense, acc_twin, acc_far_a, acc_far_b)
        )
    )
    from_y = [lax.ppermute(away, "gy", down), lax.ppermute(away, "gy", up)]
    from_far = [lax.ppermute(acc_far_a, "gx", far)]
    from_twin = lax.ppermute(acc_twin, "gx", twin)
    sides = lax.ppermute(jnp.concatenate([above, below]), "gx", twin)
    probe = lax.dot_general(
        upstream, weight, (((1,), (1,)), ((), ())), preferred_element_type=f32
    ).astype(bf16)
    acc_own = collect(slots, after(dense, probe), upstream)
    acc_own, from_twin, from_far[0] = lax.optimization_barrier((acc_own, from_twin, from_far[0]))

    def column(k, h, far_half):
        rows = slice(k * blocks, (k + 1) * blocks)
        cols = slice(h * width // 2, (h + 1) * width // 2)
        total = acc_own[rows, cols] + from_twin[rows, cols].astype(f32)
        return total + far_half[rows].astype(f32)

    to_above = column(1, 0, from_far[0]).astype(bf16)
    to_below = column(2, 0, from_far[0]).astype(bf16)
    dense, to_above, to_below, acc_far_b, sides, *from_y = lax.optimization_barrier(
        (dense, to_above, to_below, acc_far_b, sides, *from_y)
    )
    from_far.append(lax.ppermute(acc_far_b, "gx", far))
    from_below = [lax.ppermute(to_above, "gy", up)]
    from_above = [lax.ppermute(to_below, "gy", down)]
    tables = [own, above, below, across, sides, away, *from_y]
    firsts = (0, 1, 2, 3, 4, 6, 7, 8)
    pieces = tuple((k * blocks, t.shape[0]) for k, t in zip(firsts, tables))

    core, along_x, along_z = ("gx", 0, 2), ("gy", 2, size_y // 4), ("gx", 1, size_x // 2)
    stages = (core, along_x, along_z)
    sums, du, keep, send = gradients(
        places(stages, 1), slots, dense, probe, upstream, pieces, tables
    )
    sums, du, keep, send, from_below[0], from_above[0] = lax.optimization_barrier(
        (sums, du, keep, send, from_below[0], from_above[0])
    )
    sums = sums.reshape(3, 3, blocks, 1, BLK)
    part = keep + lax.ppermute(send, "gx", twin)
    sums = sums[0] + lax.ppermute(sums[1], "gx", twin) + lax.ppermute(sums[2], "gx", far)
    part, sums, far_b = lax.optimization_barrier((part, sums, from_far[1]))

    def terms(row):
        main = row.astype(bf16)
        rest = row - main.astype(f32)
        next_ = rest.astype(bf16)
        last = (rest - next_.astype(f32)).astype(bf16)
        pad = jnp.zeros((blocks, 13, BLK), bf16)
        return jnp.concatenate([main, next_, last, pad], axis=1)

    to_above = jnp.concatenate([column(1, 1, far_b).astype(bf16), terms(sums[1])], axis=1)
    to_below = jnp.concatenate([column(2, 1, far_b).astype(bf16), terms(sums[2])], axis=1)
    part, to_above, to_below = lax.optimization_barrier((part, to_above, to_below))
    from_below.append(lax.ppermute(to_above, "gy", up))
    from_above.append(lax.ppermute(to_below, "gy", down))
    part = scattered(part, along_x, 8)
    part = scattered(part, along_z, 8)
    part, from_below[1], from_above[1] = lax.optimization_barrier(
        (part, from_below[1], from_above[1])
    )
    part = sum(turned(part, ("gy", 0, 4)), part)
    vec = part[CHUNK:]
    part = part[:CHUNK].astype(bf16)
    part = jnp.stack([part] + turned(part, along_z))
    part, du = lax.optimization_barrier((part, du))
    part = jnp.concatenate([part] + turned(part, along_x))
    src, dst = attn_src[None], attn_dst[None]
    grad_features = finish_features(
        acc_own, from_twin, [from_far[0], far_b] + from_above + from_below, du, sums[0], src, dst,
        weight
    )
    part, grad_features = lax.optimization_barrier((part, grad_features))
    scale = 1.0 / math.sqrt(rows * size_x * size_y)
    grad_weight, grad_src, grad_dst = finish_weight(
        places(stages, -1), part, lax.ppermute(part, "gx", twin), vec, src, dst, weight, scale
    )
    return (grad_features, grad_weight, grad_src, grad_dst)


def solution(mesh):
    rows = P(("gx", "gy"), None)
    return jax.shard_map(
        on_device,
        mesh=mesh,
        in_specs=(rows, P(), P(), P(), rows, rows, rows, rows),
        out_specs=(rows, P(), P(), P()),
        check_vma=False,
    )
```

time: 244 us -> 168 us (0.69); the launches traced: 241 us -> 168 us
  Pallas kernels: 109 us -> 70.1 us
  waiting for transfers between devices: 51 us -> 27.3 us
  starting transfers between devices: 63.5 us -> 49.6 us
  other arithmetic: 4.85 us -> 11.6 us
  local copies, waits for them, and re-layouts: 8.56 us -> 5.29 us
    pallas_call x4, Pallas kernels: 107 us -> 66.7 us  [the longest x1 23.3 us: spread(): pl.pallas_call(functools.partial(spread_body, edges), grid_spec=pltpu.Pre...]
    ppermute x1, waiting for transfers between devices: 14.4 us -> 0.01 us  [on_device(): above = lax.ppermute(own, 'gy', down)]
    ppermute x42 -> x29, waiting for transfers between devices: 34.8 us -> 24.3 us  [the longest x2 10.4 us: on_device(): from_y = [lax.ppermute(away, 'gy', down), lax.ppermute(away, 'gy', up)]]
    ppermute x42 -> x29, starting transfers between devices: 51.8 us -> 43.3 us  [the longest x9 11.1 us: turned(): lax.ppermute(array, axis, ring(axis, low, count, k))]
    ppermute x1, starting transfers between devices: 3.73 us -> 0.4 us  [on_device(): lax.ppermute(sums[1], 'gx', twin)]
    convert_element_type x1 -> x3, other arithmetic: 3.14 us -> 6.08 us  [the longest x1 3.3 us: on_device(): to_below = column(2, 0, from_far[0]).astype(bf16)]
    unnamed x20 -> x30, local copies, waits for them, and re-layouts: 4.96 us -> 2.38 us
  transfers between devices with their start and end apart: 46 -> 33, of which waited for: 17 -> 14; matrix products, arithmetic and copies ran while one was open for 6% -> 8% of each run, Pallas kernels for 43% -> 40%
where the time goes in v2:
time: 168 us
  Pallas kernels  70.1 us (42%)
  starting transfers between devices  49.6 us (30%)
  waiting for transfers between devices  27.3 us (16%)
  other arithmetic  11.6 us (7%)
  local copies, waits for them, and re-layouts  5.29 us (3%)
  matrix products  2.75 us (2%)
    pallas_call x1, Pallas kernels, spread(): pl.pallas_call(functools.partial(spread_body, edges), grid_spec=pltpu.Pre...  23.3 us
    pallas_call x1, Pallas kernels, gradients(): pl.pallas_call(functools.partial(gradients_body, blocks, pieces), grid_sp...  22.2 us
    pallas_call x1, Pallas kernels, collect(): pl.pallas_call(collect_body, grid_spec=pltpu.PrefetchScalarGridSpec(num_s...  13.4 us
    ppermute x9, starting transfers between devices, turned(): lax.ppermute(array, axis, ring(axis, low, count, k))  11.1 us
    ppermute x2, waiting for transfers between devices, on_device(): from_y = [lax.ppermute(away, 'gy', down), lax.ppermute(away, 'gy', up)]  10.4 us
    pallas_call x1, Pallas kernels, finish_features(): pl.pallas_call(finish_features_body, grid=(blocks,), in_specs=[tile(array...  7.85 us
    ppermute x6, starting transfers between devices, scattered(): total = total + lax.ppermute(chunk(k), axis, ring(axis, low, count, k))  7.64 us
    ppermute x1, starting transfers between devices, on_device(): above = lax.ppermute(own, 'gy', down)  5.83 us
  transfers between devices with their start and end apart: 33, of which 14 were waited for; matrix products, arithmetic and copies ran while one was open for 8% of the time, Pallas kernels for 40%

profile of v2, /device:TPU:1, one launch (start us, length us, event | category | flops | bytes accessed | tf_op | source)
XLA Modules:
  0.0 167.7 jit_solution(7032219773328168130)
XLA Ops:
  0.6 5.8 %collective-permute-start = (bf16[8,128,512]{2,1,0:T(8,128)(2,1)}, bf16[8,128,512]{2,1,0:T(8,128)(2,1)S(1)}, u32[]{:S(2)}, u32[]{:S(2)}) collective-permute-start(bf16[8,128,512]{2,1,0:T(8,128)(2,1)} %bitcast.45), channel_id=1, source_target_pairs={{0,15},{1,0},{2,1},{3,2},{4,3},{5,4},{6,5},{7,6},{8,7},{9,8},{10,9... | collective-permute-start | bytes 3145736 | tf_op jit(solution)/shard_map/ppermute | solution.py:478
  6.5 2.5 %collective-permute-start.2 = (bf16[8,128,512]{2,1,0:T(8,128)(2,1)}, bf16[8,128,512]{2,1,0:T(8,128)(2,1)S(1)}, u32[]{:S(2)}, u32[]{:S(2)}) collective-permute-start(bf16[8,128,512]{2,1,0:T(8,128)(2,1)} %bitcast.47), channel_id=1, source_target_pairs={{0,112},{16,32},{32,16},{48,64},{64,48},{80,96},{96,80},{112,0},{1... | collective-permute-start | bytes 3145736 | tf_op jit(solution)/shard_map/ppermute | solution.py:480
  8.9 1.7 collective-permute-start.3
  10.6 0.7 broadcast_minimum_fusion
  11.3 0.6 add_select_fusion.5.slots
  11.9 23.3 %spread.1 = (f32[8,128,2048]{2,1,0:T(8,128)}, bf16[24,512,128]{2,1,0:T(8,128)(2,1)}, bf16[24,256,128]{2,1,0:T(8,128)(2,1)}, bf16[24,256,128]{2,1,0:T(8,128)(2,1)}) custom-call(s32[8,16]{1,0:T(8,128)} %add_select_fusion.5.slots, f32[80,1024]{1,0:T(8,128)} %bitcast.50, s32[80,1024]{1,0:T(8,128)} %bitcast.51, bf16[1024,512]{1,0:T(8,128)(2,1)} %grad_ref.5), custom_call_target="tpu_custom_call" | custom-call | flops 24000000000 | bytes 1048576 | tf_op jit(solution)/shard_map/spread/pallas_call | solution.py:96
  35.3 1.0 copy-done.7
  36.3 0.3 copy-done.2
  36.6 0.4 copy-done.3
  37.0 1.8 %pad_maximum_fusion = bf16[16,128,512]{2,1,0:T(8,128)(2,1)S(1)} fusion(bf16[8,128,512]{2,1,0:T(8,128)(2,1)} %copy-done.3, bf16[8,128,512]{2,1,0:T(8,128)(2,1)} %copy-done.2), kind=kLoop, calls=%fused_computation | loop fusion | flops 1048576 | bytes 4194304 | tf_op jit(solution)/shard_map/concatenate | solution.py:491
  38.8 0.5 collective-permute-start.6
  39.3 1.4 collective-permute-start.5
  40.7 0.5 fusion.17.place
  41.2 2.8 %convolution_convert_fusion.probe_ref = bf16[1024,512]{1,0:T(8,128)(2,1)} fusion(bf16[1024,512]{1,0:T(8,128)(2,1)S(1)} %copy-done, bf16[512,512]{1,0:T(8,128)(2,1)} %weight_ref.3), kind=kOutput, calls=%fused_computation.1 | convolution fusion | flops 537395200 | bytes 2621440 | tf_op jit(solution)/shard_map/dot_general | solution.py:492
  44.0 4.0 %collective-permute-start.7 = (bf16[8,128,512]{2,1,0:T(8,128)(2,1)S(1)}, bf16[8,128,512]{2,1,0:T(8,128)(2,1)S(1)}, u32[]{:S(2)}, u32[]{:S(2)}) collective-permute-start(bf16[8,128,512]{2,1,0:T(8,128)(2,1)S(1)} %copy-done.8), channel_id=1, source_target_pairs={{0,15},{1,0},{2,1},{3,2},{4,3},{5,4},{6,5},{7,6},{8,7},{9,8},{10,9... | collective-permute-start | bytes 3145736 | tf_op jit(solution)/shard_map/ppermute | solution.py:488
  48.0 13.4 %collect.1.own_ref = f32[24,512,128]{2,1,0:T(8,128)} custom-call(s32[8,16]{1,0:T(8,128)S(1)} %get-tuple-element.108.slots, f32[8,128,2048]{2,1,0:T(8,128)} %get-tuple-element.68.dense_ref, bf16[1024,512]{1,0:T(8,128)(2,1)S(1)} %copy-done), custom_call_target="tpu_custom_call" | custom-call | flops 11000000512 | bytes 1048576 | tf_op jit(solution)/shard_map/collect/pallas_call | solution.py:147
  61.4 3.3 %add_convert_fusion.2 = (bf16[8,256,128]{2,1,0:T(8,128)(2,1)}, bf16[8,256,128]{2,1,0:T(8,128)(2,1)S(1)}) fusion(f32[24,512,128]{2,1,0:T(8,128)} %collect.1.own_ref, bf16[24,256,128]{2,1,0:T(8,128)(2,1)} %collective-permute-done.5.far_a_ref, bf16[24,512,128]{2,1,0:T(8,128)(2,1)} %collective-permute-done.4.twin_ref), kind=kLoop, calls=%fused_computation.4 | loop fusion | flops 2621440 | bytes 5242880 | tf_op jit(solution)/shard_map/convert_element_type | solution.py:505
  64.7 5.2 %collective-permute-done.7.rest_6_ = bf16[8,128,512]{2,1,0:T(8,128)(2,1)S(1)} collective-permute-done((bf16[8,128,512]{2,1,0:T(8,128)(2,1)S(1)}, bf16[8,128,512]{2,1,0:T(8,128)(2,1)S(1)}, u32[]{:S(2)}, u32[]{:S(2)}) %collective-permute-start.7) | collective-permute-done | bytes 1048608 | tf_op jit(solution)/shard_map/ppermute | solution.py:488
  69.9 5.2 %collective-permute-done.8.rest_7_ = bf16[8,128,512]{2,1,0:T(8,128)(2,1)S(1)} collective-permute-done((bf16[8,128,512]{2,1,0:T(8,128)(2,1)S(1)}, bf16[8,128,512]{2,1,0:T(8,128)(2,1)S(1)}, u32[]{:S(2)}, u32[]{:S(2)}) %collective-permute-start.8) | collective-permute-done | bytes 1048608 | tf_op jit(solution)/shard_map/ppermute | solution.py:488
  75.1 0.4 collective-permute-start.10
  75.5 1.1 collective-permute-start.9
  76.6 3.6 %collective-permute-start.14 = (bf16[24,256,128]{2,1,0:T(8,128)(2,1)}, bf16[24,256,128]{2,1,0:T(8,128)(2,1)S(1)}, u32[]{:S(2)}, u32[]{:S(2)}) collective-permute-start(bf16[24,256,128]{2,1,0:T(8,128)(2,1)} %get-tuple-element.82), channel_id=1, source_target_pairs={{0,112},{16,32},{32,16},{48,64},{64,48},{80,96},{96,80},{112,0},{1... | collective-permute-start | bytes 4718600 | tf_op jit(solution)/shard_map/ppermute | solution.py:509
  80.1 22.2 %gradients.1 = (f32[72,1,128]{2,1,0:T(1,128)}, f32[8,1,128]{2,1,0:T(1,128)}, f32[1032,128]{1,0:T(8,128)}, f32[1032,128]{1,0:T(8,128)}) custom-call(s32[32]{0:T(128)} %fusion.17.place, s32[8,16]{1,0:T(8,128)} %copy-done.6, f32[8,128,2048]{2,1,0:T(8,128)} %get-tuple-element.68.dense_ref, bf16[1024,512]{1,0:T(8,128)(2,1)} %convolution_convert_fusion.probe_ref, ...), custom_call_target="tpu_custom_call" | custom-call | flops 22000001024 | bytes 1048576 | tf_op jit(solution)/shard_map/gradients/pallas_call | solution.py:277
  102.4 0.1 collective-permute-start.11
  102.5 0.8 fusion.38
  103.3 0.4 collective-permute-start.12
  103.7 0.0 collective-permute-start.13
  103.7 0.8 collective-permute-done.12
  104.5 2.3 %collective-permute-done.13 = f32[3,8,1,128]{3,1,2,0:T(8,128)S(1)} collective-permute-done((f32[3,8,1,128]{3,1,2,0:T(8,128)S(1)}, f32[3,8,1,128]{3,1,2,0:T(8,128)S(1)}, u32[]{:S(2)}, u32[]{:S(2)}) %collective-permute-start.13) | collective-permute-done | bytes 12320 | tf_op jit(solution)/shard_map/ppermute | solution.py:526
  106.8 1.1 add.180
  108.0 2.8 %add_convert_fusion = (bf16[8,256,128]{2,1,0:T(8,128)(2,1)S(1)}, bf16[8,256,128]{2,1,0:T(8,128)(2,1)S(1)}) fusion(f32[24,512,128]{2,1,0:T(8,128)} %collect.1.own_ref, bf16[24,256,128]{2,1,0:T(8,128)(2,1)S(1)} %collective-permute-done.14.far_b_ref, bf16[24,512,128]{2,1,0:T(8,128)(2,1)} %collective-permute-done.4.twin_ref), kind=kLoop, calls=%fused_computation.2 | loop fusion | flops 2621440 | bytes 5242880 | tf_op jit(solution)/shard_map/convert_element_type | solution.py:538
  110.9 0.4 concatenate.38
  111.3 0.4 concatenate.37
  111.8 0.1 collective-permute-start.15
  111.8 0.1 collective-permute-start.16
  111.9 2.6 %collective-permute-start.17 = (f32[264,128]{1,0:T(8,128)S(1)}, f32[264,128]{1,0:T(8,128)S(1)}, u32[]{:S(2)}, u32[]{:S(2)}) collective-permute-start(f32[264,128]{1,0:T(8,128)S(1)} %concatenate.42), channel_id=1, source_target_pairs={{0,12},{1,13},{2,14},{3,15},{4,0},{5,1},{6,2},{7,3},{8,4},{9,5},{1... | collective-permute-start | bytes 405512 | tf_op jit(solution)/shard_map/ppermute | solution.py:440
  114.5 4.8 %collective-permute-start.22 = (bf16[8,272,128]{2,1,0:T(8,128)(2,1)S(1)}, bf16[8,272,128]{2,1,0:T(8,128)(2,1)S(1)}, u32[]{:S(2)}, u32[]{:S(2)}) collective-permute-start(bf16[8,272,128]{2,1,0:T(8,128)(2,1)S(1)} %concatenate.38), channel_id=1, source_target_pairs={{0,15},{1,0},{2,1},{3,2},{4,3},{5,4},{6,5},{7,6},{8,7},{9,8},{10,9... | collective-permute-start | bytes 1671176 | tf_op jit(solution)/shard_map/ppermute | solution.py:541
  119.3 1.7 %collective-permute-done.15 = f32[264,128]{1,0:T(8,128)S(1)} collective-permute-done((f32[264,128]{1,0:T(8,128)S(1)}, f32[264,128]{1,0:T(8,128)S(1)}, u32[]{:S(2)}, u32[]{:S(2)}) %collective-permute-start.15) | collective-permute-done | bytes 135200 | tf_op jit(solution)/shard_map/ppermute | solution.py:440
  121.1 0.2 collective-permute-start.18
  121.3 4.7 %collective-permute-start.19 = (f32[72,128]{1,0:T(8,128)S(1)}, f32[72,128]{1,0:T(8,128)S(1)}, u32[]{:S(2)}, u32[]{:S(2)}) collective-permute-start(f32[72,128]{1,0:T(8,128)S(1)} %get-tuple-element.127), channel_id=1, source_target_pairs={{0,64},{16,80},{32,96},{48,112},{64,0},{80,16},{96,32},{112,48},{1... | collective-permute-start | bytes 110600 | tf_op jit(solution)/shard_map/ppermute | solution.py:440
  126.0 0.5 collective-permute-done.18
  126.5 2.0 %collective-permute-done.19 = f32[72,128]{1,0:T(8,128)S(1)} collective-permute-done((f32[72,128]{1,0:T(8,128)S(1)}, f32[72,128]{1,0:T(8,128)S(1)}, u32[]{:S(2)}, u32[]{:S(2)}) %collective-permute-start.19) | collective-permute-done | bytes 36896 | tf_op jit(solution)/shard_map/ppermute | solution.py:440
  128.4 0.7 collective-permute-done.20
  129.1 3.7 %collective-permute-done.21.below_b_ref = bf16[8,272,128]{2,1,0:T(8,128)(2,1)S(1)} collective-permute-done((bf16[8,272,128]{2,1,0:T(8,128)(2,1)S(1)}, bf16[8,272,128]{2,1,0:T(8,128)(2,1)S(1)}, u32[]{:S(2)}, u32[]{:S(2)}) %collective-permute-start.21) | collective-permute-done | bytes 557088 | tf_op jit(solution)/shard_map/ppermute | solution.py:540
  132.8 0.1 collective-permute-start.23
  132.9 2.7 %collective-permute-start.24 = (f32[72,128]{1,0:T(8,128)S(1)}, f32[72,128]{1,0:T(8,128)S(1)}, u32[]{:S(2)}, u32[]{:S(2)}) collective-permute-start(f32[72,128]{1,0:T(8,128)S(1)} %fusion.5), channel_id=1, source_target_pairs={{0,2},{1,3},{2,0},{3,1},{4,6},{5,7},{6,4},{7,5},{8,10},{9,11},{10,... | collective-permute-start | bytes 110600 | tf_op jit(solution)/shard_map/ppermute | solution.py:431
  135.6 0.6 slice.124
  136.2 0.7 collective-permute-done.23
  136.9 0.4 collective-permute-done.24
  137.3 1.1 collective-permute-done.25
  138.4 3.8 %collective-permute-start.27 = (bf16[64,128]{1,0:T(8,128)(2,1)S(1)}, bf16[64,128]{1,0:T(8,128)(2,1)S(1)}, u32[]{:S(2)}, u32[]{:S(2)}) collective-permute-start(bf16[64,128]{1,0:T(8,128)(2,1)S(1)} %slice.157), channel_id=1, source_target_pairs={{0,64},{16,80},{32,96},{48,112},{64,0},{80,16},{96,32},{112,48},{1... | collective-permute-start | bytes 49160 | tf_op jit(solution)/shard_map/ppermute | solution.py:431
  142.2 0.7 collective-permute-start.28
  142.9 0.7 collective-permute-start.26
  143.7 1.1 collective-permute-done.28
  144.8 1.9 %collective-permute-done.26 = bf16[64,128]{1,0:T(8,128)(2,1)S(1)} collective-permute-done((bf16[64,128]{1,0:T(8,128)(2,1)S(1)}, bf16[64,128]{1,0:T(8,128)(2,1)S(1)}, u32[]{:S(2)}, u32[]{:S(2)}) %collective-permute-start.26) | collective-permute-done | bytes 16416 | tf_op jit(solution)/shard_map/ppermute | solution.py:431
  146.7 0.1 collective-permute-start.29
  146.8 3.0 %collective-permute-start.30 = (bf16[4,64,128]{2,1,0:T(8,128)(2,1)S(1)}, bf16[4,64,128]{2,1,0:T(8,128)(2,1)S(1)}, u32[]{:S(2)}, u32[]{:S(2)}) collective-permute-start(bf16[4,64,128]{2,1,0:T(8,128)(2,1)S(1)} %pad_maximum_fusion.5), channel_id=1, source_target_pairs={{0,8},{1,9},{2,10},{3,11},{4,12},{5,13},{6,14},{7,15},{8,0},{9,1},... | collective-permute-start | bytes 196616 | tf_op jit(solution)/shard_map/ppermute | solution.py:431
  149.9 7.9 %finish_features.1 = bf16[1024,512]{1,0:T(8,128)(2,1)} custom-call(f32[24,512,128]{2,1,0:T(8,128)} %collect.1.own_ref, bf16[24,512,128]{2,1,0:T(8,128)(2,1)} %collective-permute-done.4.twin_ref, bf16[24,256,128]{2,1,0:T(8,128)(2,1)} %collective-permute-done.5.far_a_ref, bf16[24,256,128]{2,1,0:T(8,128)(2,1)} %copy-done.4, bf16[8,256,128]{2,1,0:T(8,128)(2,1)} %copy-done.13, ...), custom_call_target="tpu_custom_call" | custom-call | flops 8999999488 | bytes 1048576 | tf_op jit(solution)/shard_map/finish_features/pallas_call | solution.py:405
  157.8 4.6 %collective-permute-start.32 = (bf16[16,64,128]{2,1,0:T(8,128)(2,1)S(1)}, bf16[16,64,128]{2,1,0:T(8,128)(2,1)S(1)}, u32[]{:S(2)}, u32[]{:S(2)}) collective-permute-start(bf16[16,64,128]{2,1,0:T(8,128)(2,1)S(1)} %pad_maximum_fusion.1.near_ref), channel_id=1, source_target_pairs={{0,16},{16,0},{32,48},{48,32},{64,80},{80,64},{96,112},{112,96},{1... | collective-permute-start | bytes 786440 | tf_op jit(solution)/shard_map/ppermute | solution.py:561
  162.4 0.6 fusion.16.place
  163.0 0.6 slice.131.vec_ref
  163.5 0.0 collective-permute-done.32.away_ref
  163.6 0.7 copy-done.5
  164.3 3.4 %finish_weight.1 = (f32[512,512]{1,0:T(8,128)}, f32[512]{0:T(512)}, f32[512]{0:T(512)}) custom-call(s32[32]{0:T(128)} %fusion.16.place, bf16[16,64,128]{2,1,0:T(8,128)(2,1)} %copy-done.1, bf16[16,64,128]{2,1,0:T(8,128)(2,1)} %copy-done.5, f32[8,128]{1,0:T(8,128)} %slice.131.vec_ref, f32[1,512]{1,0:T(1,128)} %bitcast.42, f32[1,512]{1,0:T(1,128)} %bitcast.44, ...), custom_call_target="tpu_custom_call" | custom-call | tf_op jit(solution)/shard_map/finish_weight/pallas_call | solution.py:353
  (75 shorter events, 0.4 us)
Async XLA Ops:
  0.6 34.6 %collective-permute-start = (bf16[8,128,512]{2,1,0:T(8,128)(2,1)}, bf16[8,128,512]{2,1,0:T(8,128)(2,1)S(1)}, u32[]{:S(2)}, u32[]{:S(2)}) collective-permute-start(bf16[8,128,512]{2,1,0:T(8,128)(2,1)} %bitcast.45), channel_id=1, source_target_pairs={{0,15},{1,0},{2,1},{3,2},{4,3},{5,4},{6,5},{7,6},{8,7},{9,8},{10,9... | collective-permute-start | bytes 3145736 | tf_op jit(solution)/shard_map/ppermute | solution.py:478
  6.5 28.8 %collective-permute-start.1 = (bf16[8,128,512]{2,1,0:T(8,128)(2,1)}, bf16[8,128,512]{2,1,0:T(8,128)(2,1)S(1)}, u32[]{:S(2)}, u32[]{:S(2)}) collective-permute-start(bf16[8,128,512]{2,1,0:T(8,128)(2,1)} %bitcast.46), channel_id=1, source_target_pairs={{0,1},{1,2},{2,3},{3,4},{4,5},{5,6},{6,7},{7,8},{8,9},{9,10},{10,1... | collective-permute-start | bytes 3145736 | tf_op jit(solution)/shard_map/ppermute | solution.py:479
  6.5 28.8 %collective-permute-start.2 = (bf16[8,128,512]{2,1,0:T(8,128)(2,1)}, bf16[8,128,512]{2,1,0:T(8,128)(2,1)S(1)}, u32[]{:S(2)}, u32[]{:S(2)}) collective-permute-start(bf16[8,128,512]{2,1,0:T(8,128)(2,1)} %bitcast.47), channel_id=1, source_target_pairs={{0,112},{16,32},{32,16},{48,64},{64,48},{80,96},{96,80},{112,0},{1... | collective-permute-start | bytes 3145736 | tf_op jit(solution)/shard_map/ppermute | solution.py:480
  8.9 26.4 %collective-permute-start.3 = (bf16[8,128,512]{2,1,0:T(8,128)(2,1)}, bf16[8,128,512]{2,1,0:T(8,128)(2,1)}, u32[]{:S(2)}, u32[]{:S(2)}) collective-permute-start(bf16[8,128,512]{2,1,0:T(8,128)(2,1)} %bitcast.48), channel_id=1, source_target_pairs={{0,16},{16,0},{32,48},{48,32},{64,80},{80,64},{96,112},{112,96},{1... | collective-permute-start | bytes 3145736 | tf_op jit(solution)/shard_map/ppermute | solution.py:481
  11.3 23.9 %copy-start.6 = (s32[8,16]{1,0:T(8,128)}, s32[8,16]{1,0:T(8,128)S(1)}, u32[]{:S(2)}) copy-start(s32[8,16]{1,0:T(8,128)S(1)} %get-tuple-element.109.slots) | copy-start | bytes 1540
  35.3 1.3 copy-start.2
  35.3 1.7 copy-start.3
  35.3 1.0 copy-start.7
  36.9 4.3 %copy-start = (bf16[1024,512]{1,0:T(8,128)(2,1)S(1)}, bf16[1024,512]{1,0:T(8,128)(2,1)}, u32[]{:S(2)}) copy-start(bf16[1024,512]{1,0:T(8,128)(2,1)} %grad_ref.5) | copy-start | bytes 3145732
  36.9 24.4 %collective-permute-start.4 = (bf16[24,512,128]{2,1,0:T(8,128)(2,1)}, bf16[24,512,128]{2,1,0:T(8,128)(2,1)}, u32[]{:S(2)}, u32[]{:S(2)}) collective-permute-start(bf16[24,512,128]{2,1,0:T(8,128)(2,1)} %get-tuple-element.59), channel_id=1, source_target_pairs={{0,16},{16,0},{32,48},{48,32},{64,80},{80,64},{96,112},{112,96},{1... | collective-permute-start | bytes 9437192 | tf_op jit(solution)/shard_map/ppermute | solution.py:490
  38.8 36.3 %collective-permute-start.6 = (bf16[16,128,512]{2,1,0:T(8,128)(2,1)S(1)}, bf16[16,128,512]{2,1,0:T(8,128)(2,1)}, u32[]{:S(2)}, u32[]{:S(2)}) collective-permute-start(bf16[16,128,512]{2,1,0:T(8,128)(2,1)S(1)} %pad_maximum_fusion), channel_id=1, source_target_pairs={{0,16},{16,0},{32,48},{48,32},{64,80},{80,64},{96,112},{112,96},{1... | collective-permute-start | bytes 6291464 | tf_op jit(solution)/shard_map/ppermute | solution.py:491
  39.3 22.1 %collective-permute-start.5 = (bf16[24,256,128]{2,1,0:T(8,128)(2,1)}, bf16[24,256,128]{2,1,0:T(8,128)(2,1)}, u32[]{:S(2)}, u32[]{:S(2)}) collective-permute-start(bf16[24,256,128]{2,1,0:T(8,128)(2,1)} %get-tuple-element.60), channel_id=1, source_target_pairs={{0,112},{16,32},{32,16},{48,64},{64,48},{80,96},{96,80},{112,0},{1... | collective-permute-start | bytes 4718600 | tf_op jit(solution)/shard_map/ppermute | solution.py:489
  40.7 3.3 %copy-start.8 = (bf16[8,128,512]{2,1,0:T(8,128)(2,1)S(1)}, bf16[8,128,512]{2,1,0:T(8,128)(2,1)}, u32[]{:S(2)}) copy-start(bf16[8,128,512]{2,1,0:T(8,128)(2,1)} %copy-done.7) | copy-start | bytes 3145732
  44.0 25.9 %collective-permute-start.7 = (bf16[8,128,512]{2,1,0:T(8,128)(2,1)S(1)}, bf16[8,128,512]{2,1,0:T(8,128)(2,1)S(1)}, u32[]{:S(2)}, u32[]{:S(2)}) collective-permute-start(bf16[8,128,512]{2,1,0:T(8,128)(2,1)S(1)} %copy-done.8), channel_id=1, source_target_pairs={{0,15},{1,0},{2,1},{3,2},{4,3},{5,4},{6,5},{7,6},{8,7},{9,8},{10,9... | collective-permute-start | bytes 3145736 | tf_op jit(solution)/shard_map/ppermute | solution.py:488
  48.0 27.1 %collective-permute-start.8 = (bf16[8,128,512]{2,1,0:T(8,128)(2,1)S(1)}, bf16[8,128,512]{2,1,0:T(8,128)(2,1)S(1)}, u32[]{:S(2)}, u32[]{:S(2)}) collective-permute-start(bf16[8,128,512]{2,1,0:T(8,128)(2,1)S(1)} %copy-done.8), channel_id=1, source_target_pairs={{0,1},{1,2},{2,3},{3,4},{4,5},{5,6},{6,7},{7,8},{8,9},{9,10},{10,1... | collective-permute-start | bytes 3145736 | tf_op jit(solution)/shard_map/ppermute | solution.py:488
  69.9 6.7 %copy-start.9 = (bf16[8,128,512]{2,1,0:T(8,128)(2,1)}, bf16[8,128,512]{2,1,0:T(8,128)(2,1)S(1)}, u32[]{:S(2)}) copy-start(bf16[8,128,512]{2,1,0:T(8,128)(2,1)S(1)} %collective-permute-done.7.rest_6_) | copy-start | bytes 3145732
  75.1 1.5 copy-start.10
  75.1 27.2 %collective-permute-start.10 = (bf16[8,256,128]{2,1,0:T(8,128)(2,1)}, bf16[8,256,128]{2,1,0:T(8,128)(2,1)S(1)}, u32[]{:S(2)}, u32[]{:S(2)}) collective-permute-start(bf16[8,256,128]{2,1,0:T(8,128)(2,1)} %get-tuple-element.78), channel_id=1, source_target_pairs={{0,15},{1,0},{2,1},{3,2},{4,3},{5,4},{6,5},{7,6},{8,7},{9,8},{10,9... | collective-permute-start | bytes 1572872 | tf_op jit(solution)/shard_map/ppermute | solution.py:511
  75.5 26.9 %collective-permute-start.9 = (bf16[8,256,128]{2,1,0:T(8,128)(2,1)S(1)}, bf16[8,256,128]{2,1,0:T(8,128)(2,1)S(1)}, u32[]{:S(2)}, u32[]{:S(2)}) collective-permute-start(bf16[8,256,128]{2,1,0:T(8,128)(2,1)S(1)} %get-tuple-element.77), channel_id=1, source_target_pairs={{0,1},{1,2},{2,3},{3,4},{4,5},{5,6},{6,7},{7,8},{8,9},{9,10},{10,1... | collective-permute-start | bytes 1572872 | tf_op jit(solution)/shard_map/ppermute | solution.py:510
  76.6 31.4 %collective-permute-start.14 = (bf16[24,256,128]{2,1,0:T(8,128)(2,1)}, bf16[24,256,128]{2,1,0:T(8,128)(2,1)S(1)}, u32[]{:S(2)}, u32[]{:S(2)}) collective-permute-start(bf16[24,256,128]{2,1,0:T(8,128)(2,1)} %get-tuple-element.82), channel_id=1, source_target_pairs={{0,112},{16,32},{32,16},{48,64},{64,48},{80,96},{96,80},{112,0},{1... | collective-permute-start | bytes 4718600 | tf_op jit(solution)/shard_map/ppermute | solution.py:509
  102.3 4.5 %copy-start.13 = (bf16[8,256,128]{2,1,0:T(8,128)(2,1)}, bf16[8,256,128]{2,1,0:T(8,128)(2,1)S(1)}, u32[]{:S(2)}) copy-start(bf16[8,256,128]{2,1,0:T(8,128)(2,1)S(1)} %collective-permute-done.10.above_a_ref) | copy-start | bytes 1572868
  102.4 4.5 %copy-start.14 = (bf16[8,256,128]{2,1,0:T(8,128)(2,1)}, bf16[8,256,128]{2,1,0:T(8,128)(2,1)S(1)}, u32[]{:S(2)}) copy-start(bf16[8,256,128]{2,1,0:T(8,128)(2,1)S(1)} %collective-permute-done.9.below_a_ref) | copy-start | bytes 1572868
  102.4 4.5 %collective-permute-start.11 = (f32[1032,128]{1,0:T(8,128)}, f32[1032,128]{1,0:T(8,128)S(1)}, u32[]{:S(2)}, u32[]{:S(2)}) collective-permute-start(f32[1032,128]{1,0:T(8,128)} %get-tuple-element.80), channel_id=1, source_target_pairs={{0,16},{16,0},{32,48},{48,32},{64,80},{80,64},{96,112},{112,96},{1... | collective-permute-start | bytes 1585160 | tf_op jit(solution)/shard_map/ppermute | solution.py:525
  103.3 1.2 collective-permute-start.12
  103.7 3.1 %collective-permute-start.13 = (f32[3,8,1,128]{3,1,2,0:T(8,128)S(1)}, f32[3,8,1,128]{3,1,2,0:T(8,128)S(1)}, u32[]{:S(2)}, u32[]{:S(2)}) collective-permute-start(f32[3,8,1,128]{3,1,2,0:T(8,128)S(1)} %bitcast.38), channel_id=1, source_target_pairs={{0,112},{16,32},{32,16},{48,64},{64,48},{80,96},{96,80},{112,0},{1... | collective-permute-start | bytes 36872 | tf_op jit(solution)/shard_map/ppermute | solution.py:526
  108.0 2.8 %copy-start.4 = (bf16[24,256,128]{2,1,0:T(8,128)(2,1)}, bf16[24,256,128]{2,1,0:T(8,128)(2,1)S(1)}, u32[]{:S(2)}) copy-start(bf16[24,256,128]{2,1,0:T(8,128)(2,1)S(1)} %collective-permute-done.14.far_b_ref) | copy-start | bytes 4718596
  111.8 9.2 %collective-permute-start.15 = (f32[264,128]{1,0:T(8,128)S(1)}, f32[264,128]{1,0:T(8,128)S(1)}, u32[]{:S(2)}, u32[]{:S(2)}) collective-permute-start(f32[264,128]{1,0:T(8,128)S(1)} %get-tuple-element.128), channel_id=1, source_target_pairs={{0,4},{1,5},{2,6},{3,7},{4,8},{5,9},{6,10},{7,11},{8,12},{9,13},{1... | collective-permute-start | bytes 405512 | tf_op jit(solution)/shard_map/ppermute | solution.py:440
  111.8 9.1 %collective-permute-start.16 = (f32[264,128]{1,0:T(8,128)S(1)}, f32[264,128]{1,0:T(8,128)S(1)}, u32[]{:S(2)}, u32[]{:S(2)}) collective-permute-start(f32[264,128]{1,0:T(8,128)S(1)} %get-tuple-element.129), channel_id=1, source_target_pairs={{0,8},{1,9},{2,10},{3,11},{4,12},{5,13},{6,14},{7,15},{8,0},{9,1},... | collective-permute-start | bytes 405512 | tf_op jit(solution)/shard_map/ppermute | solution.py:440
  111.9 9.1 %collective-permute-start.17 = (f32[264,128]{1,0:T(8,128)S(1)}, f32[264,128]{1,0:T(8,128)S(1)}, u32[]{:S(2)}, u32[]{:S(2)}) collective-permute-start(f32[264,128]{1,0:T(8,128)S(1)} %concatenate.42), channel_id=1, source_target_pairs={{0,12},{1,13},{2,14},{3,15},{4,0},{5,1},{6,2},{7,3},{8,4},{9,5},{1... | collective-permute-start | bytes 405512 | tf_op jit(solution)/shard_map/ppermute | solution.py:440
  114.5 18.3 %collective-permute-start.21 = (bf16[8,272,128]{2,1,0:T(8,128)(2,1)S(1)}, bf16[8,272,128]{2,1,0:T(8,128)(2,1)S(1)}, u32[]{:S(2)}, u32[]{:S(2)}) collective-permute-start(bf16[8,272,128]{2,1,0:T(8,128)(2,1)S(1)} %concatenate.37), channel_id=1, source_target_pairs={{0,1},{1,2},{2,3},{3,4},{4,5},{5,6},{6,7},{7,8},{8,9},{9,10},{10,1... | collective-permute-start | bytes 1671176 | tf_op jit(solution)/shard_map/ppermute | solution.py:540
  114.5 18.3 %collective-permute-start.22 = (bf16[8,272,128]{2,1,0:T(8,128)(2,1)S(1)}, bf16[8,272,128]{2,1,0:T(8,128)(2,1)S(1)}, u32[]{:S(2)}, u32[]{:S(2)}) collective-permute-start(bf16[8,272,128]{2,1,0:T(8,128)(2,1)S(1)} %concatenate.38), channel_id=1, source_target_pairs={{0,15},{1,0},{2,1},{3,2},{4,3},{5,4},{6,5},{7,6},{8,7},{9,8},{10,9... | collective-permute-start | bytes 1671176 | tf_op jit(solution)/shard_map/ppermute | solution.py:541
  121.1 5.4 %collective-permute-start.18 = (f32[72,128]{1,0:T(8,128)S(1)}, f32[72,128]{1,0:T(8,128)S(1)}, u32[]{:S(2)}, u32[]{:S(2)}) collective-permute-start(f32[72,128]{1,0:T(8,128)S(1)} %get-tuple-element.126), channel_id=1, source_target_pairs={{0,32},{16,48},{32,64},{48,80},{64,96},{80,112},{96,0},{112,16},{1... | collective-permute-start | bytes 110600 | tf_op jit(solution)/shard_map/ppermute | solution.py:440
  121.3 7.2 %collective-permute-start.19 = (f32[72,128]{1,0:T(8,128)S(1)}, f32[72,128]{1,0:T(8,128)S(1)}, u32[]{:S(2)}, u32[]{:S(2)}) collective-permute-start(f32[72,128]{1,0:T(8,128)S(1)} %get-tuple-element.127), channel_id=1, source_target_pairs={{0,64},{16,80},{32,96},{48,112},{64,0},{80,16},{96,32},{112,48},{1... | collective-permute-start | bytes 110600 | tf_op jit(solution)/shard_map/ppermute | solution.py:440
  126.0 3.1 %collective-permute-start.20 = (f32[72,128]{1,0:T(8,128)S(1)}, f32[72,128]{1,0:T(8,128)S(1)}, u32[]{:S(2)}, u32[]{:S(2)}) collective-permute-start(f32[72,128]{1,0:T(8,128)S(1)} %concatenate.48), channel_id=1, source_target_pairs={{0,96},{16,112},{32,0},{48,16},{64,32},{80,48},{96,64},{112,80},{1... | collective-permute-start | bytes 110600 | tf_op jit(solution)/shard_map/ppermute | solution.py:440
  132.8 17.0 %copy-start.11 = (bf16[8,272,128]{2,1,0:T(8,128)(2,1)}, bf16[8,272,128]{2,1,0:T(8,128)(2,1)S(1)}, u32[]{:S(2)}) copy-start(bf16[8,272,128]{2,1,0:T(8,128)(2,1)S(1)} %collective-permute-done.21.below_b_ref) | copy-start | bytes 1671172
  132.8 17.0 %copy-start.12 = (bf16[8,272,128]{2,1,0:T(8,128)(2,1)}, bf16[8,272,128]{2,1,0:T(8,128)(2,1)S(1)}, u32[]{:S(2)}) copy-start(bf16[8,272,128]{2,1,0:T(8,128)(2,1)S(1)} %collective-permute-done.22.above_b_ref) | copy-start | bytes 1671172
  132.8 4.1 %collective-permute-start.23 = (f32[72,128]{1,0:T(8,128)S(1)}, f32[72,128]{1,0:T(8,128)S(1)}, u32[]{:S(2)}, u32[]{:S(2)}) collective-permute-start(f32[72,128]{1,0:T(8,128)S(1)} %fusion.5), channel_id=1, source_target_pairs={{0,1},{1,2},{2,3},{3,0},{4,5},{5,6},{6,7},{7,4},{8,9},{9,10},{10,1... | collective-permute-start | bytes 110600 | tf_op jit(solution)/shard_map/ppermute | solution.py:431
  132.9 4.4 %collective-permute-start.24 = (f32[72,128]{1,0:T(8,128)S(1)}, f32[72,128]{1,0:T(8,128)S(1)}, u32[]{:S(2)}, u32[]{:S(2)}) collective-permute-start(f32[72,128]{1,0:T(8,128)S(1)} %fusion.5), channel_id=1, source_target_pairs={{0,2},{1,3},{2,0},{3,1},{4,6},{5,7},{6,4},{7,5},{8,10},{9,11},{10,... | collective-permute-start | bytes 110600 | tf_op jit(solution)/shard_map/ppermute | solution.py:431
  135.6 2.8 %collective-permute-start.25 = (f32[72,128]{1,0:T(8,128)S(1)}, f32[72,128]{1,0:T(8,128)S(1)}, u32[]{:S(2)}, u32[]{:S(2)}) collective-permute-start(f32[72,128]{1,0:T(8,128)S(1)} %fusion.5), channel_id=1, source_target_pairs={{0,3},{1,0},{2,1},{3,2},{4,7},{5,4},{6,5},{7,6},{8,11},{9,8},{10,9... | collective-permute-start | bytes 110600 | tf_op jit(solution)/shard_map/ppermute | solution.py:431
  138.4 5.2 %collective-permute-start.27 = (bf16[64,128]{1,0:T(8,128)(2,1)S(1)}, bf16[64,128]{1,0:T(8,128)(2,1)S(1)}, u32[]{:S(2)}, u32[]{:S(2)}) collective-permute-start(bf16[64,128]{1,0:T(8,128)(2,1)S(1)} %slice.157), channel_id=1, source_target_pairs={{0,64},{16,80},{32,96},{48,112},{64,0},{80,16},{96,32},{112,48},{1... | collective-permute-start | bytes 49160 | tf_op jit(solution)/shard_map/ppermute | solution.py:431
  142.2 2.6 %collective-permute-start.28 = (bf16[64,128]{1,0:T(8,128)(2,1)S(1)}, bf16[64,128]{1,0:T(8,128)(2,1)S(1)}, u32[]{:S(2)}, u32[]{:S(2)}) collective-permute-start(bf16[64,128]{1,0:T(8,128)(2,1)S(1)} %slice.157), channel_id=1, source_target_pairs={{0,96},{16,112},{32,0},{48,16},{64,32},{80,48},{96,64},{112,80},{1... | collective-permute-start | bytes 49160 | tf_op jit(solution)/shard_map/ppermute | solution.py:431
  142.9 3.8 %collective-permute-start.26 = (bf16[64,128]{1,0:T(8,128)(2,1)S(1)}, bf16[64,128]{1,0:T(8,128)(2,1)S(1)}, u32[]{:S(2)}, u32[]{:S(2)}) collective-permute-start(bf16[64,128]{1,0:T(8,128)(2,1)S(1)} %slice.157), channel_id=1, source_target_pairs={{0,32},{16,48},{32,64},{48,80},{64,96},{80,112},{96,0},{112,16},{1... | collective-permute-start | bytes 49160 | tf_op jit(solution)/shard_map/ppermute | solution.py:431
  146.7 11.0 %collective-permute-start.29 = (bf16[4,64,128]{2,1,0:T(8,128)(2,1)S(1)}, bf16[4,64,128]{2,1,0:T(8,128)(2,1)S(1)}, u32[]{:S(2)}, u32[]{:S(2)}) collective-permute-start(bf16[4,64,128]{2,1,0:T(8,128)(2,1)S(1)} %pad_maximum_fusion.5), channel_id=1, source_target_pairs={{0,4},{1,5},{2,6},{3,7},{4,8},{5,9},{6,10},{7,11},{8,12},{9,13},{1... | collective-permute-start | bytes 196616 | tf_op jit(solution)/shard_map/ppermute | solution.py:431
  146.8 10.9 %collective-permute-start.30 = (bf16[4,64,128]{2,1,0:T(8,128)(2,1)S(1)}, bf16[4,64,128]{2,1,0:T(8,128)(2,1)S(1)}, u32[]{:S(2)}, u32[]{:S(2)}) collective-permute-start(bf16[4,64,128]{2,1,0:T(8,128)(2,1)S(1)} %pad_maximum_fusion.5), channel_id=1, source_target_pairs={{0,8},{1,9},{2,10},{3,11},{4,12},{5,13},{6,14},{7,15},{8,0},{9,1},... | collective-permute-start | bytes 196616 | tf_op jit(solution)/shard_map/ppermute | solution.py:431
  149.8 7.9 %collective-permute-start.31 = (bf16[4,64,128]{2,1,0:T(8,128)(2,1)S(1)}, bf16[4,64,128]{2,1,0:T(8,128)(2,1)S(1)}, u32[]{:S(2)}, u32[]{:S(2)}) collective-permute-start(bf16[4,64,128]{2,1,0:T(8,128)(2,1)S(1)} %pad_maximum_fusion.5), channel_id=1, source_target_pairs={{0,12},{1,13},{2,14},{3,15},{4,0},{5,1},{6,2},{7,3},{8,4},{9,5},{1... | collective-permute-start | bytes 196616 | tf_op jit(solution)/shard_map/ppermute | solution.py:431
  157.8 5.8 %copy-start.1 = (bf16[16,64,128]{2,1,0:T(8,128)(2,1)}, bf16[16,64,128]{2,1,0:T(8,128)(2,1)S(1)}, u32[]{:S(2)}) copy-start(bf16[16,64,128]{2,1,0:T(8,128)(2,1)S(1)} %pad_maximum_fusion.1.near_ref) | copy-start | bytes 786436
  157.8 5.8 %collective-permute-start.32 = (bf16[16,64,128]{2,1,0:T(8,128)(2,1)S(1)}, bf16[16,64,128]{2,1,0:T(8,128)(2,1)S(1)}, u32[]{:S(2)}, u32[]{:S(2)}) collective-permute-start(bf16[16,64,128]{2,1,0:T(8,128)(2,1)S(1)} %pad_maximum_fusion.1.near_ref), channel_id=1, source_target_pairs={{0,16},{16,0},{32,48},{48,32},{64,80},{80,64},{96,112},{112,96},{1... | collective-permute-start | bytes 786440 | tf_op jit(solution)/shard_map/ppermute | solution.py:561
  163.6 0.7 copy-start.5

commit v3 on v2

v3 whole, which is shorter than its diff:
```python
import functools
import math

import jax
import jax.numpy as jnp
from jax import lax
from jax.experimental import pallas as pl
from jax.experimental.pallas import tpu as pltpu
from jax.sharding import PartitionSpec as P

BLK = 128
NBL = 16
WIDE = 256
HALVES = NBL * BLK // WIDE
LANES = 128
CHUNK = 64
JOINED = 4
MIB = 1 << 20

f32 = jnp.float32
bf16 = jnp.bfloat16


def spread_body(edges, slots, score_ref, index_ref, grad_ref, dense_ref, own_ref, twin_o_ref,
                twin_ref, far_o_ref, far_ref, grad_t, left_scr, right_scr, low_scr, high_scr, main_scr, rest_scr, dense,
                acc, sem):
    blocks = dense.shape[0]
    pad = ((0, LANES - edges), (0, 0))
    lanes = lax.broadcasted_iota(jnp.int32, (edges, LANES), 1).astype(f32).astype(bf16)
    halves = lax.broadcasted_iota(jnp.int32, (HALVES, LANES), 0).astype(f32)
    one = jnp.ones((edges, LANES), bf16)
    none = jnp.zeros((edges, LANES), bf16)
    tail = jnp.zeros((LANES - edges, WIDE), bf16)
    acc[...] = jnp.zeros_like(acc)
    score = score_ref[...]
    logit = jnp.where(score > 0, score, 0.2 * score)
    expo = jnp.exp(logit - jnp.max(logit, axis=0, keepdims=True))
    alpha = expo / jnp.sum(expo, axis=0, keepdims=True)
    main = alpha.astype(bf16).astype(f32)
    rest = (alpha - main).astype(bf16).astype(f32)
    index = index_ref[...]
    low_scr[...] = (index % WIDE).astype(f32)
    high = jnp.pad((index // WIDE).astype(f32), pad, constant_values=-1.0)
    main = jnp.pad(jnp.where(score > 0, main, -main), pad)
    rest = jnp.pad(jnp.where(score > 0, rest, -rest), pad)
    for b in range(blocks):
        nodes = slice(b * BLK, (b + 1) * BLK)
        high_scr[nodes, :] = high[:, nodes].T
        main_scr[nodes, :] = main[:, nodes].T
        rest_scr[nodes, :] = rest[:, nodes].T
        grad_t[b] = grad_ref[nodes, :].T

    def out_copy(step):
        return pltpu.make_async_copy(dense.at[step], dense_ref.at[step], sem.at[step])

    def block(step, carry):
        nodes = pl.ds(pl.multiple_of(step * BLK, BLK), BLK)
        low = low_scr[:, nodes]
        high, main, rest = high_scr[nodes, :], main_scr[nodes, :], rest_scr[nodes, :]
        for i in range(BLK):
            here = jnp.broadcast_to(high[i:i + 1, :], (HALVES, LANES)) == halves
            lhs = jnp.concatenate(
                [
                    jnp.where(here, jnp.broadcast_to(term[i:i + 1, :], (HALVES, LANES)), 0.0)
                    for term in (main, rest)
                ],
                axis=0,
            ).astype(bf16)
            column = jnp.broadcast_to(low[:, i:i + 1], (edges, LANES)).astype(bf16)
            rhs = jnp.concatenate(
                [jnp.where(column == lanes + LANES * c, one, none) for c in range(WIDE // LANES)],
                axis=1,
            )
            rhs = jnp.concatenate([rhs, tail], axis=0)
            out = jnp.dot(lhs, rhs, preferred_element_type=f32)
            left_scr[2 * HALVES * i:2 * HALVES * (i + 1), :] = out[:, :LANES]
            right_scr[2 * HALVES * i:2 * HALVES * (i + 1), :] = out[:, LANES:]
        for s in range(NBL):
            scr = (left_scr, right_scr)[s % 2]
            main = scr[pl.ds(s // 2, BLK, stride=2 * HALVES), :]
            rest = scr[pl.ds(HALVES + s // 2, BLK, stride=2 * HALVES), :]
            dense[step, :, s * BLK:(s + 1) * BLK] = main + rest
            low = jnp.abs(main).astype(bf16)
            term = jnp.dot(grad_t[step], low, preferred_element_type=f32)[None]
            acc[pl.ds(slots[step, s], 1)] += term
        out_copy(step).start()
        return carry

    lax.fori_loop(0, blocks, block, 0)
    per = own_ref.shape[0]

    def cast(k, carry):
        own_ref[pl.ds(k, 1)] = acc[pl.ds(2 * per + k, 1)]
        return carry

    def cast_own(k, carry):
        twin_o_ref[pl.ds(k, 1)] = acc[pl.ds(k, 1)].astype(bf16)
        far_o_ref[pl.ds(k, 1)] = acc[pl.ds(per + k, 1)].astype(bf16)
        return carry

    def cast_sides(k, carry):
        twin_ref[pl.ds(k, 1)] = acc[pl.ds(blocks + k, 1)].astype(bf16)
        far_ref[pl.ds(k, 1)] = acc[pl.ds(per + blocks + k, 1)].astype(bf16)
        return carry

    lax.fori_loop(0, per, cast, 0)
    lax.fori_loop(0, blocks, cast_own, 0)
    lax.fori_loop(0, per - blocks, cast_sides, 0)
    lax.fori_loop(0, blocks, lambda step, carry: (out_copy(step).wait(), carry)[1], 0)


def fixed(shape):
    return pl.BlockSpec(shape, lambda *_: (0,) * len(shape), pipeline_mode=pl.Buffered(1))


def spread(slots, scores, index, grad):
    edges, rows = scores.shape
    blocks = rows // BLK
    width = grad.shape[1]
    per = 3 * blocks
    away = [(blocks, width, BLK), (2 * blocks, width, BLK)]
    sums = [(per, width, BLK)] + away + away + [(blocks, width, BLK)]
    types = [f32] + [bf16] * 5
    dense = (blocks, BLK, NBL * BLK)
    return pl.pallas_call(
        functools.partial(spread_body, edges),
        grid_spec=pltpu.PrefetchScalarGridSpec(
            num_scalar_prefetch=1,
            grid=(1,),
            in_specs=[fixed(scores.shape), fixed(index.shape), fixed(grad.shape)],
            out_specs=[pl.BlockSpec(memory_space=pl.ANY)] + [fixed(shape) for shape in sums],
            scratch_shapes=[
                pltpu.VMEM((2 * HALVES * BLK, LANES), f32),
                pltpu.VMEM((2 * HALVES * BLK, LANES), f32),
                pltpu.VMEM((edges, rows), f32),
                pltpu.VMEM((rows, LANES), f32),
                pltpu.VMEM((rows, LANES), f32),
                pltpu.VMEM((rows, LANES), f32),
                pltpu.VMEM(dense, f32),
                pltpu.VMEM((3 * per, width, BLK), f32),
                pltpu.SemaphoreType.DMA((blocks,)),
            ],
        ),
        out_shape=[jax.ShapeDtypeStruct(dense, f32)]
        + [jax.ShapeDtypeStruct(*pair) for pair in zip(sums, types)],
        compiler_params=pltpu.CompilerParams(
            dimension_semantics=("arbitrary",), vmem_limit_bytes=60 * MIB
        ),
        cost_estimate=pl.CostEstimate(flops=0, bytes_accessed=0, transcendentals=0),
        name="spread",
    )((slots + 2 * per) % (3 * per), scores, index, grad)


def two_terms(row, first, rows):
    at = lax.broadcasted_iota(jnp.int32, (rows, row.shape[1]), 0)
    row = jnp.broadcast_to(row, at.shape)
    main = row.astype(bf16).astype(f32)
    return jnp.where(at == first, main, jnp.where(at == first + 1, row - main, 0.0))


def gradients_body(pieces, place, slots, dense_ref, grad_ref, grad_t, weight_ref, *rest):
    count = len(pieces)
    tables = rest[:count]
    sums_ref, du_ref, keep_ref, send_ref = rest[count:count + 4]
    table, dense, probe, prod, mixed, vec, total, sem = rest[count + 4:]
    blocks = dense.shape[0]
    depth = table.shape[2]
    abreast = prod.shape[0]

    def dense_copy(step):
        return pltpu.make_async_copy(dense_ref.at[step], dense.at[step], sem.at[count + step])

    copies = [
        pltpu.make_async_copy(t, table.at[pl.ds(first, size)], sem.at[k])
        for k, (t, (first, size)) in enumerate(zip(tables, pieces))
    ]
    for copy in copies:
        copy.start()
    lax.fori_loop(0, blocks, lambda step, carry: (dense_copy(step).start(), carry)[1], 0)
    sums_ref[...] = jnp.zeros_like(sums_ref)
    vec[...] = jnp.zeros_like(vec)

    def project(step, carry):
        nodes = pl.ds(pl.multiple_of(step * BLK, BLK), BLK)
        probe[nodes, :] = lax.dot_general(
            grad_ref[nodes, :], weight_ref[...], (((1,), (1,)), ((), ())),
            preferred_element_type=f32,
        ).astype(bf16)
        return carry

    lax.fori_loop(0, blocks, project, 0)
    for copy in copies:
        copy.wait()

    def group(first, carry):
        steps = [first * abreast + u for u in range(abreast)]
        means = []
        for u, step in enumerate(steps):
            dense_copy(step).wait()
            row = probe[pl.ds(pl.multiple_of(step * BLK, BLK), BLK), :]
            inner = jnp.zeros((BLK, BLK), f32)
            sized = jnp.zeros((BLK, BLK), f32)
            for s in range(NBL):
                cols = slice(s * BLK, (s + 1) * BLK)
                d = lax.dot_general(
                    row, table[slots[step, s]], (((1,), (1,)), ((), ())),
                    preferred_element_type=f32,
                )
                prod[u, :, cols] = d
                a = jnp.abs(dense[step, :, cols])
                inner = inner + a * d
                sized = sized + a
            means.append(
                jnp.sum(inner, axis=1, keepdims=True) / jnp.sum(sized, axis=1, keepdims=True)
            )
        for u, step in enumerate(steps):
            du = jnp.zeros((BLK, BLK), f32)
            mix = jnp.zeros((BLK + 16, depth), f32)
            for first in range(0, NBL, JOINED):
                lhs, rhs = [], []
                for s in range(first, first + JOINED):
                    cols = slice(s * BLK, (s + 1) * BLK)
                    a = dense[step, :, cols]
                    dz = jnp.maximum(a, -0.2 * a) * (prod[u, :, cols] - means[u])
                    du = du + dz
                    slot = slots[step, s]
                    sums = jnp.sum(dz, axis=0, keepdims=True)
                    sums_ref[pl.ds(slot, 1)] += sums[None]
                    lhs.append(
                        jnp.concatenate(
                            [jnp.abs(a).astype(bf16), two_terms(sums, 0, 16).astype(bf16)], axis=0
                        )
                    )
                    rhs.append(table[slot])
                mix = mix + jnp.dot(
                    jnp.concatenate(lhs, axis=1), jnp.concatenate(rhs, axis=0),
                    preferred_element_type=f32,
                )
            row = jnp.broadcast_to(jnp.sum(du, axis=1, keepdims=True), (BLK, BLK)).T[0:1, :]
            du_ref[pl.ds(step, 1)] = row[None]
            mixed[step] = mix[:BLK].astype(bf16)
            vec[...] += mix[BLK:] + jnp.dot(
                two_terms(row, 2, 16).astype(bf16), table[step], preferred_element_type=f32
            )
        return carry

    lax.fori_loop(0, blocks // abreast, group, 0)
    lhs = jnp.concatenate([grad_t[b] for b in range(blocks)], axis=1)
    rhs = mixed[...].reshape(blocks * BLK, depth)
    total[...] = jnp.dot(lhs, rhs, preferred_element_type=f32)
    across = depth // LANES
    chunks = keep_ref.shape[0] // CHUNK
    for q in range(2 * chunks):
        r, c = q // across * CHUNK, q % across * LANES
        p = place[q]
        tile = total[r:r + CHUNK, c:c + LANES]

        @pl.when(p < chunks)
        def _():
            keep_ref[pl.ds(pl.multiple_of(p * CHUNK, CHUNK), CHUNK), :] = tile

        @pl.when(p >= chunks)
        def _():
            send_ref[pl.ds(pl.multiple_of((p - chunks) * CHUNK, CHUNK), CHUNK), :] = tile

    ends = jnp.concatenate(
        [
            (vec[r:r + 1, :] + vec[r + 1:r + 2, :])[:, c * LANES:(c + 1) * LANES]
            for r in (2, 0)
            for c in range(across)
        ],
        axis=0,
    )
    keep_ref[chunks * CHUNK:, :] = ends
    send_ref[chunks * CHUNK:, :] = ends


def gradients(place, slots, dense, grad, grad_t, weight, pieces, tables):
    blocks = dense.shape[0]
    width = grad.shape[1]
    depth = weight.shape[0]
    count = 9 * blocks
    message = (width * depth // (2 * LANES) + 8, LANES)
    return pl.pallas_call(
        functools.partial(gradients_body, pieces),
        grid_spec=pltpu.PrefetchScalarGridSpec(
            num_scalar_prefetch=2,
            grid=(1,),
            in_specs=[pl.BlockSpec(memory_space=pl.ANY)]
            + [fixed(a.shape) for a in (grad, grad_t, weight)]
            + [pl.BlockSpec(memory_space=pl.ANY)] * len(tables),
            out_specs=[
                fixed((count, 1, BLK)), fixed((blocks, 1, BLK)), fixed(message), fixed(message)
            ],
            scratch_shapes=[
                pltpu.VMEM((count, BLK, depth), bf16),
                pltpu.VMEM(dense.shape, f32),
                pltpu.VMEM(grad.shape[:1] + (depth,), bf16),
                pltpu.VMEM((2, BLK, NBL * BLK), f32),
                pltpu.VMEM((blocks, BLK, depth), bf16),
                pltpu.VMEM((16, depth), f32),
                pltpu.VMEM((width, depth), f32),
                pltpu.SemaphoreType.DMA((len(tables) + blocks,)),
            ],
        ),
        out_shape=[
            jax.ShapeDtypeStruct((count, 1, BLK), f32),
            jax.ShapeDtypeStruct((blocks, 1, BLK), f32),
            jax.ShapeDtypeStruct(message, f32),
            jax.ShapeDtypeStruct(message, f32),
        ],
        compiler_params=pltpu.CompilerParams(
            dimension_semantics=("arbitrary",), vmem_limit_bytes=60 * MIB
        ),
        cost_estimate=pl.CostEstimate(flops=0, bytes_accessed=0, transcendentals=0),
        name="gradients",
    )(place, slots, dense, grad, grad_t, weight, *tables)


def columns_of(row):
    return jnp.broadcast_to(row, (LANES, row.shape[1])).T


def finish_weight_body(scale, place, near_ref, away_ref, vec_ref, src_ref, dst_ref, weight_ref,
                       out_ref, grad_src_ref, grad_dst_ref, total):
    across = total.shape[1] // LANES
    chunks = near_ref.shape[0]
    for q in range(2 * chunks):
        r, c = q // across * CHUNK, q % across * LANES
        p = place[q]
        at = lax.rem(p, chunks)
        tile = jnp.where(p < chunks, near_ref[at].astype(f32), away_ref[at].astype(f32))
        total[r:r + CHUNK, c:c + LANES] = tile
    rows = [
        jnp.concatenate([vec_ref[v * across + c][None] for c in range(across)], axis=1)
        for v in range(2)
    ]
    full = total[...]
    for ref, row in zip((src_ref, dst_ref), rows):
        full = full + jnp.concatenate([columns_of(ref[...])] * across, axis=1) * row
    out_ref[...] = full.T * scale
    terms = [two_terms(rows[0], 0, 16), two_terms(rows[1], 2, 16)]
    for v, row in enumerate(rows):
        main = row.astype(bf16).astype(f32)
        last = row - main
        last = last - last.astype(bf16).astype(f32)
        at = lax.broadcasted_iota(jnp.int32, (16, row.shape[1]), 0)
        terms.append(jnp.where(at == 4 + v, last, 0.0))
    lhs = sum(terms[1:], terms[0]).astype(bf16)
    out = jnp.dot(lhs, weight_ref[...], preferred_element_type=f32) * scale
    grad_src_ref[...] = (out[0:1, :] + out[1:2, :] + out[4:5, :]).reshape(out.shape[1])
    grad_dst_ref[...] = (out[2:3, :] + out[3:4, :] + out[5:6, :]).reshape(out.shape[1])


def finish_weight(place, near, away, vec, src, dst, weight, scale):
    depth, width = weight.shape
    whole = lambda shape: pl.BlockSpec(shape, lambda i, p: (0,) * len(shape))
    args = (near, away, vec, src, dst, weight)
    return pl.pallas_call(
        functools.partial(finish_weight_body, scale),
        grid_spec=pltpu.PrefetchScalarGridSpec(
            num_scalar_prefetch=1,
            grid=(1,),
            in_specs=[whole(a.shape) for a in args],
            out_specs=[whole((depth, width)), whole((width,)), whole((width,))],
            scratch_shapes=[pltpu.VMEM((width, depth), f32)],
        ),
        out_shape=[
            jax.ShapeDtypeStruct((depth, width), f32),
            jax.ShapeDtypeStruct((width,), f32),
            jax.ShapeDtypeStruct((width,), f32),
        ],
        compiler_params=pltpu.CompilerParams(
            dimension_semantics=("arbitrary",), vmem_limit_bytes=60 * MIB
        ),
        name="finish_weight",
    )(place, *args)


def finish_features_body(own_ref, twin_ref, far_ref, above_ref, below_ref, du_ref, sums_ref,
                         src_ref, dst_ref, weight_ref, out_ref, src_cols, dst_cols):
    @pl.when(pl.program_id(0) == 0)
    def _():
        src_cols[...] = columns_of(src_ref[...])
        dst_cols[...] = columns_of(dst_ref[...])

    width = own_ref.shape[1]
    for k in range(du_ref.shape[0]):
        total = own_ref[k] + twin_ref[k].astype(f32) + far_ref[k].astype(f32)
        sums = sums_ref[k]
        for ref in (above_ref, below_ref):
            total = total + ref[k, :width].astype(f32)
            carried = ref[k, width:width + 16].astype(f32)
            sums = sums + carried[0:1] + carried[1:2] + carried[2:3]
        total = total + src_cols[...] * du_ref[k] + dst_cols[...] * sums
        out_ref[k * BLK:(k + 1) * BLK, :] = lax.dot_general(
            total.T.astype(bf16), weight_ref[...], (((1,), (1,)), ((), ())),
            preferred_element_type=f32,
        ).astype(bf16)


def finish_features(own, twin, far, above, below, du, sums, src, dst, weight):
    blocks = du.shape[0]
    depth, width = weight.shape
    group = blocks // 2
    tile = lambda array: pl.BlockSpec((group,) + array.shape[1:], lambda b: (b, 0, 0))
    line = pl.BlockSpec((1, width), lambda b: (0, 0))
    arrays = [own, twin, far, above, below, du, sums]
    return pl.pallas_call(
        finish_features_body,
        grid=(blocks // group,),
        in_specs=[tile(array) for array in arrays] + [line] * 2
        + [pl.BlockSpec(weight.shape, lambda b: (0, 0))],
        out_specs=pl.BlockSpec((group * BLK, depth), lambda b: (b, 0)),
        scratch_shapes=[pltpu.VMEM((width, BLK), f32)] * 2,
        out_shape=jax.ShapeDtypeStruct((blocks * BLK, depth), bf16),
        compiler_params=pltpu.CompilerParams(
            dimension_semantics=("arbitrary",), vmem_limit_bytes=60 * MIB
        ),
        cost_estimate=pl.CostEstimate(
            flops=6 * 10**9, bytes_accessed=MIB, transcendentals=0
        ),
        name="finish_features",
    )(*arrays, src, dst, weight)


def ring(axis, low, count, offset):
    size = lax.axis_size(axis)
    turned = lambda i: ((i >> low) + offset) % count - (i >> low) % count
    return [(i, i + (turned(i) << low)) for i in range(size)]


def turned(array, stage):
    axis, low, count = stage
    return [lax.ppermute(array, axis, ring(axis, low, count, k)) for k in range(1, count)]


def three_terms(array, axis):
    main = array.astype(bf16)
    rest = array - main.astype(f32)
    second = rest.astype(bf16)
    last = (rest - second.astype(f32)).astype(bf16)
    return jnp.concatenate([main, second, last], axis=axis)


def scattered(array, stage, tail, low=False):
    axis, start, count = stage
    rows = (array.shape[0] - tail) // count
    ends = array[count * rows:]
    total = [array[:rows], ends]
    for k in range(1, count):
        chunk = array[k * rows:(k + 1) * rows]
        if low:
            message = jnp.concatenate(
                [chunk.astype(bf16), three_terms(ends, 0), jnp.zeros((tail, LANES), bf16)]
            )
        else:
            message = jnp.concatenate([chunk, ends])
        came = lax.ppermute(message, axis, ring(axis, start, count, k)).astype(f32)
        total[0] = total[0] + came[:rows]
        for r in range(rows, rows + (3 if low else 1) * tail, tail):
            total[1] = total[1] + came[r:r + tail]
    return jnp.concatenate(total)


def after(array, *others):
    return lax.optimization_barrier((array, *others))[0]


def crossed(first, second, size):
    return [(a * size + c, b * size + d) for a, b in first for c, d in second]


def places(stages, sign):
    chunk = jnp.arange(math.prod(n for _, _, n in stages), dtype=jnp.int32)
    place, stride = jnp.zeros_like(chunk), 1
    for axis, low, count in stages[::-1]:
        here = (lax.axis_index(axis) >> low) % count
        place = place + (sign * (chunk // stride % count - here)) % count * stride
        stride = stride * count
    return place


def on_device(features, weight, attn_src, attn_dst, upstream, scores, neighbour_lists, edge_index):
    rows, depth = features.shape
    width = weight.shape[1]
    blocks = rows // BLK
    size_x = lax.axis_size("gx")
    size_y = lax.axis_size("gy")
    here_x = lax.axis_index("gx")
    here_y = lax.axis_index("gy")
    twin = [(i, i ^ 1) for i in range(size_x)]
    far = [(i, (((i + 1) ^ 1) - 1) % size_x) for i in range(size_x)]
    up = [(i, (i + 1) % size_y) for i in range(size_y)]
    down = [(i, (i - 1) % size_y) for i in range(size_y)]

    owner = neighbour_lists // blocks
    owner_x, owner_y = owner // size_y, owner % size_y
    part_x = jnp.where(owner_x == here_x, 0, jnp.where(owner_x // 2 == here_x // 2, 1, 2))
    part_y = jnp.where(owner_y == here_y, 0, jnp.where(owner_y == (here_y + 1) % size_y, 1, 2))
    slots = (part_x * 3 + part_y) * blocks + neighbour_lists % blocks

    own = features.reshape(blocks, BLK, depth)
    above = lax.ppermute(own, "gy", down)
    below = lax.ppermute(own, "gy", up)
    away = lax.ppermute(own, "gx", far)
    from_y = [lax.ppermute(own, ("gx", "gy"), crossed(far, way, size_y)) for way in (down, up)]
    dense, acc_own, twin_o, acc_twin, far_o, acc_far, grad_t = spread(
        slots, scores.T, edge_index.T, upstream
    )
    away, *from_y, dense, acc_own, acc_twin, acc_far, own_late = lax.optimization_barrier(
        (away, *from_y, dense, acc_own, acc_twin, acc_far, own)
    )
    across = lax.ppermute(own_late, "gx", twin)
    above, below, across = lax.optimization_barrier((above, below, across))
    sides = [across] + [lax.ppermute(t, "gx", twin) for t in (above, below)]
    from_far = lax.ppermute(acc_far, "gx", far)
    from_twin = lax.ppermute(acc_twin, "gx", twin)
    tables = [own, above, below, *sides, away, *from_y]
    pieces = tuple((k * blocks, blocks) for k in range(9))

    core, along_y, along_z = ("gx", 0, 2), ("gy", 0, 4), ("gx", 1, size_x // 2)
    stages = (core, along_y, along_z)
    sums, du, keep, send = gradients(
        places(stages, 1), slots, dense, upstream, grad_t, weight, pieces, tables
    )
    sums, du, keep, send, from_far, from_twin = lax.optimization_barrier(
        (sums, du, keep, send, from_far, from_twin)
    )
    sums = sums.reshape(3, 3, blocks, 1, BLK)
    part = keep + lax.ppermute(send, "gx", twin)

    part, sums = lax.optimization_barrier((part, sums))
    sums = sums[0] + lax.ppermute(sums[1], "gx", twin) + lax.ppermute(sums[2], "gx", far)

    def column(k):
        rows = slice((k - 1) * blocks, k * blocks)
        total = acc_own[k * blocks:(k + 1) * blocks] + from_twin[rows].astype(f32)
        total = total + from_far[rows].astype(f32)
        terms = jnp.pad(three_terms(sums[k], 1), ((0, 0), (0, 13), (0, 0)))
        return jnp.concatenate([total.astype(bf16), terms], axis=1)

    part = scattered(part, along_y, 8, low=True)
    part, to_above, to_below = lax.optimization_barrier((part, column(1), column(2)))
    from_below = lax.ppermute(to_above, "gy", up)
    from_above = lax.ppermute(to_below, "gy", down)
    part = scattered(part, along_z, 8)
    part, far_o, twin_o = lax.optimization_barrier((part, far_o, twin_o))
    from_far_o = lax.ppermute(far_o, "gx", far)
    from_twin_o = lax.ppermute(twin_o, "gx", twin)
    part, from_below, from_above, from_far_o, from_twin_o = lax.optimization_barrier(
        (part, from_below, from_above, from_far_o, from_twin_o)
    )
    part = sum(turned(part, ("gy", 2, size_y // 4)), part)
    vec = part[CHUNK:]
    part = part[:CHUNK].astype(bf16)
    part = jnp.stack([part] + turned(part, along_z))
    part, du = lax.optimization_barrier((part, du))
    part = jnp.concatenate([part] + turned(part, along_y))
    src, dst = attn_src[None], attn_dst[None]
    grad_features = finish_features(
        acc_own, from_twin_o, from_far_o, from_above, from_below, du, sums[0], src, dst, weight
    )
    part, grad_features = lax.optimization_barrier((part, grad_features))
    scale = 1.0 / math.sqrt(rows * size_x * size_y)
    grad_weight, grad_src, grad_dst = finish_weight(
        places(stages, -1), part, lax.ppermute(part, "gx", twin), vec, src, dst, weight, scale
    )
    return (grad_features, grad_weight, grad_src, grad_dst)


def solution(mesh):
    rows = P(("gx", "gy"), None)
    return jax.shard_map(
        on_device,
        mesh=mesh,
        in_specs=(rows, P(), P(), P(), rows, rows, rows, rows),
        out_specs=(rows, P(), P(), P()),
        check_vma=False,
    )
```

time: 168 us -> 158 us (0.940)
  Pallas kernels: 70.1 us -> 54.1 us
  waiting for transfers between devices: 27.3 us -> 36.5 us
  starting transfers between devices: 49.6 us -> 56.1 us
  other arithmetic: 11.6 us -> 6.4 us
  matrix products: 2.75 us -> 0 us
  local copies, waits for them, and re-layouts: 5.29 us -> 3 us
    pallas_call x3 -> x2, Pallas kernels: 43.4 us -> 24.3 us  [the longest x1 19.1 us: gradients(): pl.pallas_call(functools.partial(gradients_body, pieces), grid_spec=pltpu...]
    ppermute x16, waiting for transfers between devices: 19 us -> 26.7 us  [the longest x1 19.6 us: on_device(): from_below = lax.ppermute(to_above, 'gy', up)]
    ppermute x16, starting transfers between devices: 25.1 us -> 30.5 us  [the longest x6 8.91 us: scattered(): came = lax.ppermute(message, axis, ring(axis, start, count, k)).astype(f32)]
    ppermute x1, waiting for transfers between devices: 0.01 us -> 4.05 us  [on_device(): below = lax.ppermute(own, 'gy', up)]
    pallas_call x1, Pallas kernels: 23.3 us -> 26.4 us  [spread(): pl.pallas_call(functools.partial(spread_body, edges), grid_spec=pltpu.Pre...]
    dot_general x1 -> x0, matrix products: 2.75 us -> none  [on_device(): lax.dot_general(upstream, weight, (((1,), (1,)), ((), ())), preferred_ele...]
    convert_element_type x3 -> x5, other arithmetic: 6.08 us -> 3.57 us  [the longest x1 3.52 us: column(): return jnp.concatenate([total.astype(bf16), terms], axis=1)]
    ppermute x1, waiting for transfers between devices: 2.29 us -> 0.01 us  [on_device(): lax.ppermute(sums[2], 'gx', far)]
  transfers between devices with their start and end apart: 33 -> 33, of which waited for: 14 -> 12; matrix products, arithmetic and copies ran while one was open for 8% -> 5% of each run, Pallas kernels for 40% -> 32%
where the time goes in v3:
time: 158 us; the launch traced here: 157 us
  starting transfers between devices  56.1 us (36%)
  Pallas kernels  54.1 us (34%)
  waiting for transfers between devices  36.5 us (23%)
  other arithmetic  6.4 us (4%)
  local copies, waits for them, and re-layouts  3 us (2%)
    pallas_call x1, Pallas kernels, spread(): pl.pallas_call(functools.partial(spread_body, edges), grid_spec=pltpu.Pre...  26.4 us
    ppermute x1, waiting for transfers between devices, on_device(): from_below = lax.ppermute(to_above, 'gy', up)  19.6 us
    pallas_call x1, Pallas kernels, gradients(): pl.pallas_call(functools.partial(gradients_body, pieces), grid_spec=pltpu...  19.1 us
    ppermute x9, starting transfers between devices, turned(): lax.ppermute(array, axis, ring(axis, low, count, k))  9.94 us
    ppermute x6, starting transfers between devices, scattered(): came = lax.ppermute(message, axis, ring(axis, start, count, k)).astype(f32)  8.91 us
    ppermute x2, starting transfers between devices, on_device(): lax.ppermute(own, ('gx', 'gy'), crossed(far, way, size_y))  7.82 us
    ppermute x1, starting transfers between devices, on_device(): lax.ppermute(part, 'gx', twin)  6.55 us
    pallas_call x1, Pallas kernels, finish_features(): pl.pallas_call(finish_features_body, grid=(blocks // group,), in_specs=[t...  5.14 us
  transfers between devices with their start and end apart: 33, of which 12 were waited for; matrix products, arithmetic and copies ran while one was open for 5% of the time, Pallas kernels for 32%

profile of v3, /device:TPU:1, one launch (start us, length us, event | category | flops | bytes accessed | tf_op | source)
XLA Modules:
  0.0 157.2 jit_solution(15410842696905651623)
XLA Ops:
  0.6 4.1 %collective-permute-start.2 = (bf16[8,128,512]{2,1,0:T(8,128)(2,1)}, bf16[8,128,512]{2,1,0:T(8,128)(2,1)S(1)}, u32[]{:S(2)}, u32[]{:S(2)}) collective-permute-start(bf16[8,128,512]{2,1,0:T(8,128)(2,1)} %bitcast.46), channel_id=1, source_target_pairs={{0,113},{1,114},{2,115},{3,116},{4,117},{5,118},{6,119},{7,120},{8... | collective-permute-start | bytes 3145736 | tf_op jit(solution)/shard_map/ppermute | solution.py:507
  4.7 3.7 %collective-permute-start.1 = (bf16[8,128,512]{2,1,0:T(8,128)(2,1)}, bf16[8,128,512]{2,1,0:T(8,128)(2,1)S(1)}, u32[]{:S(2)}, u32[]{:S(2)}) collective-permute-start(bf16[8,128,512]{2,1,0:T(8,128)(2,1)} %bitcast.47), channel_id=1, source_target_pairs={{0,127},{1,112},{2,113},{3,114},{4,115},{5,116},{6,117},{7,118},{8... | collective-permute-start | bytes 3145736 | tf_op jit(solution)/shard_map/ppermute | solution.py:507
  8.5 1.2 collective-permute-start
  9.7 0.0 collective-permute-start.4
  9.7 4.8 %collective-permute-start.3 = (bf16[8,128,512]{2,1,0:T(8,128)(2,1)}, bf16[8,128,512]{2,1,0:T(8,128)(2,1)}, u32[]{:S(2)}, u32[]{:S(2)}) collective-permute-start(bf16[8,128,512]{2,1,0:T(8,128)(2,1)} %bitcast.50), channel_id=1, source_target_pairs={{0,15},{1,0},{2,1},{3,2},{4,3},{5,4},{6,5},{7,6},{8,7},{9,8},{10,9... | collective-permute-start | bytes 3145736 | tf_op jit(solution)/shard_map/ppermute | solution.py:504
  14.5 1.3 add_select_fusion
  15.8 26.4 %spread.1 = (f32[8,128,2048]{2,1,0:T(8,128)}, f32[24,512,128]{2,1,0:T(8,128)}, bf16[8,512,128]{2,1,0:T(8,128)(2,1)}, bf16[16,512,128]{2,1,0:T(8,128)(2,1)}, bf16...) custom-call(s32[8,16]{1,0:T(8,128)} %get-tuple-element.112.slots, ...), custom_call_target="tpu_custom_call" | custom-call | tf_op jit(solution)/shard_map/spread/pallas_call | solution.py:125
  42.2 0.0 collective-permute-done.2.rest_8_
  42.2 0.0 collective-permute-done.1.rest_7_
  42.3 1.2 collective-permute-done.rest_6_
  43.4 1.0 copy-done.2
  44.4 2.9 %collective-permute-start.5 = (bf16[8,128,512]{2,1,0:T(8,128)(2,1)}, bf16[8,128,512]{2,1,0:T(8,128)(2,1)}, u32[]{:S(2)}, u32[]{:S(2)}) collective-permute-start(bf16[8,128,512]{2,1,0:T(8,128)(2,1)} %bitcast.51), channel_id=1, source_target_pairs={{0,16},{16,0},{32,48},{48,32},{64,80},{80,64},{96,112},{112,96},{1... | collective-permute-start | bytes 3145736 | tf_op jit(solution)/shard_map/ppermute | solution.py:514
  47.3 1.1 collective-permute-start.9
  48.5 4.0 %collective-permute-done.4.rest_2_ = bf16[8,128,512]{2,1,0:T(8,128)(2,1)} collective-permute-done((bf16[8,128,512]{2,1,0:T(8,128)(2,1)}, bf16[8,128,512]{2,1,0:T(8,128)(2,1)}, u32[]{:S(2)}, u32[]{:S(2)}) %collective-permute-start.4) | collective-permute-done | bytes 1048608 | tf_op jit(solution)/shard_map/ppermute | solution.py:505
  52.5 2.6 %collective-permute-start.6 = (bf16[8,128,512]{2,1,0:T(8,128)(2,1)}, bf16[8,128,512]{2,1,0:T(8,128)(2,1)}, u32[]{:S(2)}, u32[]{:S(2)}) collective-permute-start(bf16[8,128,512]{2,1,0:T(8,128)(2,1)} %collective-permute-done.3.rest_1_), channel_id=1, source_target_pairs={{0,16},{16,0},{32,48},{48,32},{64,80},{80,64},{96,112},{112,96},{1... | collective-permute-start | bytes 3145736 | tf_op jit(solution)/shard_map/ppermute | solution.py:516
  55.1 0.1 collective-permute-start.7
  55.2 0.5 fusion.18.place
  55.7 2.0 %collective-permute-done.6.rest_4_ = bf16[8,128,512]{2,1,0:T(8,128)(2,1)} collective-permute-done((bf16[8,128,512]{2,1,0:T(8,128)(2,1)}, bf16[8,128,512]{2,1,0:T(8,128)(2,1)}, u32[]{:S(2)}, u32[]{:S(2)}) %collective-permute-start.6) | collective-permute-done | bytes 1048608 | tf_op jit(solution)/shard_map/ppermute | solution.py:516
  57.8 1.5 collective-permute-done.7.rest_5_
  59.3 19.1 %gradients.1 = (f32[72,1,128]{2,1,0:T(1,128)}, f32[8,1,128]{2,1,0:T(1,128)}, f32[1032,128]{1,0:T(8,128)}, f32[1032,128]{1,0:T(8,128)}) custom-call(s32[32]{0:T(128)} %fusion.18.place, s32[8,16]{1,0:T(8,128)} %get-tuple-element.113.slots, f32[8,128,2048]{2,1,0:T(8,128)} %get-tuple-element.56.dense_ref, bf16[1024,512]{1,0:T(8,128)(2,1)} %grad_ref.3, ...), custom_call_target="tpu_custom_call" | custom-call | tf_op jit(solution)/shard_map/gradients/pallas_call | solution.py:284
  78.4 0.4 collective-permute-start.10
  78.9 3.5 %add_convert_fusion = (bf16[8,512,128]{2,1,0:T(8,128)(2,1)S(1)}, bf16[8,512,128]{2,1,0:T(8,128)(2,1)S(1)}) fusion(f32[24,512,128]{2,1,0:T(8,128)} %get-tuple-element.75.own_ref, bf16[16,512,128]{2,1,0:T(8,128)(2,1)S(1)} %collective-permute-done.8, bf16[16,512,128]{2,1,0:T(8,128)(2,1)} %collective-permute-done.9), kind=kLoop, calls=%fused_computation.3 | loop fusion | flops 5242880 | bytes 10485760 | tf_op jit(solution)/shard_map/convert_element_type | solution.py:541
  82.4 0.1 add.216
  82.5 0.4 collective-permute-start.14
  82.9 1.2 collective-permute-start.15
  84.3 0.1 collective-permute-start.11
  84.3 2.7 %collective-permute-start.13 = (bf16[288,128]{1,0:T(8,128)(2,1)S(1)}, bf16[288,128]{1,0:T(8,128)(2,1)S(1)}, u32[]{:S(2)}, u32[]{:S(2)}) collective-permute-start(bf16[288,128]{1,0:T(8,128)(2,1)S(1)} %constant_dynamic-update-slice_fusion.8), channel_id=1, source_target_pairs={{0,3},{1,0},{2,1},{3,2},{4,7},{5,4},{6,5},{7,6},{8,11},{9,8},{10,9... | collective-permute-start | bytes 221192 | tf_op jit(solution)/shard_map/ppermute | solution.py:459
  87.0 0.9 collective-permute-start.12
  87.9 0.0 collective-permute-done.14
  88.0 0.1 fusion.3
  88.0 0.0 copy-start.10
  88.1 0.0 copy-start.9
  88.1 0.1 fusion.2
  88.2 0.6 collective-permute-done.11
  88.8 3.0 %collective-permute-done.12 = bf16[288,128]{1,0:T(8,128)(2,1)S(1)} collective-permute-done((bf16[288,128]{1,0:T(8,128)(2,1)S(1)}, bf16[288,128]{1,0:T(8,128)(2,1)S(1)}, u32[]{:S(2)}, u32[]{:S(2)}) %collective-permute-start.12) | collective-permute-done | bytes 73760 | tf_op jit(solution)/shard_map/ppermute | solution.py:459
  92.0 2.2 %collective-permute-start.18 = (f32[72,128]{1,0:T(8,128)S(1)}, f32[72,128]{1,0:T(8,128)S(1)}, u32[]{:S(2)}, u32[]{:S(2)}) collective-permute-start(f32[72,128]{1,0:T(8,128)S(1)} %concatenate.49), channel_id=1, source_target_pairs={{0,96},{16,112},{32,0},{48,16},{64,32},{80,48},{96,64},{112,80},{1... | collective-permute-start | bytes 110600 | tf_op jit(solution)/shard_map/ppermute | solution.py:459
  94.2 0.3 collective-permute-start.16
  94.5 2.8 %collective-permute-start.17 = (f32[72,128]{1,0:T(8,128)S(1)}, f32[72,128]{1,0:T(8,128)S(1)}, u32[]{:S(2)}, u32[]{:S(2)}) collective-permute-start(f32[72,128]{1,0:T(8,128)S(1)} %get-tuple-element.127), channel_id=1, source_target_pairs={{0,64},{16,80},{32,96},{48,112},{64,0},{80,16},{96,32},{112,48},{1... | collective-permute-start | bytes 110600 | tf_op jit(solution)/shard_map/ppermute | solution.py:459
  97.2 0.1 collective-permute-start.19
  97.4 4.7 %collective-permute-start.20 = (bf16[8,528,128]{2,1,0:T(8,128)(2,1)S(1)}, bf16[8,528,128]{2,1,0:T(8,128)(2,1)S(1)}, u32[]{:S(2)}, u32[]{:S(2)}) collective-permute-start(bf16[8,528,128]{2,1,0:T(8,128)(2,1)S(1)} %fusion.3), channel_id=1, source_target_pairs={{0,15},{1,0},{2,1},{3,2},{4,3},{5,4},{6,5},{7,6},{8,7},{9,8},{10,9... | collective-permute-start | bytes 3244040 | tf_op jit(solution)/shard_map/ppermute | solution.py:546
  102.1 3.3 %collective-permute-start.21 = (bf16[8,512,128]{2,1,0:T(8,128)(2,1)S(1)}, bf16[8,512,128]{2,1,0:T(8,128)(2,1)S(1)}, u32[]{:S(2)}, u32[]{:S(2)}) collective-permute-start(bf16[8,512,128]{2,1,0:T(8,128)(2,1)S(1)} %copy-done.10), channel_id=1, source_target_pairs={{0,112},{16,32},{32,16},{48,64},{64,48},{80,96},{96,80},{112,0},{1... | collective-permute-start | bytes 3145736 | tf_op jit(solution)/shard_map/ppermute | solution.py:549
  105.4 19.6 %collective-permute-done.19.below_ref = bf16[8,528,128]{2,1,0:T(8,128)(2,1)S(1)} collective-permute-done((bf16[8,528,128]{2,1,0:T(8,128)(2,1)S(1)}, bf16[8,528,128]{2,1,0:T(8,128)(2,1)S(1)}, u32[]{:S(2)}, u32[]{:S(2)}) %collective-permute-start.19) | collective-permute-done | bytes 1081376 | tf_op jit(solution)/shard_map/ppermute | solution.py:545
  125.0 0.0 copy-start.12
  125.1 1.4 collective-permute-start.25
  126.5 0.6 collective-permute-start.24
  127.1 0.9 collective-permute-start.23
  128.0 0.6 slice.194
  128.6 2.2 %collective-permute-done.24 = f32[72,128]{1,0:T(8,128)S(1)} collective-permute-done((f32[72,128]{1,0:T(8,128)S(1)}, f32[72,128]{1,0:T(8,128)S(1)}, u32[]{:S(2)}, u32[]{:S(2)}) %collective-permute-start.24) | collective-permute-done | bytes 36896 | tf_op jit(solution)/shard_map/ppermute | solution.py:435
  130.8 0.4 collective-permute-done.23
  131.2 0.1 collective-permute-start.26
  131.3 0.9 collective-permute-start.27
  132.2 1.8 %collective-permute-start.28 = (bf16[64,128]{1,0:T(8,128)(2,1)S(1)}, bf16[64,128]{1,0:T(8,128)(2,1)S(1)}, u32[]{:S(2)}, u32[]{:S(2)}) collective-permute-start(bf16[64,128]{1,0:T(8,128)(2,1)S(1)} %slice.283), channel_id=1, source_target_pairs={{0,96},{16,112},{32,0},{48,16},{64,32},{80,48},{96,64},{112,80},{1... | collective-permute-start | bytes 49160 | tf_op jit(solution)/shard_map/ppermute | solution.py:435
  134.0 1.1 collective-permute-done.26
  135.1 0.4 collective-permute-done.27
  135.5 0.4 collective-permute-done.28
  135.9 3.6 %collective-permute-start.31 = (bf16[4,64,128]{2,1,0:T(8,128)(2,1)S(1)}, bf16[4,64,128]{2,1,0:T(8,128)(2,1)S(1)}, u32[]{:S(2)}, u32[]{:S(2)}) collective-permute-start(bf16[4,64,128]{2,1,0:T(8,128)(2,1)S(1)} %pad_maximum_fusion.2), channel_id=1, source_target_pairs={{0,3},{1,0},{2,1},{3,2},{4,7},{5,4},{6,5},{7,6},{8,11},{9,8},{10,9... | collective-permute-start | bytes 196616 | tf_op jit(solution)/shard_map/ppermute | solution.py:435
  139.5 0.7 collective-permute-start.29
  140.1 5.1 %finish_features.1 = bf16[1024,512]{1,0:T(8,128)(2,1)} custom-call(f32[24,512,128]{2,1,0:T(8,128)} %get-tuple-element.75.own_ref, bf16[8,512,128]{2,1,0:T(8,128)(2,1)} %copy-done.12, bf16[8,512,128]{2,1,0:T(8,128)(2,1)} %copy-done.11, bf16[8,528,128]{2,1,0:T(8,128)(2,1)} %copy-done.8, bf16[8,528,128]{2,1,0:T(8,128)(2,1)} %copy-done.7, ...), custom_call_target="tpu_custom_call" | custom-call | flops 6000000000 | bytes 1048576 | tf_op jit(solution)/shard_map/finish_features/pallas_call | solution.py:409
  145.4 6.5 %collective-permute-start.32 = (bf16[16,64,128]{2,1,0:T(8,128)(2,1)S(1)}, bf16[16,64,128]{2,1,0:T(8,128)(2,1)S(1)}, u32[]{:S(2)}, u32[]{:S(2)}) collective-permute-start(bf16[16,64,128]{2,1,0:T(8,128)(2,1)S(1)} %pad_maximum_fusion.near_ref), channel_id=1, source_target_pairs={{0,16},{16,0},{32,48},{48,32},{64,80},{80,64},{96,112},{112,96},{1... | collective-permute-start | bytes 786440 | tf_op jit(solution)/shard_map/ppermute | solution.py:567
  151.9 0.5 fusion.17.place
  152.4 0.6 slice.195.vec_ref
  153.0 0.0 collective-permute-done.32.away_ref
  153.1 0.7 copy-done.5
  153.8 3.4 %finish_weight.1 = (f32[512,512]{1,0:T(8,128)}, f32[512]{0:T(512)}, f32[512]{0:T(512)}) custom-call(s32[32]{0:T(128)} %fusion.17.place, bf16[16,64,128]{2,1,0:T(8,128)(2,1)} %copy-done.3, bf16[16,64,128]{2,1,0:T(8,128)(2,1)} %copy-done.5, f32[8,128]{1,0:T(8,128)} %slice.195.vec_ref, f32[1,512]{1,0:T(1,128)} %bitcast.62, f32[1,512]{1,0:T(1,128)} %bitcast.64, ...), custom_call_target="tpu_custom_call" | custom-call | tf_op jit(solution)/shard_map/finish_weight/pallas_call | solution.py:359
  (74 shorter events, 0.5 us)
Async XLA Ops:
  0.6 41.6 %collective-permute-start.2 = (bf16[8,128,512]{2,1,0:T(8,128)(2,1)}, bf16[8,128,512]{2,1,0:T(8,128)(2,1)S(1)}, u32[]{:S(2)}, u32[]{:S(2)}) collective-permute-start(bf16[8,128,512]{2,1,0:T(8,128)(2,1)} %bitcast.46), channel_id=1, source_target_pairs={{0,113},{1,114},{2,115},{3,116},{4,117},{5,118},{6,119},{7,120},{8... | collective-permute-start | bytes 3145736 | tf_op jit(solution)/shard_map/ppermute | solution.py:507
  4.7 37.5 %collective-permute-start.1 = (bf16[8,128,512]{2,1,0:T(8,128)(2,1)}, bf16[8,128,512]{2,1,0:T(8,128)(2,1)S(1)}, u32[]{:S(2)}, u32[]{:S(2)}) collective-permute-start(bf16[8,128,512]{2,1,0:T(8,128)(2,1)} %bitcast.47), channel_id=1, source_target_pairs={{0,127},{1,112},{2,113},{3,114},{4,115},{5,116},{6,117},{7,118},{8... | collective-permute-start | bytes 3145736 | tf_op jit(solution)/shard_map/ppermute | solution.py:507
  8.5 35.0 %collective-permute-start = (bf16[8,128,512]{2,1,0:T(8,128)(2,1)}, bf16[8,128,512]{2,1,0:T(8,128)(2,1)S(1)}, u32[]{:S(2)}, u32[]{:S(2)}) collective-permute-start(bf16[8,128,512]{2,1,0:T(8,128)(2,1)} %bitcast.48), channel_id=1, source_target_pairs={{0,112},{16,32},{32,16},{48,64},{64,48},{80,96},{96,80},{112,0},{1... | collective-permute-start | bytes 3145736 | tf_op jit(solution)/shard_map/ppermute | solution.py:506
  9.7 42.8 %collective-permute-start.4 = (bf16[8,128,512]{2,1,0:T(8,128)(2,1)}, bf16[8,128,512]{2,1,0:T(8,128)(2,1)}, u32[]{:S(2)}, u32[]{:S(2)}) collective-permute-start(bf16[8,128,512]{2,1,0:T(8,128)(2,1)} %bitcast.49), channel_id=1, source_target_pairs={{0,1},{1,2},{2,3},{3,4},{4,5},{5,6},{6,7},{7,8},{8,9},{9,10},{10,1... | collective-permute-start | bytes 3145736 | tf_op jit(solution)/shard_map/ppermute | solution.py:505
  9.7 42.8 %collective-permute-start.3 = (bf16[8,128,512]{2,1,0:T(8,128)(2,1)}, bf16[8,128,512]{2,1,0:T(8,128)(2,1)}, u32[]{:S(2)}, u32[]{:S(2)}) collective-permute-start(bf16[8,128,512]{2,1,0:T(8,128)(2,1)} %bitcast.50), channel_id=1, source_target_pairs={{0,15},{1,0},{2,1},{3,2},{4,3},{5,4},{6,5},{7,6},{8,7},{9,8},{10,9... | collective-permute-start | bytes 3145736 | tf_op jit(solution)/shard_map/ppermute | solution.py:504
  42.2 17.0 %copy-start = (bf16[8,128,512]{2,1,0:T(8,128)(2,1)}, bf16[8,128,512]{2,1,0:T(8,128)(2,1)S(1)}, u32[]{:S(2)}) copy-start(bf16[8,128,512]{2,1,0:T(8,128)(2,1)S(1)} %collective-permute-done.2.rest_8_) | copy-start | bytes 3145732
  42.2 1.2 copy-start.1
  43.4 1.0 copy-start.2
  44.4 8.1 %collective-permute-start.5 = (bf16[8,128,512]{2,1,0:T(8,128)(2,1)}, bf16[8,128,512]{2,1,0:T(8,128)(2,1)}, u32[]{:S(2)}, u32[]{:S(2)}) collective-permute-start(bf16[8,128,512]{2,1,0:T(8,128)(2,1)} %bitcast.51), channel_id=1, source_target_pairs={{0,16},{16,0},{32,48},{48,32},{64,80},{80,64},{96,112},{112,96},{1... | collective-permute-start | bytes 3145736 | tf_op jit(solution)/shard_map/ppermute | solution.py:514
  47.3 31.1 %collective-permute-start.8 = (bf16[16,512,128]{2,1,0:T(8,128)(2,1)}, bf16[16,512,128]{2,1,0:T(8,128)(2,1)S(1)}, u32[]{:S(2)}, u32[]{:S(2)}) collective-permute-start(bf16[16,512,128]{2,1,0:T(8,128)(2,1)} %get-tuple-element.69), channel_id=1, source_target_pairs={{0,112},{16,32},{32,16},{48,64},{64,48},{80,96},{96,80},{112,0},{1... | collective-permute-start | bytes 6291464 | tf_op jit(solution)/shard_map/ppermute | solution.py:517
  47.3 31.1 %collective-permute-start.9 = (bf16[16,512,128]{2,1,0:T(8,128)(2,1)}, bf16[16,512,128]{2,1,0:T(8,128)(2,1)}, u32[]{:S(2)}, u32[]{:S(2)}) collective-permute-start(bf16[16,512,128]{2,1,0:T(8,128)(2,1)} %get-tuple-element.70), channel_id=1, source_target_pairs={{0,16},{16,0},{32,48},{48,32},{64,80},{80,64},{96,112},{112,96},{1... | collective-permute-start | bytes 6291464 | tf_op jit(solution)/shard_map/ppermute | solution.py:518
  52.5 5.2 %collective-permute-start.6 = (bf16[8,128,512]{2,1,0:T(8,128)(2,1)}, bf16[8,128,512]{2,1,0:T(8,128)(2,1)}, u32[]{:S(2)}, u32[]{:S(2)}) collective-permute-start(bf16[8,128,512]{2,1,0:T(8,128)(2,1)} %collective-permute-done.3.rest_1_), channel_id=1, source_target_pairs={{0,16},{16,0},{32,48},{48,32},{64,80},{80,64},{96,112},{112,96},{1... | collective-permute-start | bytes 3145736 | tf_op jit(solution)/shard_map/ppermute | solution.py:516
  55.1 4.1 %collective-permute-start.7 = (bf16[8,128,512]{2,1,0:T(8,128)(2,1)}, bf16[8,128,512]{2,1,0:T(8,128)(2,1)}, u32[]{:S(2)}, u32[]{:S(2)}) collective-permute-start(bf16[8,128,512]{2,1,0:T(8,128)(2,1)} %collective-permute-done.4.rest_2_), channel_id=1, source_target_pairs={{0,16},{16,0},{32,48},{48,32},{64,80},{80,64},{96,112},{112,96},{1... | collective-permute-start | bytes 3145736 | tf_op jit(solution)/shard_map/ppermute | solution.py:516
  78.4 4.0 %copy-start.4 = (f32[1032,128]{1,0:T(8,128)S(1)}, f32[1032,128]{1,0:T(8,128)}, u32[]{:S(2)}) copy-start(f32[1032,128]{1,0:T(8,128)} %get-tuple-element.71) | copy-start | bytes 1585156
  78.4 4.1 %copy-start.6 = (f32[72,1,128]{2,1,0:T(1,128)S(1)}, f32[72,1,128]{2,1,0:T(1,128)}, u32[]{:S(2)}) copy-start(f32[72,1,128]{2,1,0:T(1,128)} %get-tuple-element.73) | copy-start | bytes 110596
  78.4 4.0 %collective-permute-start.10 = (f32[1032,128]{1,0:T(8,128)}, f32[1032,128]{1,0:T(8,128)S(1)}, u32[]{:S(2)}, u32[]{:S(2)}) collective-permute-start(f32[1032,128]{1,0:T(8,128)} %get-tuple-element.72), channel_id=1, source_target_pairs={{0,16},{16,0},{32,48},{48,32},{64,80},{80,64},{96,112},{112,96},{1... | collective-permute-start | bytes 1585160 | tf_op jit(solution)/shard_map/ppermute | solution.py:531
  82.5 5.4 %collective-permute-start.14 = (f32[3,8,1,128]{3,1,0,2:T(8,128)S(1)}, f32[3,8,1,128]{3,1,0,2:T(8,128)S(1)}, u32[]{:S(2)}, u32[]{:S(2)}) collective-permute-start(f32[3,8,1,128]{3,1,0,2:T(8,128)S(1)} %get-tuple-element.121), channel_id=1, source_target_pairs={{0,16},{16,0},{32,48},{48,32},{64,80},{80,64},{96,112},{112,96},{1... | collective-permute-start | bytes 36872 | tf_op jit(solution)/shard_map/ppermute | solution.py:534
  82.9 5.0 %collective-permute-start.15 = (f32[3,8,1,128]{3,1,2,0:T(8,128)S(1)}, f32[3,8,1,128]{3,1,2,0:T(8,128)S(1)}, u32[]{:S(2)}, u32[]{:S(2)}) collective-permute-start(f32[3,8,1,128]{3,1,2,0:T(8,128)S(1)} %get-tuple-element.122), channel_id=1, source_target_pairs={{0,112},{16,32},{32,16},{48,64},{64,48},{80,96},{96,80},{112,0},{1... | collective-permute-start | bytes 36872 | tf_op jit(solution)/shard_map/ppermute | solution.py:534
  84.3 4.5 %collective-permute-start.11 = (bf16[288,128]{1,0:T(8,128)(2,1)S(1)}, bf16[288,128]{1,0:T(8,128)(2,1)S(1)}, u32[]{:S(2)}, u32[]{:S(2)}) collective-permute-start(bf16[288,128]{1,0:T(8,128)(2,1)S(1)} %constant_dynamic-update-slice_fusion), channel_id=1, source_target_pairs={{0,1},{1,2},{2,3},{3,0},{4,5},{5,6},{6,7},{7,4},{8,9},{9,10},{10,1... | collective-permute-start | bytes 221192 | tf_op jit(solution)/shard_map/ppermute | solution.py:459
  84.3 4.4 %collective-permute-start.13 = (bf16[288,128]{1,0:T(8,128)(2,1)S(1)}, bf16[288,128]{1,0:T(8,128)(2,1)S(1)}, u32[]{:S(2)}, u32[]{:S(2)}) collective-permute-start(bf16[288,128]{1,0:T(8,128)(2,1)S(1)} %constant_dynamic-update-slice_fusion.8), channel_id=1, source_target_pairs={{0,3},{1,0},{2,1},{3,2},{4,7},{5,4},{6,5},{7,6},{8,11},{9,8},{10,9... | collective-permute-start | bytes 221192 | tf_op jit(solution)/shard_map/ppermute | solution.py:459
  87.0 4.8 %collective-permute-start.12 = (bf16[288,128]{1,0:T(8,128)(2,1)S(1)}, bf16[288,128]{1,0:T(8,128)(2,1)S(1)}, u32[]{:S(2)}, u32[]{:S(2)}) collective-permute-start(bf16[288,128]{1,0:T(8,128)(2,1)S(1)} %constant_dynamic-update-slice_fusion.4), channel_id=1, source_target_pairs={{0,2},{1,3},{2,0},{3,1},{4,6},{5,7},{6,4},{7,5},{8,10},{9,11},{10,... | collective-permute-start | bytes 221192 | tf_op jit(solution)/shard_map/ppermute | solution.py:459
  88.0 14.0 %copy-start.10 = (bf16[8,512,128]{2,1,0:T(8,128)(2,1)S(1)}, bf16[8,512,128]{2,1,0:T(8,128)(2,1)}, u32[]{:S(2)}) copy-start(bf16[8,512,128]{2,1,0:T(8,128)(2,1)} %get-tuple-element.85) | copy-start | bytes 3145732
  88.1 17.4 %copy-start.9 = (bf16[8,512,128]{2,1,0:T(8,128)(2,1)S(1)}, bf16[8,512,128]{2,1,0:T(8,128)(2,1)}, u32[]{:S(2)}) copy-start(bf16[8,512,128]{2,1,0:T(8,128)(2,1)} %get-tuple-element.86) | copy-start | bytes 3145732
  92.0 10.1 %collective-permute-start.18 = (f32[72,128]{1,0:T(8,128)S(1)}, f32[72,128]{1,0:T(8,128)S(1)}, u32[]{:S(2)}, u32[]{:S(2)}) collective-permute-start(f32[72,128]{1,0:T(8,128)S(1)} %concatenate.49), channel_id=1, source_target_pairs={{0,96},{16,112},{32,0},{48,16},{64,32},{80,48},{96,64},{112,80},{1... | collective-permute-start | bytes 110600 | tf_op jit(solution)/shard_map/ppermute | solution.py:459
  94.2 7.9 %collective-permute-start.16 = (f32[72,128]{1,0:T(8,128)S(1)}, f32[72,128]{1,0:T(8,128)S(1)}, u32[]{:S(2)}, u32[]{:S(2)}) collective-permute-start(f32[72,128]{1,0:T(8,128)S(1)} %get-tuple-element.126), channel_id=1, source_target_pairs={{0,32},{16,48},{32,64},{48,80},{64,96},{80,112},{96,0},{112,16},{1... | collective-permute-start | bytes 110600 | tf_op jit(solution)/shard_map/ppermute | solution.py:459
  94.5 7.5 %collective-permute-start.17 = (f32[72,128]{1,0:T(8,128)S(1)}, f32[72,128]{1,0:T(8,128)S(1)}, u32[]{:S(2)}, u32[]{:S(2)}) collective-permute-start(f32[72,128]{1,0:T(8,128)S(1)} %get-tuple-element.127), channel_id=1, source_target_pairs={{0,64},{16,80},{32,96},{48,112},{64,0},{80,16},{96,32},{112,48},{1... | collective-permute-start | bytes 110600 | tf_op jit(solution)/shard_map/ppermute | solution.py:459
  97.2 27.8 %collective-permute-start.19 = (bf16[8,528,128]{2,1,0:T(8,128)(2,1)S(1)}, bf16[8,528,128]{2,1,0:T(8,128)(2,1)S(1)}, u32[]{:S(2)}, u32[]{:S(2)}) collective-permute-start(bf16[8,528,128]{2,1,0:T(8,128)(2,1)S(1)} %fusion.2), channel_id=1, source_target_pairs={{0,1},{1,2},{2,3},{3,4},{4,5},{5,6},{6,7},{7,8},{8,9},{9,10},{10,1... | collective-permute-start | bytes 3244040 | tf_op jit(solution)/shard_map/ppermute | solution.py:545
  97.4 27.7 %collective-permute-start.20 = (bf16[8,528,128]{2,1,0:T(8,128)(2,1)S(1)}, bf16[8,528,128]{2,1,0:T(8,128)(2,1)S(1)}, u32[]{:S(2)}, u32[]{:S(2)}) collective-permute-start(bf16[8,528,128]{2,1,0:T(8,128)(2,1)S(1)} %fusion.3), channel_id=1, source_target_pairs={{0,15},{1,0},{2,1},{3,2},{4,3},{5,4},{6,5},{7,6},{8,7},{9,8},{10,9... | collective-permute-start | bytes 3244040 | tf_op jit(solution)/shard_map/ppermute | solution.py:546
  102.1 22.9 %collective-permute-start.21 = (bf16[8,512,128]{2,1,0:T(8,128)(2,1)S(1)}, bf16[8,512,128]{2,1,0:T(8,128)(2,1)S(1)}, u32[]{:S(2)}, u32[]{:S(2)}) collective-permute-start(bf16[8,512,128]{2,1,0:T(8,128)(2,1)S(1)} %copy-done.10), channel_id=1, source_target_pairs={{0,112},{16,32},{32,16},{48,64},{64,48},{80,96},{96,80},{112,0},{1... | collective-permute-start | bytes 3145736 | tf_op jit(solution)/shard_map/ppermute | solution.py:549
  105.4 19.6 %collective-permute-start.22 = (bf16[8,512,128]{2,1,0:T(8,128)(2,1)S(1)}, bf16[8,512,128]{2,1,0:T(8,128)(2,1)S(1)}, u32[]{:S(2)}, u32[]{:S(2)}) collective-permute-start(bf16[8,512,128]{2,1,0:T(8,128)(2,1)S(1)} %copy-done.9), channel_id=1, source_target_pairs={{0,16},{16,0},{32,48},{48,32},{64,80},{80,64},{96,112},{112,96},{1... | collective-permute-start | bytes 3145736 | tf_op jit(solution)/shard_map/ppermute | solution.py:550
  125.0 15.1 %copy-start.7 = (bf16[8,528,128]{2,1,0:T(8,128)(2,1)}, bf16[8,528,128]{2,1,0:T(8,128)(2,1)S(1)}, u32[]{:S(2)}) copy-start(bf16[8,528,128]{2,1,0:T(8,128)(2,1)S(1)} %collective-permute-done.19.below_ref) | copy-start | bytes 3244036
  125.0 15.1 %copy-start.8 = (bf16[8,528,128]{2,1,0:T(8,128)(2,1)}, bf16[8,528,128]{2,1,0:T(8,128)(2,1)S(1)}, u32[]{:S(2)}) copy-start(bf16[8,528,128]{2,1,0:T(8,128)(2,1)S(1)} %collective-permute-done.20.above_ref) | copy-start | bytes 3244036
  125.0 15.1 %copy-start.11 = (bf16[8,512,128]{2,1,0:T(8,128)(2,1)}, bf16[8,512,128]{2,1,0:T(8,128)(2,1)S(1)}, u32[]{:S(2)}) copy-start(bf16[8,512,128]{2,1,0:T(8,128)(2,1)S(1)} %collective-permute-done.21.far_ref) | copy-start | bytes 3145732
  125.0 1.5 copy-start.12
  125.1 3.5 %collective-permute-start.25 = (f32[72,128]{1,0:T(8,128)S(1)}, f32[72,128]{1,0:T(8,128)S(1)}, u32[]{:S(2)}, u32[]{:S(2)}) collective-permute-start(f32[72,128]{1,0:T(8,128)S(1)} %pad_maximum_fusion.5), channel_id=1, source_target_pairs={{0,12},{1,13},{2,14},{3,15},{4,0},{5,1},{6,2},{7,3},{8,4},{9,5},{1... | collective-permute-start | bytes 110600 | tf_op jit(solution)/shard_map/ppermute | solution.py:435
  126.5 4.3 %collective-permute-start.24 = (f32[72,128]{1,0:T(8,128)S(1)}, f32[72,128]{1,0:T(8,128)S(1)}, u32[]{:S(2)}, u32[]{:S(2)}) collective-permute-start(f32[72,128]{1,0:T(8,128)S(1)} %pad_maximum_fusion.5), channel_id=1, source_target_pairs={{0,8},{1,9},{2,10},{3,11},{4,12},{5,13},{6,14},{7,15},{8,0},{9,1},... | collective-permute-start | bytes 110600 | tf_op jit(solution)/shard_map/ppermute | solution.py:435
  127.1 4.1 %collective-permute-start.23 = (f32[72,128]{1,0:T(8,128)S(1)}, f32[72,128]{1,0:T(8,128)S(1)}, u32[]{:S(2)}, u32[]{:S(2)}) collective-permute-start(f32[72,128]{1,0:T(8,128)S(1)} %pad_maximum_fusion.5), channel_id=1, source_target_pairs={{0,4},{1,5},{2,6},{3,7},{4,8},{5,9},{6,10},{7,11},{8,12},{9,13},{1... | collective-permute-start | bytes 110600 | tf_op jit(solution)/shard_map/ppermute | solution.py:435
  131.2 3.9 %collective-permute-start.26 = (bf16[64,128]{1,0:T(8,128)(2,1)S(1)}, bf16[64,128]{1,0:T(8,128)(2,1)S(1)}, u32[]{:S(2)}, u32[]{:S(2)}) collective-permute-start(bf16[64,128]{1,0:T(8,128)(2,1)S(1)} %slice.283), channel_id=1, source_target_pairs={{0,32},{16,48},{32,64},{48,80},{64,96},{80,112},{96,0},{112,16},{1... | collective-permute-start | bytes 49160 | tf_op jit(solution)/shard_map/ppermute | solution.py:435
  131.3 4.2 %collective-permute-start.27 = (bf16[64,128]{1,0:T(8,128)(2,1)S(1)}, bf16[64,128]{1,0:T(8,128)(2,1)S(1)}, u32[]{:S(2)}, u32[]{:S(2)}) collective-permute-start(bf16[64,128]{1,0:T(8,128)(2,1)S(1)} %slice.283), channel_id=1, source_target_pairs={{0,64},{16,80},{32,96},{48,112},{64,0},{80,16},{96,32},{112,48},{1... | collective-permute-start | bytes 49160 | tf_op jit(solution)/shard_map/ppermute | solution.py:435
  132.2 3.7 %collective-permute-start.28 = (bf16[64,128]{1,0:T(8,128)(2,1)S(1)}, bf16[64,128]{1,0:T(8,128)(2,1)S(1)}, u32[]{:S(2)}, u32[]{:S(2)}) collective-permute-start(bf16[64,128]{1,0:T(8,128)(2,1)S(1)} %slice.283), channel_id=1, source_target_pairs={{0,96},{16,112},{32,0},{48,16},{64,32},{80,48},{96,64},{112,80},{1... | collective-permute-start | bytes 49160 | tf_op jit(solution)/shard_map/ppermute | solution.py:435
  135.9 9.4 %collective-permute-start.31 = (bf16[4,64,128]{2,1,0:T(8,128)(2,1)S(1)}, bf16[4,64,128]{2,1,0:T(8,128)(2,1)S(1)}, u32[]{:S(2)}, u32[]{:S(2)}) collective-permute-start(bf16[4,64,128]{2,1,0:T(8,128)(2,1)S(1)} %pad_maximum_fusion.2), channel_id=1, source_target_pairs={{0,3},{1,0},{2,1},{3,2},{4,7},{5,4},{6,5},{7,6},{8,11},{9,8},{10,9... | collective-permute-start | bytes 196616 | tf_op jit(solution)/shard_map/ppermute | solution.py:435
  139.5 5.8 %collective-permute-start.30 = (bf16[4,64,128]{2,1,0:T(8,128)(2,1)S(1)}, bf16[4,64,128]{2,1,0:T(8,128)(2,1)S(1)}, u32[]{:S(2)}, u32[]{:S(2)}) collective-permute-start(bf16[4,64,128]{2,1,0:T(8,128)(2,1)S(1)} %pad_maximum_fusion.2), channel_id=1, source_target_pairs={{0,2},{1,3},{2,0},{3,1},{4,6},{5,7},{6,4},{7,5},{8,10},{9,11},{10,... | collective-permute-start | bytes 196616 | tf_op jit(solution)/shard_map/ppermute | solution.py:435
  139.5 5.8 %collective-permute-start.29 = (bf16[4,64,128]{2,1,0:T(8,128)(2,1)S(1)}, bf16[4,64,128]{2,1,0:T(8,128)(2,1)S(1)}, u32[]{:S(2)}, u32[]{:S(2)}) collective-permute-start(bf16[4,64,128]{2,1,0:T(8,128)(2,1)S(1)} %pad_maximum_fusion.2), channel_id=1, source_target_pairs={{0,1},{1,2},{2,3},{3,0},{4,5},{5,6},{6,7},{7,4},{8,9},{9,10},{10,1... | collective-permute-start | bytes 196616 | tf_op jit(solution)/shard_map/ppermute | solution.py:435
  145.3 7.7 %copy-start.3 = (bf16[16,64,128]{2,1,0:T(8,128)(2,1)}, bf16[16,64,128]{2,1,0:T(8,128)(2,1)S(1)}, u32[]{:S(2)}) copy-start(bf16[16,64,128]{2,1,0:T(8,128)(2,1)S(1)} %pad_maximum_fusion.near_ref) | copy-start | bytes 786436
  145.4 7.7 %collective-permute-start.32 = (bf16[16,64,128]{2,1,0:T(8,128)(2,1)S(1)}, bf16[16,64,128]{2,1,0:T(8,128)(2,1)S(1)}, u32[]{:S(2)}, u32[]{:S(2)}) collective-permute-start(bf16[16,64,128]{2,1,0:T(8,128)(2,1)S(1)} %pad_maximum_fusion.near_ref), channel_id=1, source_target_pairs={{0,16},{16,0},{32,48},{48,32},{64,80},{80,64},{96,112},{112,96},{1... | collective-permute-start | bytes 786440 | tf_op jit(solution)/shard_map/ppermute | solution.py:567
  153.1 0.7 copy-start.5

commit v4 on v3

--- a/solution.py
+++ b/solution.py
@@ -13,7 +13,7 @@
 WIDE = 256
 HALVES = NBL * BLK // WIDE
 LANES = 128
-CHUNK = 64
+CHUNK = 256
 JOINED = 4
 MIB = 1 << 20
 
@@ -443,24 +443,35 @@
     return jnp.concatenate([main, second, last], axis=axis)
 
 
-def scattered(array, stage, tail, low=False):
+def lowered(array, ends):
+    return jnp.concatenate(
+        [array.astype(bf16), three_terms(ends, 0), jnp.zeros(ends.shape, bf16)]
+    )
+
+
+def raised(terms):
+    tail = terms.shape[0] // 4
+    return terms[:tail] + terms[tail:2 * tail] + terms[2 * tail:3 * tail]
+
+
+def summed(array, stage):
+    first, across, last = (t.astype(f32) for t in turned(array, stage))
+    return (array.astype(f32) + across) + (first + last)
+
+
+def scattered(array, stage, tail):
     axis, start, count = stage
     rows = (array.shape[0] - tail) // count
     ends = array[count * rows:]
-    total = [array[:rows], ends]
+    own = array[:rows]
+    came = []
     for k in range(1, count):
-        chunk = array[k * rows:(k + 1) * rows]
-        if low:
-            message = jnp.concatenate(
-                [chunk.astype(bf16), three_terms(ends, 0), jnp.zeros((tail, LANES), bf16)]
-            )
-        else:
-            message = jnp.concatenate([chunk, ends])
-        came = lax.ppermute(message, axis, ring(axis, start, count, k)).astype(f32)
-        total[0] = total[0] + came[:rows]
-        for r in range(rows, rows + (3 if low else 1) * tail, tail):
-            total[1] = total[1] + came[r:r + tail]
-    return jnp.concatenate(total)
+        message = lowered(array[k * rows:(k + 1) * rows], ends)
+        came.append(lax.ppermute(message, axis, ring(axis, start, count, k)).astype(f32))
+    first, across, last = came
+    matrix = (own + across[:rows]) + (first[:rows] + last[:rows])
+    vector = (ends + raised(across[rows:])) + (raised(first[rows:]) + raised(last[rows:]))
+    return jnp.concatenate([matrix, vector])
 
 
 def after(array, *others):
@@ -520,7 +531,7 @@
     pieces = tuple((k * blocks, blocks) for k in range(9))
 
     core, along_y, along_z = ("gx", 0, 2), ("gy", 0, 4), ("gx", 1, size_x // 2)
-    stages = (core, along_y, along_z)
+    stages = (core, along_y)
     sums, du, keep, send = gradients(
         places(stages, 1), slots, dense, upstream, grad_t, weight, pieces, tables
     )
@@ -540,22 +551,23 @@
         terms = jnp.pad(three_terms(sums[k], 1), ((0, 0), (0, 13), (0, 0)))
         return jnp.concatenate([total.astype(bf16), terms], axis=1)
 
-    part = scattered(part, along_y, 8, low=True)
-    part, to_above, to_below = lax.optimization_barrier((part, column(1), column(2)))
+    part = scattered(part, along_y, 8)
+    part, sums = lax.optimization_barrier((part, sums))
+    to_above, to_below = column(1), column(2)
     from_below = lax.ppermute(to_above, "gy", up)
     from_above = lax.ppermute(to_below, "gy", down)
-    part = scattered(part, along_z, 8)
+    part = summed(part, along_z)
     part, far_o, twin_o = lax.optimization_barrier((part, far_o, twin_o))
     from_far_o = lax.ppermute(far_o, "gx", far)
     from_twin_o = lax.ppermute(twin_o, "gx", twin)
     part, from_below, from_above, from_far_o, from_twin_o = lax.optimization_barrier(
         (part, from_below, from_above, from_far_o, from_twin_o)
     )
-    part = sum(turned(part, ("gy", 2, size_y // 4)), part)
-    vec = part[CHUNK:]
+    part = summed(lowered(part[:CHUNK], part[CHUNK:]), ("gy", 2, size_y // 4))
+    vec = raised(part[CHUNK:])
     part = part[:CHUNK].astype(bf16)
-    part = jnp.stack([part] + turned(part, along_z))
     part, du = lax.optimization_barrier((part, du))
+    part = part[None]
     part = jnp.concatenate([part] + turned(part, along_y))
     src, dst = attn_src[None], attn_dst[None]
     grad_features = finish_features(

time: 158 us -> 150 us (0.949)
  starting transfers between devices: 56.1 us -> 49.6 us
    ppermute x6 -> x3, starting transfers between devices: 8.91 us -> 3.03 us  [scattered(): lax.ppermute(message, axis, ring(axis, start, count, k)).astype(f32)]
    ppermute x1, starting transfers between devices: 6.55 us -> 4.41 us  [on_device(): lax.ppermute(part, 'gx', twin)]
    ppermute x6 -> x3, waiting for transfers between devices: 3.63 us -> 4.8 us  [scattered(): lax.ppermute(message, axis, ring(axis, start, count, k)).astype(f32)]
  transfers between devices with their start and end apart: 33 -> 30, of which waited for: 12 -> 10; matrix products, arithmetic and copies ran while one was open for 5% -> 5% of each run, Pallas kernels for 32% -> 34%
where the time goes in v4:
time: 150 us
  Pallas kernels  53.8 us (36%)
  starting transfers between devices  49.6 us (33%)
  waiting for transfers between devices  36.3 us (24%)
  other arithmetic  7.02 us (5%)
  local copies, waits for them, and re-layouts  2.41 us (2%)
    pallas_call x1, Pallas kernels, spread(): pl.pallas_call(functools.partial(spread_body, edges), grid_spec=pltpu.Pre...  26.4 us
    ppermute x1, waiting for transfers between devices, on_device(): from_below = lax.ppermute(to_above, 'gy', up)  19.1 us
    pallas_call x1, Pallas kernels, gradients(): pl.pallas_call(functools.partial(gradients_body, pieces), grid_spec=pltpu...  18.9 us
    ppermute x9, starting transfers between devices, turned(): lax.ppermute(array, axis, ring(axis, low, count, k))  11.5 us
    ppermute x2, starting transfers between devices, on_device(): lax.ppermute(own, ('gx', 'gy'), crossed(far, way, size_y))  7.82 us
    pallas_call x1, Pallas kernels, finish_features(): pl.pallas_call(finish_features_body, grid=(blocks // group,), in_specs=[t...  5.14 us
    ppermute x1, starting transfers between devices, on_device(): from_above = lax.ppermute(to_below, 'gy', down)  4.84 us
    ppermute x3, waiting for transfers between devices, scattered(): lax.ppermute(message, axis, ring(axis, start, count, k)).astype(f32)  4.8 us
  transfers between devices with their start and end apart: 30, of which 10 were waited for; matrix products, arithmetic and copies ran while one was open for 5% of the time, Pallas kernels for 34%

profile of v4, /device:TPU:1, one launch (start us, length us, event | category | flops | bytes accessed | tf_op | source)
XLA Modules:
  0.0 150.1 jit_solution(14483496891423932105)
XLA Ops:
  0.6 4.1 %collective-permute-start.2 = (bf16[8,128,512]{2,1,0:T(8,128)(2,1)}, bf16[8,128,512]{2,1,0:T(8,128)(2,1)S(1)}, u32[]{:S(2)}, u32[]{:S(2)}) collective-permute-start(bf16[8,128,512]{2,1,0:T(8,128)(2,1)} %bitcast.36), channel_id=1, source_target_pairs={{0,113},{1,114},{2,115},{3,116},{4,117},{5,118},{6,119},{7,120},{8... | collective-permute-start | bytes 3145736 | tf_op jit(solution)/shard_map/ppermute | solution.py:518
  4.7 3.7 %collective-permute-start.1 = (bf16[8,128,512]{2,1,0:T(8,128)(2,1)}, bf16[8,128,512]{2,1,0:T(8,128)(2,1)S(1)}, u32[]{:S(2)}, u32[]{:S(2)}) collective-permute-start(bf16[8,128,512]{2,1,0:T(8,128)(2,1)} %bitcast.37), channel_id=1, source_target_pairs={{0,127},{1,112},{2,113},{3,114},{4,115},{5,116},{6,117},{7,118},{8... | collective-permute-start | bytes 3145736 | tf_op jit(solution)/shard_map/ppermute | solution.py:518
  8.5 1.2 collective-permute-start
  9.7 4.8 %collective-permute-start.3 = (bf16[8,128,512]{2,1,0:T(8,128)(2,1)}, bf16[8,128,512]{2,1,0:T(8,128)(2,1)}, u32[]{:S(2)}, u32[]{:S(2)}) collective-permute-start(bf16[8,128,512]{2,1,0:T(8,128)(2,1)} %bitcast.40), channel_id=1, source_target_pairs={{0,15},{1,0},{2,1},{3,2},{4,3},{5,4},{6,5},{7,6},{8,7},{9,8},{10,9... | collective-permute-start | bytes 3145736 | tf_op jit(solution)/shard_map/ppermute | solution.py:515
  14.5 1.3 add_select_fusion
  15.8 26.4 %spread.1 = (f32[8,128,2048]{2,1,0:T(8,128)}, f32[24,512,128]{2,1,0:T(8,128)}, bf16[8,512,128]{2,1,0:T(8,128)(2,1)}, bf16[16,512,128]{2,1,0:T(8,128)(2,1)}, bf16...) custom-call(s32[8,16]{1,0:T(8,128)} %get-tuple-element.110.slots, ...), custom_call_target="tpu_custom_call" | custom-call | tf_op jit(solution)/shard_map/spread/pallas_call | solution.py:125
  42.2 0.0 collective-permute-done.2.rest_8_
  42.2 0.0 collective-permute-done.1.rest_7_
  42.2 1.2 collective-permute-done.rest_6_
  43.4 1.0 copy-done.2
  44.4 2.9 %collective-permute-start.5 = (bf16[8,128,512]{2,1,0:T(8,128)(2,1)}, bf16[8,128,512]{2,1,0:T(8,128)(2,1)}, u32[]{:S(2)}, u32[]{:S(2)}) collective-permute-start(bf16[8,128,512]{2,1,0:T(8,128)(2,1)} %bitcast.41), channel_id=1, source_target_pairs={{0,16},{16,0},{32,48},{48,32},{64,80},{80,64},{96,112},{112,96},{1... | collective-permute-start | bytes 3145736 | tf_op jit(solution)/shard_map/ppermute | solution.py:525
  47.3 0.0 collective-permute-start.8
  47.3 1.1 collective-permute-start.9
  48.5 4.0 %collective-permute-done.4.rest_2_ = bf16[8,128,512]{2,1,0:T(8,128)(2,1)} collective-permute-done((bf16[8,128,512]{2,1,0:T(8,128)(2,1)}, bf16[8,128,512]{2,1,0:T(8,128)(2,1)}, u32[]{:S(2)}, u32[]{:S(2)}) %collective-permute-start.4) | collective-permute-done | bytes 1048608 | tf_op jit(solution)/shard_map/ppermute | solution.py:516
  52.5 2.6 %collective-permute-start.6 = (bf16[8,128,512]{2,1,0:T(8,128)(2,1)}, bf16[8,128,512]{2,1,0:T(8,128)(2,1)}, u32[]{:S(2)}, u32[]{:S(2)}) collective-permute-start(bf16[8,128,512]{2,1,0:T(8,128)(2,1)} %collective-permute-done.3.rest_1_), channel_id=1, source_target_pairs={{0,16},{16,0},{32,48},{48,32},{64,80},{80,64},{96,112},{112,96},{1... | collective-permute-start | bytes 3145736 | tf_op jit(solution)/shard_map/ppermute | solution.py:527
  55.1 0.1 collective-permute-start.7
  55.2 0.5 fusion.19.place
  55.7 2.0 %collective-permute-done.6.rest_4_ = bf16[8,128,512]{2,1,0:T(8,128)(2,1)} collective-permute-done((bf16[8,128,512]{2,1,0:T(8,128)(2,1)}, bf16[8,128,512]{2,1,0:T(8,128)(2,1)}, u32[]{:S(2)}, u32[]{:S(2)}) %collective-permute-start.6) | collective-permute-done | bytes 1048608 | tf_op jit(solution)/shard_map/ppermute | solution.py:527
  57.8 1.5 collective-permute-done.7.rest_5_
  59.3 18.9 %gradients.1 = (f32[72,1,128]{2,1,0:T(1,128)}, f32[8,1,128]{2,1,0:T(1,128)}, f32[1032,128]{1,0:T(8,128)}, f32[1032,128]{1,0:T(8,128)}) custom-call(s32[8]{0:T(128)} %fusion.19.place, s32[8,16]{1,0:T(8,128)} %get-tuple-element.111.slots, f32[8,128,2048]{2,1,0:T(8,128)} %get-tuple-element.55.dense_ref, bf16[1024,512]{1,0:T(8,128)(2,1)} %grad_ref.3, ...), custom_call_target="tpu_custom_call" | custom-call | tf_op jit(solution)/shard_map/gradients/pallas_call | solution.py:284
  78.1 0.0 collective-permute-done.8
  78.2 0.4 collective-permute-start.10
  78.6 3.5 %add_convert_fusion = (bf16[8,512,128]{2,1,0:T(8,128)(2,1)S(1)}, bf16[8,512,128]{2,1,0:T(8,128)(2,1)S(1)}) fusion(f32[24,512,128]{2,1,0:T(8,128)} %get-tuple-element.79.own_ref, bf16[16,512,128]{2,1,0:T(8,128)(2,1)S(1)} %collective-permute-done.8, bf16[16,512,128]{2,1,0:T(8,128)(2,1)} %collective-permute-done.9), kind=kLoop, calls=%fused_computation.3 | loop fusion | flops 5242880 | bytes 10485760 | tf_op jit(solution)/shard_map/convert_element_type | solution.py:552
  82.2 0.1 add.184
  82.3 0.2 collective-permute-start.14
  82.5 1.2 collective-permute-start.15
  83.8 0.8 collective-permute-start.11
  84.7 1.7 %collective-permute-start.13 = (bf16[288,128]{1,0:T(8,128)(2,1)S(1)}, bf16[288,128]{1,0:T(8,128)(2,1)S(1)}, u32[]{:S(2)}, u32[]{:S(2)}) collective-permute-start(bf16[288,128]{1,0:T(8,128)(2,1)S(1)} %constant_dynamic-update-slice_fusion.8), channel_id=1, source_target_pairs={{0,3},{1,0},{2,1},{3,2},{4,7},{5,4},{6,5},{7,6},{8,11},{9,8},{10,9... | collective-permute-start | bytes 221192 | tf_op jit(solution)/shard_map/ppermute | solution.py:470
  86.4 0.5 collective-permute-start.12
  86.9 1.7 %collective-permute-done.11 = bf16[288,128]{1,0:T(8,128)(2,1)S(1)} collective-permute-done((bf16[288,128]{1,0:T(8,128)(2,1)S(1)}, bf16[288,128]{1,0:T(8,128)(2,1)S(1)}, u32[]{:S(2)}, u32[]{:S(2)}) %collective-permute-start.11) | collective-permute-done | bytes 73760 | tf_op jit(solution)/shard_map/ppermute | solution.py:470
  88.6 0.8 collective-permute-done.13
  89.4 2.3 %collective-permute-done.12 = bf16[288,128]{1,0:T(8,128)(2,1)S(1)} collective-permute-done((bf16[288,128]{1,0:T(8,128)(2,1)S(1)}, bf16[288,128]{1,0:T(8,128)(2,1)S(1)}, u32[]{:S(2)}, u32[]{:S(2)}) %collective-permute-start.12) | collective-permute-done | bytes 73760 | tf_op jit(solution)/shard_map/ppermute | solution.py:470
  91.8 1.8 %collective-permute-start.18 = (f32[264,128]{1,0:T(8,128)S(1)}, f32[264,128]{1,0:T(8,128)S(1)}, u32[]{:S(2)}, u32[]{:S(2)}) collective-permute-start(f32[264,128]{1,0:T(8,128)S(1)} %pad_maximum_fusion.1), channel_id=1, source_target_pairs={{0,96},{16,112},{32,0},{48,16},{64,32},{80,48},{96,64},{112,80},{1... | collective-permute-start | bytes 405512 | tf_op jit(solution)/shard_map/ppermute | solution.py:435
  93.5 0.0 collective-permute-start.17
  93.5 2.8 %collective-permute-start.16 = (f32[264,128]{1,0:T(8,128)S(1)}, f32[264,128]{1,0:T(8,128)S(1)}, u32[]{:S(2)}, u32[]{:S(2)}) collective-permute-start(f32[264,128]{1,0:T(8,128)S(1)} %pad_maximum_fusion.1), channel_id=1, source_target_pairs={{0,64},{16,80},{32,96},{48,112},{64,0},{80,16},{96,32},{112,48},{1... | collective-permute-start | bytes 405512 | tf_op jit(solution)/shard_map/ppermute | solution.py:435
  96.3 0.0 copy-start.10
  96.3 0.0 copy-start.9
  96.4 0.1 fusion.2
  96.4 0.1 collective-permute-start.19
  96.5 0.1 fusion.3
  96.6 4.8 %collective-permute-start.20 = (bf16[8,528,128]{2,1,0:T(8,128)(2,1)S(1)}, bf16[8,528,128]{2,1,0:T(8,128)(2,1)S(1)}, u32[]{:S(2)}, u32[]{:S(2)}) collective-permute-start(bf16[8,528,128]{2,1,0:T(8,128)(2,1)S(1)} %fusion.3), channel_id=1, source_target_pairs={{0,15},{1,0},{2,1},{3,2},{4,3},{5,4},{6,5},{7,6},{8,7},{9,8},{10,9... | collective-permute-start | bytes 3244040 | tf_op jit(solution)/shard_map/ppermute | solution.py:558
  101.4 0.2 collective-permute-done.16
  101.7 3.3 %collective-permute-start.21 = (bf16[8,512,128]{2,1,0:T(8,128)(2,1)S(1)}, bf16[8,512,128]{2,1,0:T(8,128)(2,1)S(1)}, u32[]{:S(2)}, u32[]{:S(2)}) collective-permute-start(bf16[8,512,128]{2,1,0:T(8,128)(2,1)S(1)} %copy-done.10), channel_id=1, source_target_pairs={{0,112},{16,32},{32,16},{48,64},{64,48},{80,96},{96,80},{112,0},{1... | collective-permute-start | bytes 3145736 | tf_op jit(solution)/shard_map/ppermute | solution.py:561
  105.0 0.0 collective-permute-start.22
  105.0 19.1 %collective-permute-done.19.below_ref = bf16[8,528,128]{2,1,0:T(8,128)(2,1)S(1)} collective-permute-done((bf16[8,528,128]{2,1,0:T(8,128)(2,1)S(1)}, bf16[8,528,128]{2,1,0:T(8,128)(2,1)S(1)}, u32[]{:S(2)}, u32[]{:S(2)}) %collective-permute-start.19) | collective-permute-done | bytes 1081376 | tf_op jit(solution)/shard_map/ppermute | solution.py:557
  124.1 0.0 copy-start.11
  124.2 1.9 %collective-permute-start.25 = (bf16[288,128]{1,0:T(8,128)(2,1)S(1)}, bf16[288,128]{1,0:T(8,128)(2,1)S(1)}, u32[]{:S(2)}, u32[]{:S(2)}) collective-permute-start(bf16[288,128]{1,0:T(8,128)(2,1)S(1)} %constant_dynamic-update-slice_fusion.12), channel_id=1, source_target_pairs={{0,12},{1,13},{2,14},{3,15},{4,0},{5,1},{6,2},{7,3},{8,4},{9,5},{1... | collective-permute-start | bytes 221192 | tf_op jit(solution)/shard_map/ppermute | solution.py:435
  126.1 1.3 collective-permute-start.23
  127.3 0.6 slice.157
  127.9 0.0 collective-permute-done.25
  127.9 3.3 %collective-permute-done.24 = bf16[288,128]{1,0:T(8,128)(2,1)S(1)} collective-permute-done((bf16[288,128]{1,0:T(8,128)(2,1)S(1)}, bf16[288,128]{1,0:T(8,128)(2,1)S(1)}, u32[]{:S(2)}, u32[]{:S(2)}) %collective-permute-start.24) | collective-permute-done | bytes 73760 | tf_op jit(solution)/shard_map/ppermute | solution.py:435
  131.3 0.0 collective-permute-done.23
  131.3 3.2 %collective-permute-start.28 = (bf16[1,256,128]{2,1,0:T(8,128)(2,1)S(1)}, bf16[1,256,128]{2,1,0:T(8,128)(2,1)S(1)}, u32[]{:S(2)}, u32[]{:S(2)}) collective-permute-start(bf16[1,256,128]{2,1,0:T(8,128)(2,1)S(1)} %bitcast.45), channel_id=1, source_target_pairs={{0,3},{1,0},{2,1},{3,2},{4,7},{5,4},{6,5},{7,6},{8,11},{9,8},{10,9... | collective-permute-start | bytes 196616 | tf_op jit(solution)/shard_map/ppermute | solution.py:435
  134.5 0.0 collective-permute-start.27
  134.5 0.7 collective-permute-start.26
  135.2 5.1 %finish_features.1 = bf16[1024,512]{1,0:T(8,128)(2,1)} custom-call(f32[24,512,128]{2,1,0:T(8,128)} %get-tuple-element.79.own_ref, bf16[8,512,128]{2,1,0:T(8,128)(2,1)} %collective-permute-done.22.twin_ref, bf16[8,512,128]{2,1,0:T(8,128)(2,1)} %copy-done.11, bf16[8,528,128]{2,1,0:T(8,128)(2,1)} %copy-done.8, bf16[8,528,128]{2,1,0:T(8,128)(2,1)} %copy-done.7, ...), custom_call_target="tpu_custom_call" | custom-call | flops 6000000000 | bytes 1048576 | tf_op jit(solution)/shard_map/finish_features/pallas_call | solution.py:409
  140.3 0.0 collective-permute-done.28
  140.4 0.0 collective-permute-done.26
  140.4 4.4 %collective-permute-start.29 = (bf16[4,256,128]{2,1,0:T(8,128)(2,1)S(1)}, bf16[4,256,128]{2,1,0:T(8,128)(2,1)S(1)}, u32[]{:S(2)}, u32[]{:S(2)}) collective-permute-start(bf16[4,256,128]{2,1,0:T(8,128)(2,1)S(1)} %pad_maximum_fusion.near_ref), channel_id=1, source_target_pairs={{0,16},{16,0},{32,48},{48,32},{64,80},{80,64},{96,112},{112,96},{1... | collective-permute-start | bytes 786440 | tf_op jit(solution)/shard_map/ppermute | solution.py:579
  144.8 0.5 fusion.20.place
  145.4 0.6 slice_add_fusion.2.vec_ref
  146.0 0.0 collective-permute-done.29.away_ref
  146.0 0.7 copy-done.5
  146.7 3.4 %finish_weight.1 = (f32[512,512]{1,0:T(8,128)}, f32[512]{0:T(512)}, f32[512]{0:T(512)}) custom-call(s32[8]{0:T(128)} %fusion.20.place, bf16[4,256,128]{2,1,0:T(8,128)(2,1)} %copy-done.3, bf16[4,256,128]{2,1,0:T(8,128)(2,1)} %copy-done.5, f32[8,128]{1,0:T(8,128)} %slice_add_fusion.2.vec_ref, f32[1,512]{1,0:T(1,128)} %bitcast.53, f32[1,512]{1,0:T(1,128)} %bitcast.55, ...), custom_call_target="tpu_custom_call" | custom-call | tf_op jit(solution)/shard_map/finish_weight/pallas_call | solution.py:359
  (63 shorter events, 0.5 us)
Async XLA Ops:
  0.6 41.6 %collective-permute-start.2 = (bf16[8,128,512]{2,1,0:T(8,128)(2,1)}, bf16[8,128,512]{2,1,0:T(8,128)(2,1)S(1)}, u32[]{:S(2)}, u32[]{:S(2)}) collective-permute-start(bf16[8,128,512]{2,1,0:T(8,128)(2,1)} %bitcast.36), channel_id=1, source_target_pairs={{0,113},{1,114},{2,115},{3,116},{4,117},{5,118},{6,119},{7,120},{8... | collective-permute-start | bytes 3145736 | tf_op jit(solution)/shard_map/ppermute | solution.py:518
  4.7 37.5 %collective-permute-start.1 = (bf16[8,128,512]{2,1,0:T(8,128)(2,1)}, bf16[8,128,512]{2,1,0:T(8,128)(2,1)S(1)}, u32[]{:S(2)}, u32[]{:S(2)}) collective-permute-start(bf16[8,128,512]{2,1,0:T(8,128)(2,1)} %bitcast.37), channel_id=1, source_target_pairs={{0,127},{1,112},{2,113},{3,114},{4,115},{5,116},{6,117},{7,118},{8... | collective-permute-start | bytes 3145736 | tf_op jit(solution)/shard_map/ppermute | solution.py:518
  8.5 35.0 %collective-permute-start = (bf16[8,128,512]{2,1,0:T(8,128)(2,1)}, bf16[8,128,512]{2,1,0:T(8,128)(2,1)S(1)}, u32[]{:S(2)}, u32[]{:S(2)}) collective-permute-start(bf16[8,128,512]{2,1,0:T(8,128)(2,1)} %bitcast.38), channel_id=1, source_target_pairs={{0,112},{16,32},{32,16},{48,64},{64,48},{80,96},{96,80},{112,0},{1... | collective-permute-start | bytes 3145736 | tf_op jit(solution)/shard_map/ppermute | solution.py:517
  9.7 42.8 %collective-permute-start.4 = (bf16[8,128,512]{2,1,0:T(8,128)(2,1)}, bf16[8,128,512]{2,1,0:T(8,128)(2,1)}, u32[]{:S(2)}, u32[]{:S(2)}) collective-permute-start(bf16[8,128,512]{2,1,0:T(8,128)(2,1)} %bitcast.39), channel_id=1, source_target_pairs={{0,1},{1,2},{2,3},{3,4},{4,5},{5,6},{6,7},{7,8},{8,9},{9,10},{10,1... | collective-permute-start | bytes 3145736 | tf_op jit(solution)/shard_map/ppermute | solution.py:516
  9.7 42.8 %collective-permute-start.3 = (bf16[8,128,512]{2,1,0:T(8,128)(2,1)}, bf16[8,128,512]{2,1,0:T(8,128)(2,1)}, u32[]{:S(2)}, u32[]{:S(2)}) collective-permute-start(bf16[8,128,512]{2,1,0:T(8,128)(2,1)} %bitcast.40), channel_id=1, source_target_pairs={{0,15},{1,0},{2,1},{3,2},{4,3},{5,4},{6,5},{7,6},{8,7},{9,8},{10,9... | collective-permute-start | bytes 3145736 | tf_op jit(solution)/shard_map/ppermute | solution.py:515
  42.2 17.1 %copy-start = (bf16[8,128,512]{2,1,0:T(8,128)(2,1)}, bf16[8,128,512]{2,1,0:T(8,128)(2,1)S(1)}, u32[]{:S(2)}) copy-start(bf16[8,128,512]{2,1,0:T(8,128)(2,1)S(1)} %collective-permute-done.2.rest_8_) | copy-start | bytes 3145732
  42.2 1.2 copy-start.1
  43.4 1.0 copy-start.2
  44.4 8.1 %collective-permute-start.5 = (bf16[8,128,512]{2,1,0:T(8,128)(2,1)}, bf16[8,128,512]{2,1,0:T(8,128)(2,1)}, u32[]{:S(2)}, u32[]{:S(2)}) collective-permute-start(bf16[8,128,512]{2,1,0:T(8,128)(2,1)} %bitcast.41), channel_id=1, source_target_pairs={{0,16},{16,0},{32,48},{48,32},{64,80},{80,64},{96,112},{112,96},{1... | collective-permute-start | bytes 3145736 | tf_op jit(solution)/shard_map/ppermute | solution.py:525
  47.3 30.8 %collective-permute-start.8 = (bf16[16,512,128]{2,1,0:T(8,128)(2,1)}, bf16[16,512,128]{2,1,0:T(8,128)(2,1)S(1)}, u32[]{:S(2)}, u32[]{:S(2)}) collective-permute-start(bf16[16,512,128]{2,1,0:T(8,128)(2,1)} %get-tuple-element.68), channel_id=1, source_target_pairs={{0,112},{16,32},{32,16},{48,64},{64,48},{80,96},{96,80},{112,0},{1... | collective-permute-start | bytes 6291464 | tf_op jit(solution)/shard_map/ppermute | solution.py:528
  47.3 30.8 %collective-permute-start.9 = (bf16[16,512,128]{2,1,0:T(8,128)(2,1)}, bf16[16,512,128]{2,1,0:T(8,128)(2,1)}, u32[]{:S(2)}, u32[]{:S(2)}) collective-permute-start(bf16[16,512,128]{2,1,0:T(8,128)(2,1)} %get-tuple-element.69), channel_id=1, source_target_pairs={{0,16},{16,0},{32,48},{48,32},{64,80},{80,64},{96,112},{112,96},{1... | collective-permute-start | bytes 6291464 | tf_op jit(solution)/shard_map/ppermute | solution.py:529
  52.5 5.2 %collective-permute-start.6 = (bf16[8,128,512]{2,1,0:T(8,128)(2,1)}, bf16[8,128,512]{2,1,0:T(8,128)(2,1)}, u32[]{:S(2)}, u32[]{:S(2)}) collective-permute-start(bf16[8,128,512]{2,1,0:T(8,128)(2,1)} %collective-permute-done.3.rest_1_), channel_id=1, source_target_pairs={{0,16},{16,0},{32,48},{48,32},{64,80},{80,64},{96,112},{112,96},{1... | collective-permute-start | bytes 3145736 | tf_op jit(solution)/shard_map/ppermute | solution.py:527
  55.1 4.1 %collective-permute-start.7 = (bf16[8,128,512]{2,1,0:T(8,128)(2,1)}, bf16[8,128,512]{2,1,0:T(8,128)(2,1)}, u32[]{:S(2)}, u32[]{:S(2)}) collective-permute-start(bf16[8,128,512]{2,1,0:T(8,128)(2,1)} %collective-permute-done.4.rest_2_), channel_id=1, source_target_pairs={{0,16},{16,0},{32,48},{48,32},{64,80},{80,64},{96,112},{112,96},{1... | collective-permute-start | bytes 3145736 | tf_op jit(solution)/shard_map/ppermute | solution.py:527
  78.2 4.0 %copy-start.4 = (f32[1032,128]{1,0:T(8,128)S(1)}, f32[1032,128]{1,0:T(8,128)}, u32[]{:S(2)}) copy-start(f32[1032,128]{1,0:T(8,128)} %get-tuple-element.70) | copy-start | bytes 1585156
  78.2 4.1 %copy-start.6 = (f32[72,1,128]{2,1,0:T(1,128)S(1)}, f32[72,1,128]{2,1,0:T(1,128)}, u32[]{:S(2)}) copy-start(f32[72,1,128]{2,1,0:T(1,128)} %get-tuple-element.72) | copy-start | bytes 110596
  78.2 4.0 %collective-permute-start.10 = (f32[1032,128]{1,0:T(8,128)}, f32[1032,128]{1,0:T(8,128)S(1)}, u32[]{:S(2)}, u32[]{:S(2)}) collective-permute-start(f32[1032,128]{1,0:T(8,128)} %get-tuple-element.71), channel_id=1, source_target_pairs={{0,16},{16,0},{32,48},{48,32},{64,80},{80,64},{96,112},{112,96},{1... | collective-permute-start | bytes 1585160 | tf_op jit(solution)/shard_map/ppermute | solution.py:542
  82.3 4.6 %collective-permute-start.14 = (f32[3,8,1,128]{3,1,0,2:T(8,128)S(1)}, f32[3,8,1,128]{3,1,0,2:T(8,128)S(1)}, u32[]{:S(2)}, u32[]{:S(2)}) collective-permute-start(f32[3,8,1,128]{3,1,0,2:T(8,128)S(1)} %get-tuple-element.117), channel_id=1, source_target_pairs={{0,16},{16,0},{32,48},{48,32},{64,80},{80,64},{96,112},{112,96},{1... | collective-permute-start | bytes 36872 | tf_op jit(solution)/shard_map/ppermute | solution.py:545
  82.5 4.4 %collective-permute-start.15 = (f32[3,8,1,128]{3,1,2,0:T(8,128)S(1)}, f32[3,8,1,128]{3,1,2,0:T(8,128)S(1)}, u32[]{:S(2)}, u32[]{:S(2)}) collective-permute-start(f32[3,8,1,128]{3,1,2,0:T(8,128)S(1)} %get-tuple-element.118), channel_id=1, source_target_pairs={{0,112},{16,32},{32,16},{48,64},{64,48},{80,96},{96,80},{112,0},{1... | collective-permute-start | bytes 36872 | tf_op jit(solution)/shard_map/ppermute | solution.py:545
  83.8 4.8 %collective-permute-start.11 = (bf16[288,128]{1,0:T(8,128)(2,1)S(1)}, bf16[288,128]{1,0:T(8,128)(2,1)S(1)}, u32[]{:S(2)}, u32[]{:S(2)}) collective-permute-start(bf16[288,128]{1,0:T(8,128)(2,1)S(1)} %constant_dynamic-update-slice_fusion), channel_id=1, source_target_pairs={{0,2},{1,3},{2,0},{3,1},{4,6},{5,7},{6,4},{7,5},{8,10},{9,11},{10,... | collective-permute-start | bytes 221192 | tf_op jit(solution)/shard_map/ppermute | solution.py:470
  84.7 4.7 %collective-permute-start.13 = (bf16[288,128]{1,0:T(8,128)(2,1)S(1)}, bf16[288,128]{1,0:T(8,128)(2,1)S(1)}, u32[]{:S(2)}, u32[]{:S(2)}) collective-permute-start(bf16[288,128]{1,0:T(8,128)(2,1)S(1)} %constant_dynamic-update-slice_fusion.8), channel_id=1, source_target_pairs={{0,3},{1,0},{2,1},{3,2},{4,7},{5,4},{6,5},{7,6},{8,11},{9,8},{10,9... | collective-permute-start | bytes 221192 | tf_op jit(solution)/shard_map/ppermute | solution.py:470
  86.4 5.3 %collective-permute-start.12 = (bf16[288,128]{1,0:T(8,128)(2,1)S(1)}, bf16[288,128]{1,0:T(8,128)(2,1)S(1)}, u32[]{:S(2)}, u32[]{:S(2)}) collective-permute-start(bf16[288,128]{1,0:T(8,128)(2,1)S(1)} %constant_dynamic-update-slice_fusion.4), channel_id=1, source_target_pairs={{0,1},{1,2},{2,3},{3,0},{4,5},{5,6},{6,7},{7,4},{8,9},{9,10},{10,1... | collective-permute-start | bytes 221192 | tf_op jit(solution)/shard_map/ppermute | solution.py:470
  91.8 9.7 %collective-permute-start.18 = (f32[264,128]{1,0:T(8,128)S(1)}, f32[264,128]{1,0:T(8,128)S(1)}, u32[]{:S(2)}, u32[]{:S(2)}) collective-permute-start(f32[264,128]{1,0:T(8,128)S(1)} %pad_maximum_fusion.1), channel_id=1, source_target_pairs={{0,96},{16,112},{32,0},{48,16},{64,32},{80,48},{96,64},{112,80},{1... | collective-permute-start | bytes 405512 | tf_op jit(solution)/shard_map/ppermute | solution.py:435
  93.5 7.9 %collective-permute-start.17 = (f32[264,128]{1,0:T(8,128)S(1)}, f32[264,128]{1,0:T(8,128)S(1)}, u32[]{:S(2)}, u32[]{:S(2)}) collective-permute-start(f32[264,128]{1,0:T(8,128)S(1)} %pad_maximum_fusion.1), channel_id=1, source_target_pairs={{0,32},{16,48},{32,64},{48,80},{64,96},{80,112},{96,0},{112,16},{1... | collective-permute-start | bytes 405512 | tf_op jit(solution)/shard_map/ppermute | solution.py:435
  93.5 8.2 %collective-permute-start.16 = (f32[264,128]{1,0:T(8,128)S(1)}, f32[264,128]{1,0:T(8,128)S(1)}, u32[]{:S(2)}, u32[]{:S(2)}) collective-permute-start(f32[264,128]{1,0:T(8,128)S(1)} %pad_maximum_fusion.1), channel_id=1, source_target_pairs={{0,64},{16,80},{32,96},{48,112},{64,0},{80,16},{96,32},{112,48},{1... | collective-permute-start | bytes 405512 | tf_op jit(solution)/shard_map/ppermute | solution.py:435
  96.3 5.4 %copy-start.10 = (bf16[8,512,128]{2,1,0:T(8,128)(2,1)S(1)}, bf16[8,512,128]{2,1,0:T(8,128)(2,1)}, u32[]{:S(2)}) copy-start(bf16[8,512,128]{2,1,0:T(8,128)(2,1)} %get-tuple-element.83) | copy-start | bytes 3145732
  96.3 8.7 %copy-start.9 = (bf16[8,512,128]{2,1,0:T(8,128)(2,1)S(1)}, bf16[8,512,128]{2,1,0:T(8,128)(2,1)}, u32[]{:S(2)}) copy-start(bf16[8,512,128]{2,1,0:T(8,128)(2,1)} %get-tuple-element.84) | copy-start | bytes 3145732
  96.4 27.7 %collective-permute-start.19 = (bf16[8,528,128]{2,1,0:T(8,128)(2,1)S(1)}, bf16[8,528,128]{2,1,0:T(8,128)(2,1)S(1)}, u32[]{:S(2)}, u32[]{:S(2)}) collective-permute-start(bf16[8,528,128]{2,1,0:T(8,128)(2,1)S(1)} %fusion.2), channel_id=1, source_target_pairs={{0,1},{1,2},{2,3},{3,4},{4,5},{5,6},{6,7},{7,8},{8,9},{9,10},{10,1... | collective-permute-start | bytes 3244040 | tf_op jit(solution)/shard_map/ppermute | solution.py:557
  96.6 27.5 %collective-permute-start.20 = (bf16[8,528,128]{2,1,0:T(8,128)(2,1)S(1)}, bf16[8,528,128]{2,1,0:T(8,128)(2,1)S(1)}, u32[]{:S(2)}, u32[]{:S(2)}) collective-permute-start(bf16[8,528,128]{2,1,0:T(8,128)(2,1)S(1)} %fusion.3), channel_id=1, source_target_pairs={{0,15},{1,0},{2,1},{3,2},{4,3},{5,4},{6,5},{7,6},{8,7},{9,8},{10,9... | collective-permute-start | bytes 3244040 | tf_op jit(solution)/shard_map/ppermute | solution.py:558
  101.7 22.4 %collective-permute-start.21 = (bf16[8,512,128]{2,1,0:T(8,128)(2,1)S(1)}, bf16[8,512,128]{2,1,0:T(8,128)(2,1)S(1)}, u32[]{:S(2)}, u32[]{:S(2)}) collective-permute-start(bf16[8,512,128]{2,1,0:T(8,128)(2,1)S(1)} %copy-done.10), channel_id=1, source_target_pairs={{0,112},{16,32},{32,16},{48,64},{64,48},{80,96},{96,80},{112,0},{1... | collective-permute-start | bytes 3145736 | tf_op jit(solution)/shard_map/ppermute | solution.py:561
  105.0 19.1 %collective-permute-start.22 = (bf16[8,512,128]{2,1,0:T(8,128)(2,1)S(1)}, bf16[8,512,128]{2,1,0:T(8,128)(2,1)}, u32[]{:S(2)}, u32[]{:S(2)}) collective-permute-start(bf16[8,512,128]{2,1,0:T(8,128)(2,1)S(1)} %copy-done.9), channel_id=1, source_target_pairs={{0,16},{16,0},{32,48},{48,32},{64,80},{80,64},{96,112},{112,96},{1... | collective-permute-start | bytes 3145736 | tf_op jit(solution)/shard_map/ppermute | solution.py:562
  124.1 11.1 %copy-start.7 = (bf16[8,528,128]{2,1,0:T(8,128)(2,1)}, bf16[8,528,128]{2,1,0:T(8,128)(2,1)S(1)}, u32[]{:S(2)}) copy-start(bf16[8,528,128]{2,1,0:T(8,128)(2,1)S(1)} %collective-permute-done.19.below_ref) | copy-start | bytes 3244036
  124.1 11.1 %copy-start.8 = (bf16[8,528,128]{2,1,0:T(8,128)(2,1)}, bf16[8,528,128]{2,1,0:T(8,128)(2,1)S(1)}, u32[]{:S(2)}) copy-start(bf16[8,528,128]{2,1,0:T(8,128)(2,1)S(1)} %collective-permute-done.20.above_ref) | copy-start | bytes 3244036
  124.1 11.1 %copy-start.11 = (bf16[8,512,128]{2,1,0:T(8,128)(2,1)}, bf16[8,512,128]{2,1,0:T(8,128)(2,1)S(1)}, u32[]{:S(2)}) copy-start(bf16[8,512,128]{2,1,0:T(8,128)(2,1)S(1)} %collective-permute-done.21.far_ref) | copy-start | bytes 3145732
  124.2 3.7 %collective-permute-start.25 = (bf16[288,128]{1,0:T(8,128)(2,1)S(1)}, bf16[288,128]{1,0:T(8,128)(2,1)S(1)}, u32[]{:S(2)}, u32[]{:S(2)}) collective-permute-start(bf16[288,128]{1,0:T(8,128)(2,1)S(1)} %constant_dynamic-update-slice_fusion.12), channel_id=1, source_target_pairs={{0,12},{1,13},{2,14},{3,15},{4,0},{5,1},{6,2},{7,3},{8,4},{9,5},{1... | collective-permute-start | bytes 221192 | tf_op jit(solution)/shard_map/ppermute | solution.py:435
  126.1 5.2 %collective-permute-start.24 = (bf16[288,128]{1,0:T(8,128)(2,1)S(1)}, bf16[288,128]{1,0:T(8,128)(2,1)S(1)}, u32[]{:S(2)}, u32[]{:S(2)}) collective-permute-start(bf16[288,128]{1,0:T(8,128)(2,1)S(1)} %constant_dynamic-update-slice_fusion.12), channel_id=1, source_target_pairs={{0,4},{1,5},{2,6},{3,7},{4,8},{5,9},{6,10},{7,11},{8,12},{9,13},{1... | collective-permute-start | bytes 221192 | tf_op jit(solution)/shard_map/ppermute | solution.py:435
  126.1 5.2 %collective-permute-start.23 = (bf16[288,128]{1,0:T(8,128)(2,1)S(1)}, bf16[288,128]{1,0:T(8,128)(2,1)S(1)}, u32[]{:S(2)}, u32[]{:S(2)}) collective-permute-start(bf16[288,128]{1,0:T(8,128)(2,1)S(1)} %constant_dynamic-update-slice_fusion.12), channel_id=1, source_target_pairs={{0,8},{1,9},{2,10},{3,11},{4,12},{5,13},{6,14},{7,15},{8,0},{9,1},... | collective-permute-start | bytes 221192 | tf_op jit(solution)/shard_map/ppermute | solution.py:435
  131.3 9.0 %collective-permute-start.28 = (bf16[1,256,128]{2,1,0:T(8,128)(2,1)S(1)}, bf16[1,256,128]{2,1,0:T(8,128)(2,1)S(1)}, u32[]{:S(2)}, u32[]{:S(2)}) collective-permute-start(bf16[1,256,128]{2,1,0:T(8,128)(2,1)S(1)} %bitcast.45), channel_id=1, source_target_pairs={{0,3},{1,0},{2,1},{3,2},{4,7},{5,4},{6,5},{7,6},{8,11},{9,8},{10,9... | collective-permute-start | bytes 196616 | tf_op jit(solution)/shard_map/ppermute | solution.py:435
  134.5 5.8 %collective-permute-start.27 = (bf16[1,256,128]{2,1,0:T(8,128)(2,1)S(1)}, bf16[1,256,128]{2,1,0:T(8,128)(2,1)S(1)}, u32[]{:S(2)}, u32[]{:S(2)}) collective-permute-start(bf16[1,256,128]{2,1,0:T(8,128)(2,1)S(1)} %bitcast.46), channel_id=1, source_target_pairs={{0,2},{1,3},{2,0},{3,1},{4,6},{5,7},{6,4},{7,5},{8,10},{9,11},{10,... | collective-permute-start | bytes 196616 | tf_op jit(solution)/shard_map/ppermute | solution.py:435
  134.5 5.8 %collective-permute-start.26 = (bf16[1,256,128]{2,1,0:T(8,128)(2,1)S(1)}, bf16[1,256,128]{2,1,0:T(8,128)(2,1)S(1)}, u32[]{:S(2)}, u32[]{:S(2)}) collective-permute-start(bf16[1,256,128]{2,1,0:T(8,128)(2,1)S(1)} %bitcast.47), channel_id=1, source_target_pairs={{0,1},{1,2},{2,3},{3,0},{4,5},{5,6},{6,7},{7,4},{8,9},{9,10},{10,1... | collective-permute-start | bytes 196616 | tf_op jit(solution)/shard_map/ppermute | solution.py:435
  140.4 5.6 %copy-start.3 = (bf16[4,256,128]{2,1,0:T(8,128)(2,1)}, bf16[4,256,128]{2,1,0:T(8,128)(2,1)S(1)}, u32[]{:S(2)}) copy-start(bf16[4,256,128]{2,1,0:T(8,128)(2,1)S(1)} %pad_maximum_fusion.near_ref) | copy-start | bytes 786436
  140.4 5.6 %collective-permute-start.29 = (bf16[4,256,128]{2,1,0:T(8,128)(2,1)S(1)}, bf16[4,256,128]{2,1,0:T(8,128)(2,1)S(1)}, u32[]{:S(2)}, u32[]{:S(2)}) collective-permute-start(bf16[4,256,128]{2,1,0:T(8,128)(2,1)S(1)} %pad_maximum_fusion.near_ref), channel_id=1, source_target_pairs={{0,16},{16,0},{32,48},{48,32},{64,80},{80,64},{96,112},{112,96},{1... | collective-permute-start | bytes 786440 | tf_op jit(solution)/shard_map/ppermute | solution.py:579
  146.0 0.7 copy-start.5

commit v5 on v4

--- a/solution.py
+++ b/solution.py
@@ -130,8 +130,8 @@
             in_specs=[fixed(scores.shape), fixed(index.shape), fixed(grad.shape)],
             out_specs=[pl.BlockSpec(memory_space=pl.ANY)] + [fixed(shape) for shape in sums],
             scratch_shapes=[
-                pltpu.VMEM((2 * HALVES * BLK, LANES), f32),
-                pltpu.VMEM((2 * HALVES * BLK, LANES), f32),
+                pltpu.VMEM((2 * HALVES * (BLK + 1), LANES), f32),
+                pltpu.VMEM((2 * HALVES * (BLK + 1), LANES), f32),
                 pltpu.VMEM((edges, rows), f32),
                 pltpu.VMEM((rows, LANES), f32),
                 pltpu.VMEM((rows, LANES), f32),

time: 150 us -> 150 us (level)
  no operation moved by 1% of the time
where the time goes in v5:
time: 150 us
  Pallas kernels  53.8 us (36%)
  starting transfers between devices  49.6 us (33%)
  waiting for transfers between devices  36.3 us (24%)
  other arithmetic  7.02 us (5%)
  local copies, waits for them, and re-layouts  2.41 us (2%)
    pallas_call x1, Pallas kernels, spread(): pl.pallas_call(functools.partial(spread_body, edges), grid_spec=pltpu.Pre...  26.4 us
    ppermute x1, waiting for transfers between devices, on_device(): from_below = lax.ppermute(to_above, 'gy', up)  19.1 us
    pallas_call x1, Pallas kernels, gradients(): pl.pallas_call(functools.partial(gradients_body, pieces), grid_spec=pltpu...  18.9 us
    ppermute x9, starting transfers between devices, turned(): lax.ppermute(array, axis, ring(axis, low, count, k))  11.5 us
    ppermute x2, starting transfers between devices, on_device(): lax.ppermute(own, ('gx', 'gy'), crossed(far, way, size_y))  7.82 us
    pallas_call x1, Pallas kernels, finish_features(): pl.pallas_call(finish_features_body, grid=(blocks // group,), in_specs=[t...  5.15 us
    ppermute x1, starting transfers between devices, on_device(): from_above = lax.ppermute(to_below, 'gy', down)  4.84 us
    ppermute x3, waiting for transfers between devices, scattered(): lax.ppermute(message, axis, ring(axis, start, count, k)).astype(f32)  4.79 us
  transfers between devices with their start and end apart: 30, of which 10 were waited for; matrix products, arithmetic and copies ran while one was open for 5% of the time, Pallas kernels for 34%

profile of v5, /device:TPU:1, one launch (start us, length us, event | category | flops | bytes accessed | tf_op | source)
XLA Modules:
  0.0 150.1 jit_solution(16830767673286808208)
XLA Ops:
  0.6 4.1 %collective-permute-start.2 = (bf16[8,128,512]{2,1,0:T(8,128)(2,1)}, bf16[8,128,512]{2,1,0:T(8,128)(2,1)S(1)}, u32[]{:S(2)}, u32[]{:S(2)}) collective-permute-start(bf16[8,128,512]{2,1,0:T(8,128)(2,1)} %bitcast.36), channel_id=1, source_target_pairs={{0,113},{1,114},{2,115},{3,116},{4,117},{5,118},{6,119},{7,120},{8... | collective-permute-start | bytes 3145736 | tf_op jit(solution)/shard_map/ppermute | solution.py:518
  4.7 3.7 %collective-permute-start.1 = (bf16[8,128,512]{2,1,0:T(8,128)(2,1)}, bf16[8,128,512]{2,1,0:T(8,128)(2,1)S(1)}, u32[]{:S(2)}, u32[]{:S(2)}) collective-permute-start(bf16[8,128,512]{2,1,0:T(8,128)(2,1)} %bitcast.37), channel_id=1, source_target_pairs={{0,127},{1,112},{2,113},{3,114},{4,115},{5,116},{6,117},{7,118},{8... | collective-permute-start | bytes 3145736 | tf_op jit(solution)/shard_map/ppermute | solution.py:518
  8.5 1.2 collective-permute-start
  9.7 4.8 %collective-permute-start.3 = (bf16[8,128,512]{2,1,0:T(8,128)(2,1)}, bf16[8,128,512]{2,1,0:T(8,128)(2,1)}, u32[]{:S(2)}, u32[]{:S(2)}) collective-permute-start(bf16[8,128,512]{2,1,0:T(8,128)(2,1)} %bitcast.40), channel_id=1, source_target_pairs={{0,15},{1,0},{2,1},{3,2},{4,3},{5,4},{6,5},{7,6},{8,7},{9,8},{10,9... | collective-permute-start | bytes 3145736 | tf_op jit(solution)/shard_map/ppermute | solution.py:515
  14.5 1.3 add_select_fusion
  15.8 26.4 %spread.1 = (f32[8,128,2048]{2,1,0:T(8,128)}, f32[24,512,128]{2,1,0:T(8,128)}, bf16[8,512,128]{2,1,0:T(8,128)(2,1)}, bf16[16,512,128]{2,1,0:T(8,128)(2,1)}, bf16...) custom-call(s32[8,16]{1,0:T(8,128)} %get-tuple-element.110.slots, ...), custom_call_target="tpu_custom_call" | custom-call | tf_op jit(solution)/shard_map/spread/pallas_call | solution.py:125
  42.2 0.0 collective-permute-done.2.rest_8_
  42.2 1.2 collective-permute-done.rest_6_
  43.4 1.0 copy-done.2
  44.4 2.9 %collective-permute-start.5 = (bf16[8,128,512]{2,1,0:T(8,128)(2,1)}, bf16[8,128,512]{2,1,0:T(8,128)(2,1)}, u32[]{:S(2)}, u32[]{:S(2)}) collective-permute-start(bf16[8,128,512]{2,1,0:T(8,128)(2,1)} %bitcast.41), channel_id=1, source_target_pairs={{0,16},{16,0},{32,48},{48,32},{64,80},{80,64},{96,112},{112,96},{1... | collective-permute-start | bytes 3145736 | tf_op jit(solution)/shard_map/ppermute | solution.py:525
  47.3 0.0 collective-permute-start.8
  47.3 1.1 collective-permute-start.9
  48.5 4.0 %collective-permute-done.4.rest_2_ = bf16[8,128,512]{2,1,0:T(8,128)(2,1)} collective-permute-done((bf16[8,128,512]{2,1,0:T(8,128)(2,1)}, bf16[8,128,512]{2,1,0:T(8,128)(2,1)}, u32[]{:S(2)}, u32[]{:S(2)}) %collective-permute-start.4) | collective-permute-done | bytes 1048608 | tf_op jit(solution)/shard_map/ppermute | solution.py:516
  52.5 2.6 %collective-permute-start.6 = (bf16[8,128,512]{2,1,0:T(8,128)(2,1)}, bf16[8,128,512]{2,1,0:T(8,128)(2,1)}, u32[]{:S(2)}, u32[]{:S(2)}) collective-permute-start(bf16[8,128,512]{2,1,0:T(8,128)(2,1)} %collective-permute-done.3.rest_1_), channel_id=1, source_target_pairs={{0,16},{16,0},{32,48},{48,32},{64,80},{80,64},{96,112},{112,96},{1... | collective-permute-start | bytes 3145736 | tf_op jit(solution)/shard_map/ppermute | solution.py:527
  55.1 0.1 collective-permute-start.7
  55.2 0.5 fusion.19.place
  55.7 2.0 %collective-permute-done.6.rest_4_ = bf16[8,128,512]{2,1,0:T(8,128)(2,1)} collective-permute-done((bf16[8,128,512]{2,1,0:T(8,128)(2,1)}, bf16[8,128,512]{2,1,0:T(8,128)(2,1)}, u32[]{:S(2)}, u32[]{:S(2)}) %collective-permute-start.6) | collective-permute-done | bytes 1048608 | tf_op jit(solution)/shard_map/ppermute | solution.py:527
  57.8 1.5 collective-permute-done.7.rest_5_
  59.3 18.9 %gradients.1 = (f32[72,1,128]{2,1,0:T(1,128)}, f32[8,1,128]{2,1,0:T(1,128)}, f32[1032,128]{1,0:T(8,128)}, f32[1032,128]{1,0:T(8,128)}) custom-call(s32[8]{0:T(128)} %fusion.19.place, s32[8,16]{1,0:T(8,128)} %get-tuple-element.111.slots, f32[8,128,2048]{2,1,0:T(8,128)} %get-tuple-element.55.dense_ref, bf16[1024,512]{1,0:T(8,128)(2,1)} %grad_ref.3, ...), custom_call_target="tpu_custom_call" | custom-call | tf_op jit(solution)/shard_map/gradients/pallas_call | solution.py:284
  78.2 0.0 collective-permute-done.9
  78.2 0.4 collective-permute-start.10
  78.6 3.5 %add_convert_fusion = (bf16[8,512,128]{2,1,0:T(8,128)(2,1)S(1)}, bf16[8,512,128]{2,1,0:T(8,128)(2,1)S(1)}) fusion(f32[24,512,128]{2,1,0:T(8,128)} %get-tuple-element.79.own_ref, bf16[16,512,128]{2,1,0:T(8,128)(2,1)S(1)} %collective-permute-done.8, bf16[16,512,128]{2,1,0:T(8,128)(2,1)} %collective-permute-done.9), kind=kLoop, calls=%fused_computation.3 | loop fusion | flops 5242880 | bytes 10485760 | tf_op jit(solution)/shard_map/convert_element_type | solution.py:552
  82.2 0.1 add.184
  82.3 0.2 collective-permute-start.14
  82.5 1.2 collective-permute-start.15
  83.8 0.8 collective-permute-start.11
  84.7 1.7 %collective-permute-start.13 = (bf16[288,128]{1,0:T(8,128)(2,1)S(1)}, bf16[288,128]{1,0:T(8,128)(2,1)S(1)}, u32[]{:S(2)}, u32[]{:S(2)}) collective-permute-start(bf16[288,128]{1,0:T(8,128)(2,1)S(1)} %constant_dynamic-update-slice_fusion.8), channel_id=1, source_target_pairs={{0,3},{1,0},{2,1},{3,2},{4,7},{5,4},{6,5},{7,6},{8,11},{9,8},{10,9... | collective-permute-start | bytes 221192 | tf_op jit(solution)/shard_map/ppermute | solution.py:470
  86.4 0.5 collective-permute-start.12
  86.9 0.0 collective-permute-done.15
  86.9 1.7 %collective-permute-done.11 = bf16[288,128]{1,0:T(8,128)(2,1)S(1)} collective-permute-done((bf16[288,128]{1,0:T(8,128)(2,1)S(1)}, bf16[288,128]{1,0:T(8,128)(2,1)S(1)}, u32[]{:S(2)}, u32[]{:S(2)}) %collective-permute-start.11) | collective-permute-done | bytes 73760 | tf_op jit(solution)/shard_map/ppermute | solution.py:470
  88.6 0.7 collective-permute-done.13
  89.4 2.3 %collective-permute-done.12 = bf16[288,128]{1,0:T(8,128)(2,1)S(1)} collective-permute-done((bf16[288,128]{1,0:T(8,128)(2,1)S(1)}, bf16[288,128]{1,0:T(8,128)(2,1)S(1)}, u32[]{:S(2)}, u32[]{:S(2)}) %collective-permute-start.12) | collective-permute-done | bytes 73760 | tf_op jit(solution)/shard_map/ppermute | solution.py:470
  91.8 1.7 %collective-permute-start.18 = (f32[264,128]{1,0:T(8,128)S(1)}, f32[264,128]{1,0:T(8,128)S(1)}, u32[]{:S(2)}, u32[]{:S(2)}) collective-permute-start(f32[264,128]{1,0:T(8,128)S(1)} %pad_maximum_fusion.1), channel_id=1, source_target_pairs={{0,96},{16,112},{32,0},{48,16},{64,32},{80,48},{96,64},{112,80},{1... | collective-permute-start | bytes 405512 | tf_op jit(solution)/shard_map/ppermute | solution.py:435
  93.5 2.8 %collective-permute-start.16 = (f32[264,128]{1,0:T(8,128)S(1)}, f32[264,128]{1,0:T(8,128)S(1)}, u32[]{:S(2)}, u32[]{:S(2)}) collective-permute-start(f32[264,128]{1,0:T(8,128)S(1)} %pad_maximum_fusion.1), channel_id=1, source_target_pairs={{0,64},{16,80},{32,96},{48,112},{64,0},{80,16},{96,32},{112,48},{1... | collective-permute-start | bytes 405512 | tf_op jit(solution)/shard_map/ppermute | solution.py:435
  96.3 0.0 copy-start.10
  96.3 0.0 copy-start.9
  96.3 0.1 fusion.2
  96.4 0.1 collective-permute-start.19
  96.5 0.1 fusion.3
  96.6 4.8 %collective-permute-start.20 = (bf16[8,528,128]{2,1,0:T(8,128)(2,1)S(1)}, bf16[8,528,128]{2,1,0:T(8,128)(2,1)S(1)}, u32[]{:S(2)}, u32[]{:S(2)}) collective-permute-start(bf16[8,528,128]{2,1,0:T(8,128)(2,1)S(1)} %fusion.3), channel_id=1, source_target_pairs={{0,15},{1,0},{2,1},{3,2},{4,3},{5,4},{6,5},{7,6},{8,7},{9,8},{10,9... | collective-permute-start | bytes 3244040 | tf_op jit(solution)/shard_map/ppermute | solution.py:558
  101.4 0.0 collective-permute-done.18
  101.4 0.0 collective-permute-done.17
  101.4 0.2 collective-permute-done.16
  101.7 3.3 %collective-permute-start.21 = (bf16[8,512,128]{2,1,0:T(8,128)(2,1)S(1)}, bf16[8,512,128]{2,1,0:T(8,128)(2,1)S(1)}, u32[]{:S(2)}, u32[]{:S(2)}) collective-permute-start(bf16[8,512,128]{2,1,0:T(8,128)(2,1)S(1)} %copy-done.10), channel_id=1, source_target_pairs={{0,112},{16,32},{32,16},{48,64},{64,48},{80,96},{96,80},{112,0},{1... | collective-permute-start | bytes 3145736 | tf_op jit(solution)/shard_map/ppermute | solution.py:561
  105.0 19.1 %collective-permute-done.19.below_ref = bf16[8,528,128]{2,1,0:T(8,128)(2,1)S(1)} collective-permute-done((bf16[8,528,128]{2,1,0:T(8,128)(2,1)S(1)}, bf16[8,528,128]{2,1,0:T(8,128)(2,1)S(1)}, u32[]{:S(2)}, u32[]{:S(2)}) %collective-permute-start.19) | collective-permute-done | bytes 1081376 | tf_op jit(solution)/shard_map/ppermute | solution.py:557
  124.1 0.0 collective-permute-done.20.above_ref
  124.1 0.0 collective-permute-done.21.far_ref
  124.1 0.0 copy-start.11
  124.1 0.0 collective-permute-done.22.twin_ref
  124.2 1.9 %collective-permute-start.25 = (bf16[288,128]{1,0:T(8,128)(2,1)S(1)}, bf16[288,128]{1,0:T(8,128)(2,1)S(1)}, u32[]{:S(2)}, u32[]{:S(2)}) collective-permute-start(bf16[288,128]{1,0:T(8,128)(2,1)S(1)} %constant_dynamic-update-slice_fusion.12), channel_id=1, source_target_pairs={{0,12},{1,13},{2,14},{3,15},{4,0},{5,1},{6,2},{7,3},{8,4},{9,5},{1... | collective-permute-start | bytes 221192 | tf_op jit(solution)/shard_map/ppermute | solution.py:435
  126.0 1.3 collective-permute-start.23
  127.3 0.6 slice.157
  127.9 0.0 collective-permute-done.25
  127.9 3.3 %collective-permute-done.24 = bf16[288,128]{1,0:T(8,128)(2,1)S(1)} collective-permute-done((bf16[288,128]{1,0:T(8,128)(2,1)S(1)}, bf16[288,128]{1,0:T(8,128)(2,1)S(1)}, u32[]{:S(2)}, u32[]{:S(2)}) %collective-permute-start.24) | collective-permute-done | bytes 73760 | tf_op jit(solution)/shard_map/ppermute | solution.py:435
  131.3 3.2 %collective-permute-start.28 = (bf16[1,256,128]{2,1,0:T(8,128)(2,1)S(1)}, bf16[1,256,128]{2,1,0:T(8,128)(2,1)S(1)}, u32[]{:S(2)}, u32[]{:S(2)}) collective-permute-start(bf16[1,256,128]{2,1,0:T(8,128)(2,1)S(1)} %bitcast.45), channel_id=1, source_target_pairs={{0,3},{1,0},{2,1},{3,2},{4,7},{5,4},{6,5},{7,6},{8,11},{9,8},{10,9... | collective-permute-start | bytes 196616 | tf_op jit(solution)/shard_map/ppermute | solution.py:435
  134.5 0.0 collective-permute-start.27
  134.5 0.7 collective-permute-start.26
  135.2 5.1 %finish_features.1 = bf16[1024,512]{1,0:T(8,128)(2,1)} custom-call(f32[24,512,128]{2,1,0:T(8,128)} %get-tuple-element.79.own_ref, bf16[8,512,128]{2,1,0:T(8,128)(2,1)} %collective-permute-done.22.twin_ref, bf16[8,512,128]{2,1,0:T(8,128)(2,1)} %copy-done.11, bf16[8,528,128]{2,1,0:T(8,128)(2,1)} %copy-done.8, bf16[8,528,128]{2,1,0:T(8,128)(2,1)} %copy-done.7, ...), custom_call_target="tpu_custom_call" | custom-call | flops 6000000000 | bytes 1048576 | tf_op jit(solution)/shard_map/finish_features/pallas_call | solution.py:409
  140.4 4.4 %collective-permute-start.29 = (bf16[4,256,128]{2,1,0:T(8,128)(2,1)S(1)}, bf16[4,256,128]{2,1,0:T(8,128)(2,1)S(1)}, u32[]{:S(2)}, u32[]{:S(2)}) collective-permute-start(bf16[4,256,128]{2,1,0:T(8,128)(2,1)S(1)} %pad_maximum_fusion.near_ref), channel_id=1, source_target_pairs={{0,16},{16,0},{32,48},{48,32},{64,80},{80,64},{96,112},{112,96},{1... | collective-permute-start | bytes 786440 | tf_op jit(solution)/shard_map/ppermute | solution.py:579
  144.8 0.5 fusion.20.place
  145.4 0.6 slice_add_fusion.2.vec_ref
  146.0 0.0 collective-permute-done.29.away_ref
  146.0 0.7 copy-done.5
  146.7 3.4 %finish_weight.1 = (f32[512,512]{1,0:T(8,128)}, f32[512]{0:T(512)}, f32[512]{0:T(512)}) custom-call(s32[8]{0:T(128)} %fusion.20.place, bf16[4,256,128]{2,1,0:T(8,128)(2,1)} %copy-done.3, bf16[4,256,128]{2,1,0:T(8,128)(2,1)} %copy-done.5, f32[8,128]{1,0:T(8,128)} %slice_add_fusion.2.vec_ref, f32[1,512]{1,0:T(1,128)} %bitcast.53, f32[1,512]{1,0:T(1,128)} %bitcast.55, ...), custom_call_target="tpu_custom_call" | custom-call | tf_op jit(solution)/shard_map/finish_weight/pallas_call | solution.py:359
  (63 shorter events, 0.5 us)
Async XLA Ops:
  0.6 41.6 %collective-permute-start.2 = (bf16[8,128,512]{2,1,0:T(8,128)(2,1)}, bf16[8,128,512]{2,1,0:T(8,128)(2,1)S(1)}, u32[]{:S(2)}, u32[]{:S(2)}) collective-permute-start(bf16[8,128,512]{2,1,0:T(8,128)(2,1)} %bitcast.36), channel_id=1, source_target_pairs={{0,113},{1,114},{2,115},{3,116},{4,117},{5,118},{6,119},{7,120},{8... | collective-permute-start | bytes 3145736 | tf_op jit(solution)/shard_map/ppermute | solution.py:518
  4.7 37.5 %collective-permute-start.1 = (bf16[8,128,512]{2,1,0:T(8,128)(2,1)}, bf16[8,128,512]{2,1,0:T(8,128)(2,1)S(1)}, u32[]{:S(2)}, u32[]{:S(2)}) collective-permute-start(bf16[8,128,512]{2,1,0:T(8,128)(2,1)} %bitcast.37), channel_id=1, source_target_pairs={{0,127},{1,112},{2,113},{3,114},{4,115},{5,116},{6,117},{7,118},{8... | collective-permute-start | bytes 3145736 | tf_op jit(solution)/shard_map/ppermute | solution.py:518
  8.5 35.0 %collective-permute-start = (bf16[8,128,512]{2,1,0:T(8,128)(2,1)}, bf16[8,128,512]{2,1,0:T(8,128)(2,1)S(1)}, u32[]{:S(2)}, u32[]{:S(2)}) collective-permute-start(bf16[8,128,512]{2,1,0:T(8,128)(2,1)} %bitcast.38), channel_id=1, source_target_pairs={{0,112},{16,32},{32,16},{48,64},{64,48},{80,96},{96,80},{112,0},{1... | collective-permute-start | bytes 3145736 | tf_op jit(solution)/shard_map/ppermute | solution.py:517
  9.7 42.8 %collective-permute-start.4 = (bf16[8,128,512]{2,1,0:T(8,128)(2,1)}, bf16[8,128,512]{2,1,0:T(8,128)(2,1)}, u32[]{:S(2)}, u32[]{:S(2)}) collective-permute-start(bf16[8,128,512]{2,1,0:T(8,128)(2,1)} %bitcast.39), channel_id=1, source_target_pairs={{0,1},{1,2},{2,3},{3,4},{4,5},{5,6},{6,7},{7,8},{8,9},{9,10},{10,1... | collective-permute-start | bytes 3145736 | tf_op jit(solution)/shard_map/ppermute | solution.py:516
  9.7 42.8 %collective-permute-start.3 = (bf16[8,128,512]{2,1,0:T(8,128)(2,1)}, bf16[8,128,512]{2,1,0:T(8,128)(2,1)}, u32[]{:S(2)}, u32[]{:S(2)}) collective-permute-start(bf16[8,128,512]{2,1,0:T(8,128)(2,1)} %bitcast.40), channel_id=1, source_target_pairs={{0,15},{1,0},{2,1},{3,2},{4,3},{5,4},{6,5},{7,6},{8,7},{9,8},{10,9... | collective-permute-start | bytes 3145736 | tf_op jit(solution)/shard_map/ppermute | solution.py:515
  42.2 17.1 %copy-start = (bf16[8,128,512]{2,1,0:T(8,128)(2,1)}, bf16[8,128,512]{2,1,0:T(8,128)(2,1)S(1)}, u32[]{:S(2)}) copy-start(bf16[8,128,512]{2,1,0:T(8,128)(2,1)S(1)} %collective-permute-done.2.rest_8_) | copy-start | bytes 3145732
  42.2 1.2 copy-start.1
  43.4 1.0 copy-start.2
  44.4 8.1 %collective-permute-start.5 = (bf16[8,128,512]{2,1,0:T(8,128)(2,1)}, bf16[8,128,512]{2,1,0:T(8,128)(2,1)}, u32[]{:S(2)}, u32[]{:S(2)}) collective-permute-start(bf16[8,128,512]{2,1,0:T(8,128)(2,1)} %bitcast.41), channel_id=1, source_target_pairs={{0,16},{16,0},{32,48},{48,32},{64,80},{80,64},{96,112},{112,96},{1... | collective-permute-start | bytes 3145736 | tf_op jit(solution)/shard_map/ppermute | solution.py:525
  47.3 30.8 %collective-permute-start.8 = (bf16[16,512,128]{2,1,0:T(8,128)(2,1)}, bf16[16,512,128]{2,1,0:T(8,128)(2,1)S(1)}, u32[]{:S(2)}, u32[]{:S(2)}) collective-permute-start(bf16[16,512,128]{2,1,0:T(8,128)(2,1)} %get-tuple-element.68), channel_id=1, source_target_pairs={{0,112},{16,32},{32,16},{48,64},{64,48},{80,96},{96,80},{112,0},{1... | collective-permute-start | bytes 6291464 | tf_op jit(solution)/shard_map/ppermute | solution.py:528
  47.3 30.8 %collective-permute-start.9 = (bf16[16,512,128]{2,1,0:T(8,128)(2,1)}, bf16[16,512,128]{2,1,0:T(8,128)(2,1)}, u32[]{:S(2)}, u32[]{:S(2)}) collective-permute-start(bf16[16,512,128]{2,1,0:T(8,128)(2,1)} %get-tuple-element.69), channel_id=1, source_target_pairs={{0,16},{16,0},{32,48},{48,32},{64,80},{80,64},{96,112},{112,96},{1... | collective-permute-start | bytes 6291464 | tf_op jit(solution)/shard_map/ppermute | solution.py:529
  52.5 5.2 %collective-permute-start.6 = (bf16[8,128,512]{2,1,0:T(8,128)(2,1)}, bf16[8,128,512]{2,1,0:T(8,128)(2,1)}, u32[]{:S(2)}, u32[]{:S(2)}) collective-permute-start(bf16[8,128,512]{2,1,0:T(8,128)(2,1)} %collective-permute-done.3.rest_1_), channel_id=1, source_target_pairs={{0,16},{16,0},{32,48},{48,32},{64,80},{80,64},{96,112},{112,96},{1... | collective-permute-start | bytes 3145736 | tf_op jit(solution)/shard_map/ppermute | solution.py:527
  55.1 4.1 %collective-permute-start.7 = (bf16[8,128,512]{2,1,0:T(8,128)(2,1)}, bf16[8,128,512]{2,1,0:T(8,128)(2,1)}, u32[]{:S(2)}, u32[]{:S(2)}) collective-permute-start(bf16[8,128,512]{2,1,0:T(8,128)(2,1)} %collective-permute-done.4.rest_2_), channel_id=1, source_target_pairs={{0,16},{16,0},{32,48},{48,32},{64,80},{80,64},{96,112},{112,96},{1... | collective-permute-start | bytes 3145736 | tf_op jit(solution)/shard_map/ppermute | solution.py:527
  78.2 4.0 %copy-start.4 = (f32[1032,128]{1,0:T(8,128)S(1)}, f32[1032,128]{1,0:T(8,128)}, u32[]{:S(2)}) copy-start(f32[1032,128]{1,0:T(8,128)} %get-tuple-element.70) | copy-start | bytes 1585156
  78.2 4.1 %copy-start.6 = (f32[72,1,128]{2,1,0:T(1,128)S(1)}, f32[72,1,128]{2,1,0:T(1,128)}, u32[]{:S(2)}) copy-start(f32[72,1,128]{2,1,0:T(1,128)} %get-tuple-element.72) | copy-start | bytes 110596
  78.2 4.0 %collective-permute-start.10 = (f32[1032,128]{1,0:T(8,128)}, f32[1032,128]{1,0:T(8,128)S(1)}, u32[]{:S(2)}, u32[]{:S(2)}) collective-permute-start(f32[1032,128]{1,0:T(8,128)} %get-tuple-element.71), channel_id=1, source_target_pairs={{0,16},{16,0},{32,48},{48,32},{64,80},{80,64},{96,112},{112,96},{1... | collective-permute-start | bytes 1585160 | tf_op jit(solution)/shard_map/ppermute | solution.py:542
  82.3 4.6 %collective-permute-start.14 = (f32[3,8,1,128]{3,1,0,2:T(8,128)S(1)}, f32[3,8,1,128]{3,1,0,2:T(8,128)S(1)}, u32[]{:S(2)}, u32[]{:S(2)}) collective-permute-start(f32[3,8,1,128]{3,1,0,2:T(8,128)S(1)} %get-tuple-element.117), channel_id=1, source_target_pairs={{0,16},{16,0},{32,48},{48,32},{64,80},{80,64},{96,112},{112,96},{1... | collective-permute-start | bytes 36872 | tf_op jit(solution)/shard_map/ppermute | solution.py:545
  82.5 4.4 %collective-permute-start.15 = (f32[3,8,1,128]{3,1,2,0:T(8,128)S(1)}, f32[3,8,1,128]{3,1,2,0:T(8,128)S(1)}, u32[]{:S(2)}, u32[]{:S(2)}) collective-permute-start(f32[3,8,1,128]{3,1,2,0:T(8,128)S(1)} %get-tuple-element.118), channel_id=1, source_target_pairs={{0,112},{16,32},{32,16},{48,64},{64,48},{80,96},{96,80},{112,0},{1... | collective-permute-start | bytes 36872 | tf_op jit(solution)/shard_map/ppermute | solution.py:545
  83.8 4.8 %collective-permute-start.11 = (bf16[288,128]{1,0:T(8,128)(2,1)S(1)}, bf16[288,128]{1,0:T(8,128)(2,1)S(1)}, u32[]{:S(2)}, u32[]{:S(2)}) collective-permute-start(bf16[288,128]{1,0:T(8,128)(2,1)S(1)} %constant_dynamic-update-slice_fusion), channel_id=1, source_target_pairs={{0,2},{1,3},{2,0},{3,1},{4,6},{5,7},{6,4},{7,5},{8,10},{9,11},{10,... | collective-permute-start | bytes 221192 | tf_op jit(solution)/shard_map/ppermute | solution.py:470
  84.7 4.7 %collective-permute-start.13 = (bf16[288,128]{1,0:T(8,128)(2,1)S(1)}, bf16[288,128]{1,0:T(8,128)(2,1)S(1)}, u32[]{:S(2)}, u32[]{:S(2)}) collective-permute-start(bf16[288,128]{1,0:T(8,128)(2,1)S(1)} %constant_dynamic-update-slice_fusion.8), channel_id=1, source_target_pairs={{0,3},{1,0},{2,1},{3,2},{4,7},{5,4},{6,5},{7,6},{8,11},{9,8},{10,9... | collective-permute-start | bytes 221192 | tf_op jit(solution)/shard_map/ppermute | solution.py:470
  86.4 5.3 %collective-permute-start.12 = (bf16[288,128]{1,0:T(8,128)(2,1)S(1)}, bf16[288,128]{1,0:T(8,128)(2,1)S(1)}, u32[]{:S(2)}, u32[]{:S(2)}) collective-permute-start(bf16[288,128]{1,0:T(8,128)(2,1)S(1)} %constant_dynamic-update-slice_fusion.4), channel_id=1, source_target_pairs={{0,1},{1,2},{2,3},{3,0},{4,5},{5,6},{6,7},{7,4},{8,9},{9,10},{10,1... | collective-permute-start | bytes 221192 | tf_op jit(solution)/shard_map/ppermute | solution.py:470
  91.8 9.7 %collective-permute-start.18 = (f32[264,128]{1,0:T(8,128)S(1)}, f32[264,128]{1,0:T(8,128)S(1)}, u32[]{:S(2)}, u32[]{:S(2)}) collective-permute-start(f32[264,128]{1,0:T(8,128)S(1)} %pad_maximum_fusion.1), channel_id=1, source_target_pairs={{0,96},{16,112},{32,0},{48,16},{64,32},{80,48},{96,64},{112,80},{1... | collective-permute-start | bytes 405512 | tf_op jit(solution)/shard_map/ppermute | solution.py:435
  93.5 7.9 %collective-permute-start.17 = (f32[264,128]{1,0:T(8,128)S(1)}, f32[264,128]{1,0:T(8,128)S(1)}, u32[]{:S(2)}, u32[]{:S(2)}) collective-permute-start(f32[264,128]{1,0:T(8,128)S(1)} %pad_maximum_fusion.1), channel_id=1, source_target_pairs={{0,32},{16,48},{32,64},{48,80},{64,96},{80,112},{96,0},{112,16},{1... | collective-permute-start | bytes 405512 | tf_op jit(solution)/shard_map/ppermute | solution.py:435
  93.5 8.2 %collective-permute-start.16 = (f32[264,128]{1,0:T(8,128)S(1)}, f32[264,128]{1,0:T(8,128)S(1)}, u32[]{:S(2)}, u32[]{:S(2)}) collective-permute-start(f32[264,128]{1,0:T(8,128)S(1)} %pad_maximum_fusion.1), channel_id=1, source_target_pairs={{0,64},{16,80},{32,96},{48,112},{64,0},{80,16},{96,32},{112,48},{1... | collective-permute-start | bytes 405512 | tf_op jit(solution)/shard_map/ppermute | solution.py:435
  96.3 5.4 %copy-start.10 = (bf16[8,512,128]{2,1,0:T(8,128)(2,1)S(1)}, bf16[8,512,128]{2,1,0:T(8,128)(2,1)}, u32[]{:S(2)}) copy-start(bf16[8,512,128]{2,1,0:T(8,128)(2,1)} %get-tuple-element.83) | copy-start | bytes 3145732
  96.3 8.7 %copy-start.9 = (bf16[8,512,128]{2,1,0:T(8,128)(2,1)S(1)}, bf16[8,512,128]{2,1,0:T(8,128)(2,1)}, u32[]{:S(2)}) copy-start(bf16[8,512,128]{2,1,0:T(8,128)(2,1)} %get-tuple-element.84) | copy-start | bytes 3145732
  96.4 27.7 %collective-permute-start.19 = (bf16[8,528,128]{2,1,0:T(8,128)(2,1)S(1)}, bf16[8,528,128]{2,1,0:T(8,128)(2,1)S(1)}, u32[]{:S(2)}, u32[]{:S(2)}) collective-permute-start(bf16[8,528,128]{2,1,0:T(8,128)(2,1)S(1)} %fusion.2), channel_id=1, source_target_pairs={{0,1},{1,2},{2,3},{3,4},{4,5},{5,6},{6,7},{7,8},{8,9},{9,10},{10,1... | collective-permute-start | bytes 3244040 | tf_op jit(solution)/shard_map/ppermute | solution.py:557
  96.6 27.5 %collective-permute-start.20 = (bf16[8,528,128]{2,1,0:T(8,128)(2,1)S(1)}, bf16[8,528,128]{2,1,0:T(8,128)(2,1)S(1)}, u32[]{:S(2)}, u32[]{:S(2)}) collective-permute-start(bf16[8,528,128]{2,1,0:T(8,128)(2,1)S(1)} %fusion.3), channel_id=1, source_target_pairs={{0,15},{1,0},{2,1},{3,2},{4,3},{5,4},{6,5},{7,6},{8,7},{9,8},{10,9... | collective-permute-start | bytes 3244040 | tf_op jit(solution)/shard_map/ppermute | solution.py:558
  101.7 22.4 %collective-permute-start.21 = (bf16[8,512,128]{2,1,0:T(8,128)(2,1)S(1)}, bf16[8,512,128]{2,1,0:T(8,128)(2,1)S(1)}, u32[]{:S(2)}, u32[]{:S(2)}) collective-permute-start(bf16[8,512,128]{2,1,0:T(8,128)(2,1)S(1)} %copy-done.10), channel_id=1, source_target_pairs={{0,112},{16,32},{32,16},{48,64},{64,48},{80,96},{96,80},{112,0},{1... | collective-permute-start | bytes 3145736 | tf_op jit(solution)/shard_map/ppermute | solution.py:561
  105.0 19.1 %collective-permute-start.22 = (bf16[8,512,128]{2,1,0:T(8,128)(2,1)S(1)}, bf16[8,512,128]{2,1,0:T(8,128)(2,1)}, u32[]{:S(2)}, u32[]{:S(2)}) collective-permute-start(bf16[8,512,128]{2,1,0:T(8,128)(2,1)S(1)} %copy-done.9), channel_id=1, source_target_pairs={{0,16},{16,0},{32,48},{48,32},{64,80},{80,64},{96,112},{112,96},{1... | collective-permute-start | bytes 3145736 | tf_op jit(solution)/shard_map/ppermute | solution.py:562
  124.1 11.1 %copy-start.7 = (bf16[8,528,128]{2,1,0:T(8,128)(2,1)}, bf16[8,528,128]{2,1,0:T(8,128)(2,1)S(1)}, u32[]{:S(2)}) copy-start(bf16[8,528,128]{2,1,0:T(8,128)(2,1)S(1)} %collective-permute-done.19.below_ref) | copy-start | bytes 3244036
  124.1 11.1 %copy-start.8 = (bf16[8,528,128]{2,1,0:T(8,128)(2,1)}, bf16[8,528,128]{2,1,0:T(8,128)(2,1)S(1)}, u32[]{:S(2)}) copy-start(bf16[8,528,128]{2,1,0:T(8,128)(2,1)S(1)} %collective-permute-done.20.above_ref) | copy-start | bytes 3244036
  124.1 11.1 %copy-start.11 = (bf16[8,512,128]{2,1,0:T(8,128)(2,1)}, bf16[8,512,128]{2,1,0:T(8,128)(2,1)S(1)}, u32[]{:S(2)}) copy-start(bf16[8,512,128]{2,1,0:T(8,128)(2,1)S(1)} %collective-permute-done.21.far_ref) | copy-start | bytes 3145732
  124.2 3.7 %collective-permute-start.25 = (bf16[288,128]{1,0:T(8,128)(2,1)S(1)}, bf16[288,128]{1,0:T(8,128)(2,1)S(1)}, u32[]{:S(2)}, u32[]{:S(2)}) collective-permute-start(bf16[288,128]{1,0:T(8,128)(2,1)S(1)} %constant_dynamic-update-slice_fusion.12), channel_id=1, source_target_pairs={{0,12},{1,13},{2,14},{3,15},{4,0},{5,1},{6,2},{7,3},{8,4},{9,5},{1... | collective-permute-start | bytes 221192 | tf_op jit(solution)/shard_map/ppermute | solution.py:435
  126.0 5.2 %collective-permute-start.24 = (bf16[288,128]{1,0:T(8,128)(2,1)S(1)}, bf16[288,128]{1,0:T(8,128)(2,1)S(1)}, u32[]{:S(2)}, u32[]{:S(2)}) collective-permute-start(bf16[288,128]{1,0:T(8,128)(2,1)S(1)} %constant_dynamic-update-slice_fusion.12), channel_id=1, source_target_pairs={{0,4},{1,5},{2,6},{3,7},{4,8},{5,9},{6,10},{7,11},{8,12},{9,13},{1... | collective-permute-start | bytes 221192 | tf_op jit(solution)/shard_map/ppermute | solution.py:435
  126.0 5.2 %collective-permute-start.23 = (bf16[288,128]{1,0:T(8,128)(2,1)S(1)}, bf16[288,128]{1,0:T(8,128)(2,1)S(1)}, u32[]{:S(2)}, u32[]{:S(2)}) collective-permute-start(bf16[288,128]{1,0:T(8,128)(2,1)S(1)} %constant_dynamic-update-slice_fusion.12), channel_id=1, source_target_pairs={{0,8},{1,9},{2,10},{3,11},{4,12},{5,13},{6,14},{7,15},{8,0},{9,1},... | collective-permute-start | bytes 221192 | tf_op jit(solution)/shard_map/ppermute | solution.py:435
  131.3 9.0 %collective-permute-start.28 = (bf16[1,256,128]{2,1,0:T(8,128)(2,1)S(1)}, bf16[1,256,128]{2,1,0:T(8,128)(2,1)S(1)}, u32[]{:S(2)}, u32[]{:S(2)}) collective-permute-start(bf16[1,256,128]{2,1,0:T(8,128)(2,1)S(1)} %bitcast.45), channel_id=1, source_target_pairs={{0,3},{1,0},{2,1},{3,2},{4,7},{5,4},{6,5},{7,6},{8,11},{9,8},{10,9... | collective-permute-start | bytes 196616 | tf_op jit(solution)/shard_map/ppermute | solution.py:435
  134.5 5.8 %collective-permute-start.27 = (bf16[1,256,128]{2,1,0:T(8,128)(2,1)S(1)}, bf16[1,256,128]{2,1,0:T(8,128)(2,1)S(1)}, u32[]{:S(2)}, u32[]{:S(2)}) collective-permute-start(bf16[1,256,128]{2,1,0:T(8,128)(2,1)S(1)} %bitcast.46), channel_id=1, source_target_pairs={{0,2},{1,3},{2,0},{3,1},{4,6},{5,7},{6,4},{7,5},{8,10},{9,11},{10,... | collective-permute-start | bytes 196616 | tf_op jit(solution)/shard_map/ppermute | solution.py:435
  134.5 5.8 %collective-permute-start.26 = (bf16[1,256,128]{2,1,0:T(8,128)(2,1)S(1)}, bf16[1,256,128]{2,1,0:T(8,128)(2,1)S(1)}, u32[]{:S(2)}, u32[]{:S(2)}) collective-permute-start(bf16[1,256,128]{2,1,0:T(8,128)(2,1)S(1)} %bitcast.47), channel_id=1, source_target_pairs={{0,1},{1,2},{2,3},{3,0},{4,5},{5,6},{6,7},{7,4},{8,9},{9,10},{10,1... | collective-permute-start | bytes 196616 | tf_op jit(solution)/shard_map/ppermute | solution.py:435
  140.4 5.6 %copy-start.3 = (bf16[4,256,128]{2,1,0:T(8,128)(2,1)}, bf16[4,256,128]{2,1,0:T(8,128)(2,1)S(1)}, u32[]{:S(2)}) copy-start(bf16[4,256,128]{2,1,0:T(8,128)(2,1)S(1)} %pad_maximum_fusion.near_ref) | copy-start | bytes 786436
  140.4 5.6 %collective-permute-start.29 = (bf16[4,256,128]{2,1,0:T(8,128)(2,1)S(1)}, bf16[4,256,128]{2,1,0:T(8,128)(2,1)S(1)}, u32[]{:S(2)}, u32[]{:S(2)}) collective-permute-start(bf16[4,256,128]{2,1,0:T(8,128)(2,1)S(1)} %pad_maximum_fusion.near_ref), channel_id=1, source_target_pairs={{0,16},{16,0},{32,48},{48,32},{64,80},{80,64},{96,112},{112,96},{1... | collective-permute-start | bytes 786440 | tf_op jit(solution)/shard_map/ppermute | solution.py:579
  146.0 0.7 copy-start.5

commit v6 on v5

--- a/solution.py
+++ b/solution.py
@@ -371,7 +371,7 @@
             jax.ShapeDtypeStruct((width,), f32),
         ],
         compiler_params=pltpu.CompilerParams(
-            dimension_semantics=("arbitrary",), vmem_limit_bytes=60 * MIB
+            dimension_semantics=("arbitrary",), vmem_limit_bytes=20 * MIB
         ),
         name="finish_weight",
     )(place, *args)
@@ -415,7 +415,7 @@
         scratch_shapes=[pltpu.VMEM((width, BLK), f32)] * 2,
         out_shape=jax.ShapeDtypeStruct((blocks * BLK, depth), bf16),
         compiler_params=pltpu.CompilerParams(
-            dimension_semantics=("arbitrary",), vmem_limit_bytes=60 * MIB
+            dimension_semantics=("arbitrary",), vmem_limit_bytes=20 * MIB
         ),
         cost_estimate=pl.CostEstimate(
             flops=6 * 10**9, bytes_accessed=MIB, transcendentals=0

time: 150 us -> 149 us (level)
  waiting for transfers between devices: 36.3 us -> 40.3 us
  Pallas kernels: 53.8 us -> 50.4 us
  local copies, waits for them, and re-layouts: 2.41 us -> 0.18 us
    pallas_call x1, Pallas kernels: 5.15 us -> 2.94 us  [finish_features(): pl.pallas_call(finish_features_body, grid=(blocks // group,), in_specs=[t...]
    ppermute x9, waiting for transfers between devices: 3.61 us -> 5.53 us  [turned(): lax.ppermute(array, axis, ring(axis, low, count, k))]
    unnamed x31, local copies, waits for them, and re-layouts: 1.78 us -> 0.13 us
  transfers between devices with their start and end apart: 30 -> 30, of which waited for: 10 -> 14; matrix products, arithmetic and copies ran while one was open for 5% -> 4% of each run, Pallas kernels for 34% -> 32%
where the time goes in v6:
time: 149 us
  starting transfers between devices  50.4 us (34%)
  Pallas kernels  50.4 us (34%)
  waiting for transfers between devices  40.3 us (27%)
  other arithmetic  6.66 us (4%)
    pallas_call x1, Pallas kernels, spread(): pl.pallas_call(functools.partial(spread_body, edges), grid_spec=pltpu.Pre...  26.4 us
    ppermute x1, waiting for transfers between devices, on_device(): from_below = lax.ppermute(to_above, 'gy', up)  19.1 us
    pallas_call x1, Pallas kernels, gradients(): pl.pallas_call(functools.partial(gradients_body, pieces), grid_spec=pltpu...  19 us
    ppermute x9, starting transfers between devices, turned(): lax.ppermute(array, axis, ring(axis, low, count, k))  11.5 us
    ppermute x2, starting transfers between devices, on_device(): lax.ppermute(own, ('gx', 'gy'), crossed(far, way, size_y))  7.82 us
    ppermute x9, waiting for transfers between devices, turned(): lax.ppermute(array, axis, ring(axis, low, count, k))  5.53 us
    ppermute x1, starting transfers between devices, on_device(): lax.ppermute(part, 'gx', twin)  5.23 us
    ppermute x1, waiting for transfers between devices, on_device(): below = lax.ppermute(own, 'gy', up)  5.01 us
  transfers between devices with their start and end apart: 30, of which 14 were waited for; matrix products, arithmetic and copies ran while one was open for 4% of the time, Pallas kernels for 32%

profile of v6, /device:TPU:1, one launch (start us, length us, event | category | flops | bytes accessed | tf_op | source)
XLA Modules:
  0.0 149.0 jit_solution(11247229997033244245)
XLA Ops:
  0.6 4.1 %collective-permute-start.2 = (bf16[8,128,512]{2,1,0:T(8,128)(2,1)}, bf16[8,128,512]{2,1,0:T(8,128)(2,1)S(1)}, u32[]{:S(2)}, u32[]{:S(2)}) collective-permute-start(bf16[8,128,512]{2,1,0:T(8,128)(2,1)} %bitcast.43), channel_id=1, source_target_pairs={{0,113},{1,114},{2,115},{3,116},{4,117},{5,118},{6,119},{7,120},{8... | collective-permute-start | bytes 3145736 | tf_op jit(solution)/shard_map/ppermute | solution.py:518
  4.7 3.7 %collective-permute-start.1 = (bf16[8,128,512]{2,1,0:T(8,128)(2,1)}, bf16[8,128,512]{2,1,0:T(8,128)(2,1)S(1)}, u32[]{:S(2)}, u32[]{:S(2)}) collective-permute-start(bf16[8,128,512]{2,1,0:T(8,128)(2,1)} %bitcast.44), channel_id=1, source_target_pairs={{0,127},{1,112},{2,113},{3,114},{4,115},{5,116},{6,117},{7,118},{8... | collective-permute-start | bytes 3145736 | tf_op jit(solution)/shard_map/ppermute | solution.py:518
  8.5 1.2 collective-permute-start
  9.7 0.0 collective-permute-start.4
  9.7 4.8 %collective-permute-start.3 = (bf16[8,128,512]{2,1,0:T(8,128)(2,1)}, bf16[8,128,512]{2,1,0:T(8,128)(2,1)}, u32[]{:S(2)}, u32[]{:S(2)}) collective-permute-start(bf16[8,128,512]{2,1,0:T(8,128)(2,1)} %bitcast.47), channel_id=1, source_target_pairs={{0,15},{1,0},{2,1},{3,2},{4,3},{5,4},{6,5},{7,6},{8,7},{9,8},{10,9... | collective-permute-start | bytes 3145736 | tf_op jit(solution)/shard_map/ppermute | solution.py:515
  14.5 1.3 add_select_fusion
  15.8 26.4 %spread.1 = (f32[8,128,2048]{2,1,0:T(8,128)}, f32[24,512,128]{2,1,0:T(8,128)}, bf16[8,512,128]{2,1,0:T(8,128)(2,1)}, bf16[16,512,128]{2,1,0:T(8,128)(2,1)}, bf16...) custom-call(s32[8,16]{1,0:T(8,128)} %get-tuple-element.110.slots, ...), custom_call_target="tpu_custom_call" | custom-call | tf_op jit(solution)/shard_map/spread/pallas_call | solution.py:125
  42.2 0.0 collective-permute-done.2.rest_8_
  42.2 0.0 collective-permute-done.1.rest_7_
  42.2 1.2 collective-permute-done.rest_6_
  43.4 2.6 %collective-permute-start.5 = (bf16[8,128,512]{2,1,0:T(8,128)(2,1)}, bf16[8,128,512]{2,1,0:T(8,128)(2,1)}, u32[]{:S(2)}, u32[]{:S(2)}) collective-permute-start(bf16[8,128,512]{2,1,0:T(8,128)(2,1)} %bitcast.48), channel_id=1, source_target_pairs={{0,16},{16,0},{32,48},{48,32},{64,80},{80,64},{96,112},{112,96},{1... | collective-permute-start | bytes 3145736 | tf_op jit(solution)/shard_map/ppermute | solution.py:525
  46.1 0.0 collective-permute-start.8
  46.1 1.5 collective-permute-start.9
  47.5 5.0 %collective-permute-done.4.rest_2_ = bf16[8,128,512]{2,1,0:T(8,128)(2,1)} collective-permute-done((bf16[8,128,512]{2,1,0:T(8,128)(2,1)}, bf16[8,128,512]{2,1,0:T(8,128)(2,1)}, u32[]{:S(2)}, u32[]{:S(2)}) %collective-permute-start.4) | collective-permute-done | bytes 1048608 | tf_op jit(solution)/shard_map/ppermute | solution.py:516
  52.5 0.0 collective-permute-done.3.rest_1_
  52.5 0.0 collective-permute-done.5.rest_3_
  52.5 2.6 %collective-permute-start.6 = (bf16[8,128,512]{2,1,0:T(8,128)(2,1)}, bf16[8,128,512]{2,1,0:T(8,128)(2,1)}, u32[]{:S(2)}, u32[]{:S(2)}) collective-permute-start(bf16[8,128,512]{2,1,0:T(8,128)(2,1)} %collective-permute-done.3.rest_1_), channel_id=1, source_target_pairs={{0,16},{16,0},{32,48},{48,32},{64,80},{80,64},{96,112},{112,96},{1... | collective-permute-start | bytes 3145736 | tf_op jit(solution)/shard_map/ppermute | solution.py:527
  55.1 0.1 collective-permute-start.7
  55.2 0.5 fusion.19.place
  55.7 2.0 %collective-permute-done.6.rest_4_ = bf16[8,128,512]{2,1,0:T(8,128)(2,1)} collective-permute-done((bf16[8,128,512]{2,1,0:T(8,128)(2,1)}, bf16[8,128,512]{2,1,0:T(8,128)(2,1)}, u32[]{:S(2)}, u32[]{:S(2)}) %collective-permute-start.6) | collective-permute-done | bytes 1048608 | tf_op jit(solution)/shard_map/ppermute | solution.py:527
  57.8 1.5 %collective-permute-done.7.rest_5_ = bf16[8,128,512]{2,1,0:T(8,128)(2,1)} collective-permute-done((bf16[8,128,512]{2,1,0:T(8,128)(2,1)}, bf16[8,128,512]{2,1,0:T(8,128)(2,1)}, u32[]{:S(2)}, u32[]{:S(2)}) %collective-permute-start.7) | collective-permute-done | bytes 1048608 | tf_op jit(solution)/shard_map/ppermute | solution.py:527
  59.3 19.0 %gradients.1 = (f32[72,1,128]{2,1,0:T(1,128)}, f32[8,1,128]{2,1,0:T(1,128)}, f32[1032,128]{1,0:T(8,128)}, f32[1032,128]{1,0:T(8,128)}) custom-call(s32[8]{0:T(128)} %fusion.19.place, s32[8,16]{1,0:T(8,128)} %get-tuple-element.111.slots, f32[8,128,2048]{2,1,0:T(8,128)} %get-tuple-element.55.dense_ref, bf16[1024,512]{1,0:T(8,128)(2,1)} %grad_ref.3, ...), custom_call_target="tpu_custom_call" | custom-call | tf_op jit(solution)/shard_map/gradients/pallas_call | solution.py:284
  78.3 0.0 collective-permute-done.8
  78.3 0.0 collective-permute-done.9
  78.3 0.5 collective-permute-start.10
  78.8 4.3 %add_convert_fusion = (bf16[8,512,128]{2,1,0:T(8,128)(2,1)S(1)}, bf16[8,512,128]{2,1,0:T(8,128)(2,1)S(1)}) fusion(f32[24,512,128]{2,1,0:T(8,128)} %get-tuple-element.79.own_ref, bf16[16,512,128]{2,1,0:T(8,128)(2,1)} %collective-permute-done.8, bf16[16,512,128]{2,1,0:T(8,128)(2,1)} %collective-permute-done.9), kind=kLoop, calls=%fused_computation.3 | loop fusion | flops 5242880 | bytes 10485760 | tf_op jit(solution)/shard_map/convert_element_type | solution.py:552
  83.1 0.1 add.184
  83.2 0.2 collective-permute-start.14
  83.4 1.2 collective-permute-start.15
  84.8 0.8 collective-permute-start.11
  85.6 1.7 %collective-permute-start.13 = (bf16[288,128]{1,0:T(8,128)(2,1)S(1)}, bf16[288,128]{1,0:T(8,128)(2,1)S(1)}, u32[]{:S(2)}, u32[]{:S(2)}) collective-permute-start(bf16[288,128]{1,0:T(8,128)(2,1)S(1)} %constant_dynamic-update-slice_fusion.8), channel_id=1, source_target_pairs={{0,3},{1,0},{2,1},{3,2},{4,7},{5,4},{6,5},{7,6},{8,11},{9,8},{10,9... | collective-permute-start | bytes 221192 | tf_op jit(solution)/shard_map/ppermute | solution.py:470
  87.3 0.5 collective-permute-start.12
  87.8 1.7 %collective-permute-done.11 = bf16[288,128]{1,0:T(8,128)(2,1)S(1)} collective-permute-done((bf16[288,128]{1,0:T(8,128)(2,1)S(1)}, bf16[288,128]{1,0:T(8,128)(2,1)S(1)}, u32[]{:S(2)}, u32[]{:S(2)}) %collective-permute-start.11) | collective-permute-done | bytes 73760 | tf_op jit(solution)/shard_map/ppermute | solution.py:470
  89.6 0.8 collective-permute-done.13
  90.3 2.3 %collective-permute-done.12 = bf16[288,128]{1,0:T(8,128)(2,1)S(1)} collective-permute-done((bf16[288,128]{1,0:T(8,128)(2,1)S(1)}, bf16[288,128]{1,0:T(8,128)(2,1)S(1)}, u32[]{:S(2)}, u32[]{:S(2)}) %collective-permute-start.12) | collective-permute-done | bytes 73760 | tf_op jit(solution)/shard_map/ppermute | solution.py:470
  92.7 1.7 %collective-permute-start.18 = (f32[264,128]{1,0:T(8,128)S(1)}, f32[264,128]{1,0:T(8,128)S(1)}, u32[]{:S(2)}, u32[]{:S(2)}) collective-permute-start(f32[264,128]{1,0:T(8,128)S(1)} %pad_maximum_fusion.1), channel_id=1, source_target_pairs={{0,96},{16,112},{32,0},{48,16},{64,32},{80,48},{96,64},{112,80},{1... | collective-permute-start | bytes 405512 | tf_op jit(solution)/shard_map/ppermute | solution.py:435
  94.4 2.8 %collective-permute-start.16 = (f32[264,128]{1,0:T(8,128)S(1)}, f32[264,128]{1,0:T(8,128)S(1)}, u32[]{:S(2)}, u32[]{:S(2)}) collective-permute-start(f32[264,128]{1,0:T(8,128)S(1)} %pad_maximum_fusion.1), channel_id=1, source_target_pairs={{0,64},{16,80},{32,96},{48,112},{64,0},{80,16},{96,32},{112,48},{1... | collective-permute-start | bytes 405512 | tf_op jit(solution)/shard_map/ppermute | solution.py:435
  97.2 0.0 copy-start.9
  97.3 0.0 copy-start.8
  97.3 0.1 fusion.2
  97.3 0.0 copy-start
  97.4 0.0 copy-start.1
  97.4 0.0 copy-start.2
  97.4 0.1 collective-permute-start.19
  97.5 0.1 fusion.3
  97.6 4.8 %collective-permute-start.20 = (bf16[8,528,128]{2,1,0:T(8,128)(2,1)S(1)}, bf16[8,528,128]{2,1,0:T(8,128)(2,1)S(1)}, u32[]{:S(2)}, u32[]{:S(2)}) collective-permute-start(bf16[8,528,128]{2,1,0:T(8,128)(2,1)S(1)} %fusion.3), channel_id=1, source_target_pairs={{0,15},{1,0},{2,1},{3,2},{4,3},{5,4},{6,5},{7,6},{8,7},{9,8},{10,9... | collective-permute-start | bytes 3244040 | tf_op jit(solution)/shard_map/ppermute | solution.py:558
  102.4 0.0 collective-permute-done.18
  102.4 0.0 collective-permute-done.17
  102.4 0.2 collective-permute-done.16
  102.6 3.3 %collective-permute-start.21 = (bf16[8,512,128]{2,1,0:T(8,128)(2,1)S(1)}, bf16[8,512,128]{2,1,0:T(8,128)(2,1)S(1)}, u32[]{:S(2)}, u32[]{:S(2)}) collective-permute-start(bf16[8,512,128]{2,1,0:T(8,128)(2,1)S(1)} %copy-done.9), channel_id=1, source_target_pairs={{0,112},{16,32},{32,16},{48,64},{64,48},{80,96},{96,80},{112,0},{1... | collective-permute-start | bytes 3145736 | tf_op jit(solution)/shard_map/ppermute | solution.py:561
  106.0 19.1 %collective-permute-done.19.below_ref = bf16[8,528,128]{2,1,0:T(8,128)(2,1)S(1)} collective-permute-done((bf16[8,528,128]{2,1,0:T(8,128)(2,1)S(1)}, bf16[8,528,128]{2,1,0:T(8,128)(2,1)S(1)}, u32[]{:S(2)}, u32[]{:S(2)}) %collective-permute-start.19) | collective-permute-done | bytes 1081376 | tf_op jit(solution)/shard_map/ppermute | solution.py:557
  125.1 1.9 %collective-permute-start.25 = (bf16[288,128]{1,0:T(8,128)(2,1)S(1)}, bf16[288,128]{1,0:T(8,128)(2,1)S(1)}, u32[]{:S(2)}, u32[]{:S(2)}) collective-permute-start(bf16[288,128]{1,0:T(8,128)(2,1)S(1)} %constant_dynamic-update-slice_fusion.12), channel_id=1, source_target_pairs={{0,12},{1,13},{2,14},{3,15},{4,0},{5,1},{6,2},{7,3},{8,4},{9,5},{1... | collective-permute-start | bytes 221192 | tf_op jit(solution)/shard_map/ppermute | solution.py:435
  127.0 0.0 collective-permute-start.24
  127.0 1.3 collective-permute-start.23
  128.3 0.1 collective-permute-done.25
  128.4 3.8 %collective-permute-done.24 = bf16[288,128]{1,0:T(8,128)(2,1)S(1)} collective-permute-done((bf16[288,128]{1,0:T(8,128)(2,1)S(1)}, bf16[288,128]{1,0:T(8,128)(2,1)S(1)}, u32[]{:S(2)}, u32[]{:S(2)}) %collective-permute-start.24) | collective-permute-done | bytes 73760 | tf_op jit(solution)/shard_map/ppermute | solution.py:435
  132.3 3.2 %collective-permute-start.28 = (bf16[1,256,128]{2,1,0:T(8,128)(2,1)S(1)}, bf16[1,256,128]{2,1,0:T(8,128)(2,1)S(1)}, u32[]{:S(2)}, u32[]{:S(2)}) collective-permute-start(bf16[1,256,128]{2,1,0:T(8,128)(2,1)S(1)} %bitcast.52), channel_id=1, source_target_pairs={{0,3},{1,0},{2,1},{3,2},{4,7},{5,4},{6,5},{7,6},{8,11},{9,8},{10,9... | collective-permute-start | bytes 196616 | tf_op jit(solution)/shard_map/ppermute | solution.py:435
  135.5 0.7 collective-permute-start.26
  136.2 2.9 %finish_features.1 = bf16[1024,512]{1,0:T(8,128)(2,1)} custom-call(f32[24,512,128]{2,1,0:T(8,128)S(1)} %bitcast.37, bf16[8,512,128]{2,1,0:T(8,128)(2,1)S(1)} %collective-permute-done.22.twin_ref, bf16[8,512,128]{2,1,0:T(8,128)(2,1)S(1)} %collective-permute-done.21.far_ref, bf16[8,528,128]{2,1,0:T(8,128)(2,1)S(1)} %collective-permute-done.20.above_ref, ...), custom_call_target="tpu_custom_call" | custom-call | flops 6000000000 | bytes 1048576 | tf_op jit(solution)/shard_map/finish_features/pallas_call | solution.py:409
  139.1 1.1 collective-permute-done.27
  140.2 0.3 collective-permute-done.26
  140.5 5.2 %collective-permute-start.29 = (bf16[4,256,128]{2,1,0:T(8,128)(2,1)S(1)}, bf16[4,256,128]{2,1,0:T(8,128)(2,1)S(1)}, u32[]{:S(2)}, u32[]{:S(2)}) collective-permute-start(bf16[4,256,128]{2,1,0:T(8,128)(2,1)S(1)} %pad_maximum_fusion.near_ref), channel_id=1, source_target_pairs={{0,16},{16,0},{32,48},{48,32},{64,80},{80,64},{96,112},{112,96},{1... | collective-permute-start | bytes 786440 | tf_op jit(solution)/shard_map/ppermute | solution.py:579
  145.8 1.1 collective-permute-done.29.away_ref
  146.9 2.0 %finish_weight.1 = (f32[512,512]{1,0:T(8,128)}, f32[512]{0:T(512)}, f32[512]{0:T(512)}) custom-call(s32[8]{0:T(128)S(1)} %fusion.20.place, bf16[4,256,128]{2,1,0:T(8,128)(2,1)S(1)} %pad_maximum_fusion.near_ref, bf16[4,256,128]{2,1,0:T(8,128)(2,1)S(1)} %collective-permute-done.29.away_ref, f32[8,128]{1,0:T(8,128)S(1)} %slice_add_fusion.2.vec_ref, ...), custom_call_target="tpu_custom_call" | custom-call | tf_op jit(solution)/shard_map/finish_weight/pallas_call | solution.py:359
  (64 shorter events, 0.5 us)
Async XLA Ops:
  0.6 41.6 %collective-permute-start.2 = (bf16[8,128,512]{2,1,0:T(8,128)(2,1)}, bf16[8,128,512]{2,1,0:T(8,128)(2,1)S(1)}, u32[]{:S(2)}, u32[]{:S(2)}) collective-permute-start(bf16[8,128,512]{2,1,0:T(8,128)(2,1)} %bitcast.43), channel_id=1, source_target_pairs={{0,113},{1,114},{2,115},{3,116},{4,117},{5,118},{6,119},{7,120},{8... | collective-permute-start | bytes 3145736 | tf_op jit(solution)/shard_map/ppermute | solution.py:518
  4.7 37.5 %collective-permute-start.1 = (bf16[8,128,512]{2,1,0:T(8,128)(2,1)}, bf16[8,128,512]{2,1,0:T(8,128)(2,1)S(1)}, u32[]{:S(2)}, u32[]{:S(2)}) collective-permute-start(bf16[8,128,512]{2,1,0:T(8,128)(2,1)} %bitcast.44), channel_id=1, source_target_pairs={{0,127},{1,112},{2,113},{3,114},{4,115},{5,116},{6,117},{7,118},{8... | collective-permute-start | bytes 3145736 | tf_op jit(solution)/shard_map/ppermute | solution.py:518
  8.5 35.0 %collective-permute-start = (bf16[8,128,512]{2,1,0:T(8,128)(2,1)}, bf16[8,128,512]{2,1,0:T(8,128)(2,1)}, u32[]{:S(2)}, u32[]{:S(2)}) collective-permute-start(bf16[8,128,512]{2,1,0:T(8,128)(2,1)} %bitcast.45), channel_id=1, source_target_pairs={{0,112},{16,32},{32,16},{48,64},{64,48},{80,96},{96,80},{112,0},{1... | collective-permute-start | bytes 3145736 | tf_op jit(solution)/shard_map/ppermute | solution.py:517
  9.7 42.8 %collective-permute-start.4 = (bf16[8,128,512]{2,1,0:T(8,128)(2,1)}, bf16[8,128,512]{2,1,0:T(8,128)(2,1)}, u32[]{:S(2)}, u32[]{:S(2)}) collective-permute-start(bf16[8,128,512]{2,1,0:T(8,128)(2,1)} %bitcast.46), channel_id=1, source_target_pairs={{0,1},{1,2},{2,3},{3,4},{4,5},{5,6},{6,7},{7,8},{8,9},{9,10},{10,1... | collective-permute-start | bytes 3145736 | tf_op jit(solution)/shard_map/ppermute | solution.py:516
  9.7 42.8 %collective-permute-start.3 = (bf16[8,128,512]{2,1,0:T(8,128)(2,1)}, bf16[8,128,512]{2,1,0:T(8,128)(2,1)}, u32[]{:S(2)}, u32[]{:S(2)}) collective-permute-start(bf16[8,128,512]{2,1,0:T(8,128)(2,1)} %bitcast.47), channel_id=1, source_target_pairs={{0,15},{1,0},{2,1},{3,2},{4,3},{5,4},{6,5},{7,6},{8,7},{9,8},{10,9... | collective-permute-start | bytes 3145736 | tf_op jit(solution)/shard_map/ppermute | solution.py:515
  42.2 17.1 %copy-start.4 = (bf16[8,128,512]{2,1,0:T(8,128)(2,1)}, bf16[8,128,512]{2,1,0:T(8,128)(2,1)S(1)}, u32[]{:S(2)}) copy-start(bf16[8,128,512]{2,1,0:T(8,128)(2,1)S(1)} %collective-permute-done.2.rest_8_) | copy-start | bytes 3145732
  42.2 17.0 %copy-start.5 = (bf16[8,128,512]{2,1,0:T(8,128)(2,1)}, bf16[8,128,512]{2,1,0:T(8,128)(2,1)S(1)}, u32[]{:S(2)}) copy-start(bf16[8,128,512]{2,1,0:T(8,128)(2,1)S(1)} %collective-permute-done.1.rest_7_) | copy-start | bytes 3145732
  43.4 9.1 %collective-permute-start.5 = (bf16[8,128,512]{2,1,0:T(8,128)(2,1)}, bf16[8,128,512]{2,1,0:T(8,128)(2,1)}, u32[]{:S(2)}, u32[]{:S(2)}) collective-permute-start(bf16[8,128,512]{2,1,0:T(8,128)(2,1)} %bitcast.48), channel_id=1, source_target_pairs={{0,16},{16,0},{32,48},{48,32},{64,80},{80,64},{96,112},{112,96},{1... | collective-permute-start | bytes 3145736 | tf_op jit(solution)/shard_map/ppermute | solution.py:525
  46.1 32.2 %collective-permute-start.8 = (bf16[16,512,128]{2,1,0:T(8,128)(2,1)}, bf16[16,512,128]{2,1,0:T(8,128)(2,1)}, u32[]{:S(2)}, u32[]{:S(2)}) collective-permute-start(bf16[16,512,128]{2,1,0:T(8,128)(2,1)} %get-tuple-element.68), channel_id=1, source_target_pairs={{0,112},{16,32},{32,16},{48,64},{64,48},{80,96},{96,80},{112,0},{1... | collective-permute-start | bytes 6291464 | tf_op jit(solution)/shard_map/ppermute | solution.py:528
  46.1 32.2 %collective-permute-start.9 = (bf16[16,512,128]{2,1,0:T(8,128)(2,1)}, bf16[16,512,128]{2,1,0:T(8,128)(2,1)}, u32[]{:S(2)}, u32[]{:S(2)}) collective-permute-start(bf16[16,512,128]{2,1,0:T(8,128)(2,1)} %get-tuple-element.69), channel_id=1, source_target_pairs={{0,16},{16,0},{32,48},{48,32},{64,80},{80,64},{96,112},{112,96},{1... | collective-permute-start | bytes 6291464 | tf_op jit(solution)/shard_map/ppermute | solution.py:529
  52.5 5.2 %collective-permute-start.6 = (bf16[8,128,512]{2,1,0:T(8,128)(2,1)}, bf16[8,128,512]{2,1,0:T(8,128)(2,1)}, u32[]{:S(2)}, u32[]{:S(2)}) collective-permute-start(bf16[8,128,512]{2,1,0:T(8,128)(2,1)} %collective-permute-done.3.rest_1_), channel_id=1, source_target_pairs={{0,16},{16,0},{32,48},{48,32},{64,80},{80,64},{96,112},{112,96},{1... | collective-permute-start | bytes 3145736 | tf_op jit(solution)/shard_map/ppermute | solution.py:527
  55.1 4.1 %collective-permute-start.7 = (bf16[8,128,512]{2,1,0:T(8,128)(2,1)}, bf16[8,128,512]{2,1,0:T(8,128)(2,1)}, u32[]{:S(2)}, u32[]{:S(2)}) collective-permute-start(bf16[8,128,512]{2,1,0:T(8,128)(2,1)} %collective-permute-done.4.rest_2_), channel_id=1, source_target_pairs={{0,16},{16,0},{32,48},{48,32},{64,80},{80,64},{96,112},{112,96},{1... | collective-permute-start | bytes 3145736 | tf_op jit(solution)/shard_map/ppermute | solution.py:527
  59.3 76.9 %slice-start = ((s8[6291456]{0:T(1024)(128)(4,1)}), s8[2097152]{0:T(1024)(128)(4,1)S(1)}, s32[]{:S(2)}) async-start(s8[6291456]{0:T(1024)(128)(4,1)} %bitcast.36), calls=%async_computation | async-start | bytes 4194304
  78.3 4.8 %copy-start.6 = (f32[1032,128]{1,0:T(8,128)S(1)}, f32[1032,128]{1,0:T(8,128)}, u32[]{:S(2)}) copy-start(f32[1032,128]{1,0:T(8,128)} %get-tuple-element.70) | copy-start | bytes 1585156
  78.3 4.9 %copy-start.7 = (f32[72,1,128]{2,1,0:T(1,128)S(1)}, f32[72,1,128]{2,1,0:T(1,128)}, u32[]{:S(2)}) copy-start(f32[72,1,128]{2,1,0:T(1,128)} %get-tuple-element.72) | copy-start | bytes 110596
  78.3 57.8 %slice-start.1 = ((s8[6291456]{0:T(1024)(128)(4,1)}), s8[4194304]{0:T(1024)(128)(4,1)S(1)}, s32[]{:S(2)}) async-start(s8[6291456]{0:T(1024)(128)(4,1)} %bitcast.36), calls=%async_computation.1 | async-start | bytes 8388608
  78.3 4.7 %collective-permute-start.10 = (f32[1032,128]{1,0:T(8,128)}, f32[1032,128]{1,0:T(8,128)S(1)}, u32[]{:S(2)}, u32[]{:S(2)}) collective-permute-start(f32[1032,128]{1,0:T(8,128)} %get-tuple-element.71), channel_id=1, source_target_pairs={{0,16},{16,0},{32,48},{48,32},{64,80},{80,64},{96,112},{112,96},{1... | collective-permute-start | bytes 1585160 | tf_op jit(solution)/shard_map/ppermute | solution.py:542
  83.2 4.6 %collective-permute-start.14 = (f32[3,8,1,128]{3,1,0,2:T(8,128)S(1)}, f32[3,8,1,128]{3,1,0,2:T(8,128)S(1)}, u32[]{:S(2)}, u32[]{:S(2)}) collective-permute-start(f32[3,8,1,128]{3,1,0,2:T(8,128)S(1)} %get-tuple-element.117), channel_id=1, source_target_pairs={{0,16},{16,0},{32,48},{48,32},{64,80},{80,64},{96,112},{112,96},{1... | collective-permute-start | bytes 36872 | tf_op jit(solution)/shard_map/ppermute | solution.py:545
  83.4 4.4 %collective-permute-start.15 = (f32[3,8,1,128]{3,1,2,0:T(8,128)S(1)}, f32[3,8,1,128]{3,1,2,0:T(8,128)S(1)}, u32[]{:S(2)}, u32[]{:S(2)}) collective-permute-start(f32[3,8,1,128]{3,1,2,0:T(8,128)S(1)} %get-tuple-element.118), channel_id=1, source_target_pairs={{0,112},{16,32},{32,16},{48,64},{64,48},{80,96},{96,80},{112,0},{1... | collective-permute-start | bytes 36872 | tf_op jit(solution)/shard_map/ppermute | solution.py:545
  84.8 4.8 %collective-permute-start.11 = (bf16[288,128]{1,0:T(8,128)(2,1)S(1)}, bf16[288,128]{1,0:T(8,128)(2,1)S(1)}, u32[]{:S(2)}, u32[]{:S(2)}) collective-permute-start(bf16[288,128]{1,0:T(8,128)(2,1)S(1)} %constant_dynamic-update-slice_fusion), channel_id=1, source_target_pairs={{0,2},{1,3},{2,0},{3,1},{4,6},{5,7},{6,4},{7,5},{8,10},{9,11},{10,... | collective-permute-start | bytes 221192 | tf_op jit(solution)/shard_map/ppermute | solution.py:470
  85.6 4.7 %collective-permute-start.13 = (bf16[288,128]{1,0:T(8,128)(2,1)S(1)}, bf16[288,128]{1,0:T(8,128)(2,1)S(1)}, u32[]{:S(2)}, u32[]{:S(2)}) collective-permute-start(bf16[288,128]{1,0:T(8,128)(2,1)S(1)} %constant_dynamic-update-slice_fusion.8), channel_id=1, source_target_pairs={{0,3},{1,0},{2,1},{3,2},{4,7},{5,4},{6,5},{7,6},{8,11},{9,8},{10,9... | collective-permute-start | bytes 221192 | tf_op jit(solution)/shard_map/ppermute | solution.py:470
  87.3 5.4 %collective-permute-start.12 = (bf16[288,128]{1,0:T(8,128)(2,1)S(1)}, bf16[288,128]{1,0:T(8,128)(2,1)S(1)}, u32[]{:S(2)}, u32[]{:S(2)}) collective-permute-start(bf16[288,128]{1,0:T(8,128)(2,1)S(1)} %constant_dynamic-update-slice_fusion.4), channel_id=1, source_target_pairs={{0,1},{1,2},{2,3},{3,0},{4,5},{5,6},{6,7},{7,4},{8,9},{9,10},{10,1... | collective-permute-start | bytes 221192 | tf_op jit(solution)/shard_map/ppermute | solution.py:470
  92.7 9.7 %collective-permute-start.18 = (f32[264,128]{1,0:T(8,128)S(1)}, f32[264,128]{1,0:T(8,128)S(1)}, u32[]{:S(2)}, u32[]{:S(2)}) collective-permute-start(f32[264,128]{1,0:T(8,128)S(1)} %pad_maximum_fusion.1), channel_id=1, source_target_pairs={{0,96},{16,112},{32,0},{48,16},{64,32},{80,48},{96,64},{112,80},{1... | collective-permute-start | bytes 405512 | tf_op jit(solution)/shard_map/ppermute | solution.py:435
  94.4 8.0 %collective-permute-start.17 = (f32[264,128]{1,0:T(8,128)S(1)}, f32[264,128]{1,0:T(8,128)S(1)}, u32[]{:S(2)}, u32[]{:S(2)}) collective-permute-start(f32[264,128]{1,0:T(8,128)S(1)} %pad_maximum_fusion.1), channel_id=1, source_target_pairs={{0,32},{16,48},{32,64},{48,80},{64,96},{80,112},{96,0},{112,16},{1... | collective-permute-start | bytes 405512 | tf_op jit(solution)/shard_map/ppermute | solution.py:435
  94.4 8.2 %collective-permute-start.16 = (f32[264,128]{1,0:T(8,128)S(1)}, f32[264,128]{1,0:T(8,128)S(1)}, u32[]{:S(2)}, u32[]{:S(2)}) collective-permute-start(f32[264,128]{1,0:T(8,128)S(1)} %pad_maximum_fusion.1), channel_id=1, source_target_pairs={{0,64},{16,80},{32,96},{48,112},{64,0},{80,16},{96,32},{112,48},{1... | collective-permute-start | bytes 405512 | tf_op jit(solution)/shard_map/ppermute | solution.py:435
  97.2 5.4 %copy-start.9 = (bf16[8,512,128]{2,1,0:T(8,128)(2,1)S(1)}, bf16[8,512,128]{2,1,0:T(8,128)(2,1)}, u32[]{:S(2)}) copy-start(bf16[8,512,128]{2,1,0:T(8,128)(2,1)} %get-tuple-element.83) | copy-start | bytes 3145732
  97.3 8.7 %copy-start.8 = (bf16[8,512,128]{2,1,0:T(8,128)(2,1)S(1)}, bf16[8,512,128]{2,1,0:T(8,128)(2,1)}, u32[]{:S(2)}) copy-start(bf16[8,512,128]{2,1,0:T(8,128)(2,1)} %get-tuple-element.84) | copy-start | bytes 3145732
  97.3 38.8 %copy-start = (bf16[512,512]{1,0:T(8,128)(2,1)S(1)}, bf16[512,512]{1,0:T(8,128)(2,1)}, u32[]{:S(2)}) copy-start(bf16[512,512]{1,0:T(8,128)(2,1)} %weight_ref.5) | copy-start | bytes 1572868
  97.4 38.8 %copy-start.1 = (f32[512]{0:T(512)S(1)}, f32[512]{0:T(512)}, u32[]{:S(2)}) copy-start(f32[512]{0:T(512)} %param.10) | copy-start | bytes 6148
  97.4 38.8 %copy-start.2 = (f32[512]{0:T(512)S(1)}, f32[512]{0:T(512)}, u32[]{:S(2)}) copy-start(f32[512]{0:T(512)} %param.11) | copy-start | bytes 6148
  97.4 38.8 %copy-start.3 = (f32[8,1,128]{2,1,0:T(1,128)S(1)}, f32[8,1,128]{2,1,0:T(1,128)}, u32[]{:S(2)}) copy-start(f32[8,1,128]{2,1,0:T(1,128)} %get-tuple-element.92.du_ref) | copy-start | bytes 12292
  97.4 27.7 %collective-permute-start.19 = (bf16[8,528,128]{2,1,0:T(8,128)(2,1)S(1)}, bf16[8,528,128]{2,1,0:T(8,128)(2,1)S(1)}, u32[]{:S(2)}, u32[]{:S(2)}) collective-permute-start(bf16[8,528,128]{2,1,0:T(8,128)(2,1)S(1)} %fusion.2), channel_id=1, source_target_pairs={{0,1},{1,2},{2,3},{3,4},{4,5},{5,6},{6,7},{7,8},{8,9},{9,10},{10,1... | collective-permute-start | bytes 3244040 | tf_op jit(solution)/shard_map/ppermute | solution.py:557
  97.6 27.5 %collective-permute-start.20 = (bf16[8,528,128]{2,1,0:T(8,128)(2,1)S(1)}, bf16[8,528,128]{2,1,0:T(8,128)(2,1)S(1)}, u32[]{:S(2)}, u32[]{:S(2)}) collective-permute-start(bf16[8,528,128]{2,1,0:T(8,128)(2,1)S(1)} %fusion.3), channel_id=1, source_target_pairs={{0,15},{1,0},{2,1},{3,2},{4,3},{5,4},{6,5},{7,6},{8,7},{9,8},{10,9... | collective-permute-start | bytes 3244040 | tf_op jit(solution)/shard_map/ppermute | solution.py:558
  102.6 22.4 %collective-permute-start.21 = (bf16[8,512,128]{2,1,0:T(8,128)(2,1)S(1)}, bf16[8,512,128]{2,1,0:T(8,128)(2,1)S(1)}, u32[]{:S(2)}, u32[]{:S(2)}) collective-permute-start(bf16[8,512,128]{2,1,0:T(8,128)(2,1)S(1)} %copy-done.9), channel_id=1, source_target_pairs={{0,112},{16,32},{32,16},{48,64},{64,48},{80,96},{96,80},{112,0},{1... | collective-permute-start | bytes 3145736 | tf_op jit(solution)/shard_map/ppermute | solution.py:561
  106.0 19.1 %collective-permute-start.22 = (bf16[8,512,128]{2,1,0:T(8,128)(2,1)S(1)}, bf16[8,512,128]{2,1,0:T(8,128)(2,1)S(1)}, u32[]{:S(2)}, u32[]{:S(2)}) collective-permute-start(bf16[8,512,128]{2,1,0:T(8,128)(2,1)S(1)} %copy-done.8), channel_id=1, source_target_pairs={{0,16},{16,0},{32,48},{48,32},{64,80},{80,64},{96,112},{112,96},{1... | collective-permute-start | bytes 3145736 | tf_op jit(solution)/shard_map/ppermute | solution.py:562
  125.1 3.3 %collective-permute-start.25 = (bf16[288,128]{1,0:T(8,128)(2,1)S(1)}, bf16[288,128]{1,0:T(8,128)(2,1)S(1)}, u32[]{:S(2)}, u32[]{:S(2)}) collective-permute-start(bf16[288,128]{1,0:T(8,128)(2,1)S(1)} %constant_dynamic-update-slice_fusion.12), channel_id=1, source_target_pairs={{0,12},{1,13},{2,14},{3,15},{4,0},{5,1},{6,2},{7,3},{8,4},{9,5},{1... | collective-permute-start | bytes 221192 | tf_op jit(solution)/shard_map/ppermute | solution.py:435
  127.0 5.2 %collective-permute-start.24 = (bf16[288,128]{1,0:T(8,128)(2,1)S(1)}, bf16[288,128]{1,0:T(8,128)(2,1)S(1)}, u32[]{:S(2)}, u32[]{:S(2)}) collective-permute-start(bf16[288,128]{1,0:T(8,128)(2,1)S(1)} %constant_dynamic-update-slice_fusion.12), channel_id=1, source_target_pairs={{0,4},{1,5},{2,6},{3,7},{4,8},{5,9},{6,10},{7,11},{8,12},{9,13},{1... | collective-permute-start | bytes 221192 | tf_op jit(solution)/shard_map/ppermute | solution.py:435
  127.0 5.2 %collective-permute-start.23 = (bf16[288,128]{1,0:T(8,128)(2,1)S(1)}, bf16[288,128]{1,0:T(8,128)(2,1)S(1)}, u32[]{:S(2)}, u32[]{:S(2)}) collective-permute-start(bf16[288,128]{1,0:T(8,128)(2,1)S(1)} %constant_dynamic-update-slice_fusion.12), channel_id=1, source_target_pairs={{0,8},{1,9},{2,10},{3,11},{4,12},{5,13},{6,14},{7,15},{8,0},{9,1},... | collective-permute-start | bytes 221192 | tf_op jit(solution)/shard_map/ppermute | solution.py:435
  132.3 6.8 %collective-permute-start.28 = (bf16[1,256,128]{2,1,0:T(8,128)(2,1)S(1)}, bf16[1,256,128]{2,1,0:T(8,128)(2,1)S(1)}, u32[]{:S(2)}, u32[]{:S(2)}) collective-permute-start(bf16[1,256,128]{2,1,0:T(8,128)(2,1)S(1)} %bitcast.52), channel_id=1, source_target_pairs={{0,3},{1,0},{2,1},{3,2},{4,7},{5,4},{6,5},{7,6},{8,11},{9,8},{10,9... | collective-permute-start | bytes 196616 | tf_op jit(solution)/shard_map/ppermute | solution.py:435
  135.5 4.7 %collective-permute-start.27 = (bf16[1,256,128]{2,1,0:T(8,128)(2,1)S(1)}, bf16[1,256,128]{2,1,0:T(8,128)(2,1)S(1)}, u32[]{:S(2)}, u32[]{:S(2)}) collective-permute-start(bf16[1,256,128]{2,1,0:T(8,128)(2,1)S(1)} %bitcast.53), channel_id=1, source_target_pairs={{0,2},{1,3},{2,0},{3,1},{4,6},{5,7},{6,4},{7,5},{8,10},{9,11},{10,... | collective-permute-start | bytes 196616 | tf_op jit(solution)/shard_map/ppermute | solution.py:435
  135.5 5.0 %collective-permute-start.26 = (bf16[1,256,128]{2,1,0:T(8,128)(2,1)S(1)}, bf16[1,256,128]{2,1,0:T(8,128)(2,1)S(1)}, u32[]{:S(2)}, u32[]{:S(2)}) collective-permute-start(bf16[1,256,128]{2,1,0:T(8,128)(2,1)S(1)} %bitcast.54), channel_id=1, source_target_pairs={{0,1},{1,2},{2,3},{3,0},{4,5},{5,6},{6,7},{7,4},{8,9},{9,10},{10,1... | collective-permute-start | bytes 196616 | tf_op jit(solution)/shard_map/ppermute | solution.py:435
  140.5 6.4 %collective-permute-start.29 = (bf16[4,256,128]{2,1,0:T(8,128)(2,1)S(1)}, bf16[4,256,128]{2,1,0:T(8,128)(2,1)S(1)}, u32[]{:S(2)}, u32[]{:S(2)}) collective-permute-start(bf16[4,256,128]{2,1,0:T(8,128)(2,1)S(1)} %pad_maximum_fusion.near_ref), channel_id=1, source_target_pairs={{0,16},{16,0},{32,48},{48,32},{64,80},{80,64},{96,112},{112,96},{1... | collective-permute-start | bytes 786440 | tf_op jit(solution)/shard_map/ppermute | solution.py:579
